TPU v7x, 512 devices: a whole 4x4x16 slice. The times are simulated.
512 devices in a mesh: patch: 64 (over x_lo, z, core), head: 8 (over y, x_hi).
Axes of the slice: x: 4 (x_hi: 2, x_lo: 2; x = x_hi * 2 + x_lo), y: 4, z: 16, core: 2. Of those that a mesh axis runs over, the one named last changes fastest.
Arguments:
- query_raw: bfloat16 [12288, 2048], P('patch', 'head'), may hold values from -6 to 6
- key_raw: bfloat16 [12288, 2048], P('patch', 'head'), may hold values from -6 to 6
- value_raw: bfloat16 [12288, 2048], P('patch', 'head'), may hold values from -6 to 6
- stale_pairs: bfloat16 [2, 12288, 2048], P(None, 'patch', 'head'), as said below
- query_gain: float32 [128], replicated, may hold values from 1.2 to 5.5
- key_gain: float32 [128], replicated, may hold values from 1.2 to 5.5
- patch_offsets: int32 [64], P('patch'), may hold values from 0 to 12096, as said below
- attn_gate: float32 [3072], P('head'), may hold values from 1 to 3
- out_weight: bfloat16 [2048, 3072], P(None, 'head'), may hold values from -0.125 to 0.125
Outputs:
- attn_branch: bfloat16 [12288, 3072], P('patch', 'head')
- fresh_keys: bfloat16 [12288, 2048], P('patch', 'head')
Inputs may be any that keep to these rules, and one draw needn't show every extreme that they name: `patch_offsets`: every multiple of 192 from 0 to 12096 appears exactly once. `stale_pairs`: index 0 holds keys normed with key_gain and rotated at each token's own position, as fresh_keys are; index 1 holds values like value_raw.
All inputs are finite; a program needn't handle non-finite values.
Results may differ from a plain program's by a relative error of at most 0.017.
Values may be sent and summed in bfloat16 or wider, within the bound.
No kernel may reach another device: no remote copies, remote signals or barrier semaphores. Data moves between devices by JAX's collectives and lax.ppermute only.
A program may use at most 128 MiB of HBM per device.

v0:
```python
import jax
import jax.numpy as jnp
from jax import lax
from jax.sharding import PartitionSpec as P


def rotated_norm(raw_heads, gain_vector, positions):
    head_width = raw_heads.shape[-1]
    halfway = head_width // 2
    squares = jnp.mean(raw_heads * raw_heads, axis=-1, keepdims=True)
    normed = raw_heads * lax.rsqrt(squares + 1e-06) * gain_vector
    frequency = jnp.exp(
        -(2.0 * jnp.arange(halfway, dtype=jnp.float32) / head_width) * jnp.log(256.0)
    )
    angles = positions.astype(jnp.float32)[..., None] * frequency
    cosine = jnp.cos(angles)[..., None, :]
    sinusoid = jnp.sin(angles)[..., None, :]
    leading = normed[..., :halfway]
    trailing = normed[..., halfway:]
    return jnp.concatenate(
        [leading * cosine - trailing * sinusoid, trailing * cosine + leading * sinusoid], axis=-1
    )


def absorb(softmax_state, queries, key_block, value_block, keep_mask):
    previous_peak, previous_total, previous_sum = softmax_state
    scale_factor = queries.shape[-1] ** (-0.5)
    scores = (
        jnp.einsum("qhd,khd->qhk", queries, key_block, preferred_element_type=jnp.float32)
        * scale_factor
    )
    scores = jnp.where(keep_mask[None, None, :], scores, -jnp.inf)
    next_peak = jnp.maximum(previous_peak, jnp.max(scores, axis=-1))
    shrink_factor = jnp.exp(previous_peak - next_peak)
    weights = jnp.exp(scores - next_peak[..., None])
    next_total = previous_total * shrink_factor + jnp.sum(weights, axis=-1)
    next_sum = previous_sum * shrink_factor[..., None] + jnp.einsum(
        "qhk,khd->qhd",
        weights.astype(jnp.bfloat16),
        value_block,
        preferred_element_type=jnp.float32,
    )
    return (next_peak, next_total, next_sum)


def absorb_rows(softmax_state, queries, key_rows, value_rows, first_row, shard_rows, my_patch):
    row_count = key_rows.shape[0]
    block_rows = row_count
    while block_rows > 2048 and block_rows % 2 == 0:
        block_rows = block_rows // 2
    block_count = row_count // block_rows
    key_blocks = key_rows.reshape(block_count, block_rows, key_rows.shape[1], key_rows.shape[2])
    value_blocks = value_rows.reshape(
        block_count, block_rows, value_rows.shape[1], value_rows.shape[2]
    )

    def advance(current, block_item):
        key_part, value_part, block_number = block_item
        row_ids = first_row + block_number * block_rows + jnp.arange(block_rows, dtype=jnp.int32)
        keep_mask = row_ids // shard_rows != my_patch
        return (absorb(current, queries, key_part, value_part, keep_mask), None)

    softmax_state, unused_output = lax.scan(
        advance, softmax_state, (key_blocks, value_blocks, jnp.arange(block_count, dtype=jnp.int32))
    )
    return softmax_state


def shards(
    query_raw,
    key_raw,
    value_raw,
    stale_pairs,
    query_gain,
    key_gain,
    patch_offsets,
    attn_gate,
    out_weight,
):
    token_rows, local_width = query_raw.shape
    head_width = query_gain.shape[0]
    local_heads = local_width // head_width
    positions = patch_offsets[0] + jnp.arange(token_rows, dtype=jnp.int32)
    queries = rotated_norm(
        query_raw.astype(jnp.float32).reshape(token_rows, local_heads, head_width),
        query_gain,
        positions,
    ).astype(jnp.bfloat16)
    fresh_keys = rotated_norm(
        key_raw.astype(jnp.float32).reshape(token_rows, local_heads, head_width),
        key_gain,
        positions,
    ).astype(jnp.bfloat16)
    values_now = value_raw.reshape(token_rows, local_heads, head_width)
    my_patch = lax.axis_index("patch")
    start_state = (
        jnp.full((token_rows, local_heads), -jnp.inf, jnp.float32),
        jnp.zeros((token_rows, local_heads), jnp.float32),
        jnp.zeros((token_rows, local_heads, head_width), jnp.float32),
    )
    every_row = jnp.arange(token_rows, dtype=jnp.int32) >= 0
    softmax_state = absorb(start_state, queries, fresh_keys, values_now, every_row)
    gathered = lax.all_gather(stale_pairs, "patch", axis=1, tiled=True)
    whole_rows = gathered.shape[1]
    softmax_state = absorb_rows(
        softmax_state,
        queries,
        gathered[0].reshape(whole_rows, local_heads, head_width),
        gathered[1].reshape(whole_rows, local_heads, head_width),
        0,
        token_rows,
        my_patch,
    )
    final_peak, denominators, numerators = softmax_state
    attended = (
        (numerators / denominators[..., None]).astype(jnp.bfloat16).reshape(token_rows, local_width)
    )
    projected = jnp.dot(
        lax.all_gather(attended, "head", axis=1, tiled=True),
        out_weight,
        preferred_element_type=jnp.float32,
    )
    attn_branch = (projected * attn_gate[None, :]).astype(jnp.bfloat16)
    return (attn_branch, fresh_keys.reshape(token_rows, local_width))


def solution(mesh):
    return jax.shard_map(
        shards,
        mesh=mesh,
        in_specs=(
            P("patch", "head"),
            P("patch", "head"),
            P("patch", "head"),
            P(None, "patch", "head"),
            P(),
            P(),
            P("patch"),
            P("head"),
            P(None, "head"),
        ),
        out_specs=(P("patch", "head"), P("patch", "head")),
        check_vma=False,
    )
```

profile of v0, /device:TPU:1, one launch (start us, length us, event | category | flops | bytes accessed | tf_op | source)
XLA Modules:
  0.0 264.0 jit_solution(14885232441419779486)
XLA Ops:
  7.2 0.7 all-gather.2.cloned.1.call-update
  8.6 1.0 reshape.135
  9.6 0.3 multiply_reduce_fusion
  9.8 0.1 copy.37
  9.9 1.0 reshape.133
  10.9 0.3 multiply_reduce_fusion.1
  11.3 0.4 multiply_cosine_fusion
  11.8 1.0 fusion.21
  12.8 1.0 fusion.22
  13.8 0.1 subtract_convert_fusion
  14.0 0.1 multiply_subtract_fusion
  14.1 0.1 maximum_convert_fusion
  14.2 0.2 fusion.30
  14.5 0.1 fusion.19
  14.6 0.7 copy_bitcast_fusion.4
  15.2 0.3 fusion.17
  15.5 136.2 %all-gather.2.cloned.1.call-done = bf16[2,12288,256]{2,1,0:T(8,128)(2,1)} async-done(((bf16[2,192,256]{2,1,0:T(8,128)(2,1)}), bf16[2,12288,256]{2,1,0:T(8,128)(2,1)}) %all-gather.2.cloned.1.call-update) | async-done | bytes 12582928 | tf_op jit(solution)/shard_map/all_gather | solution.py:103
  151.7 10.2 %fusion.29 = (bf16[1,12288,256]{2,1,0:T(8,128)(2,1)}, bf16[1,12288,256]{2,1,0:T(8,128)(2,1)}) fusion(bf16[2,12288,256]{2,1,0:T(8,128)(2,1)} %all-gather.2.cloned.1.call-done), kind=kLoop, calls=%fused_computation.61 | loop fusion | bytes 25165824 | tf_op jit(solution)/shard_map/slice | solution.py:109
  161.9 9.7 %reshape.137 = bf16[8,1536,2,128]{3,2,1,0:T(2,128)(2,1)} reshape(bf16[1,12288,256]{2,1,0:T(8,128)(2,1)} %get-tuple-element.170) | data formatting | bytes 12582912 | tf_op jit(solution)/shard_map/reshape;reshape;squeeze | solution.py:53
  171.6 9.8 %reshape.136 = bf16[8,1536,2,128]{3,2,1,0:T(2,128)(2,1)} reshape(bf16[1,12288,256]{2,1,0:T(8,128)(2,1)} %get-tuple-element.171) | data formatting | bytes 12582912 | tf_op jit(solution)/shard_map/reshape;reshape;squeeze | solution.py:52
  181.3 42.1 %while.16 = (s32[]{:T(128)}, f32[192,2]{0,1:T(2,128)S(1)}, f32[192,2]{0,1:T(2,128)S(1)}, f32[192,2,128]{2,0,1:T(8,128)S(1)}, s32[8]{0:T(128)S(1)}, /*index=5*/s3...) while((s32[]{:T(128)}, f32[192,2]{0,1:T(2,128)S(1)}, ...), condition=%wide.region_7.8_spmd, body=%wide.region_4.7_spmd.sunk | while | flops 306233088 | bytes 12315801 | solution.py:63
  181.3 0.6 dynamic_slice.25
  182.6 2.2 constant_dynamic-slice_fusion.3
  184.8 0.6 fusion.48
  185.4 0.5 fusion.49
  185.9 0.6 fusion.50
  186.6 0.6 dynamic_slice.25
  187.9 2.2 constant_dynamic-slice_fusion.3
  190.1 0.6 fusion.48
  190.7 0.5 fusion.49
  191.2 0.6 fusion.50
  191.9 0.6 dynamic_slice.25
  193.1 2.2 constant_dynamic-slice_fusion.3
  195.4 0.6 fusion.48
  196.0 0.5 fusion.49
  196.5 0.6 fusion.50
  197.1 0.6 dynamic_slice.25
  198.4 2.2 constant_dynamic-slice_fusion.3
  200.6 0.6 fusion.48
  201.2 0.5 fusion.49
  201.7 0.6 fusion.50
  202.4 0.6 dynamic_slice.25
  203.7 2.2 constant_dynamic-slice_fusion.3
  205.9 0.6 fusion.48
  206.5 0.5 fusion.49
  207.0 0.6 fusion.50
  207.7 0.6 dynamic_slice.25
  208.9 2.2 constant_dynamic-slice_fusion.3
  211.2 0.6 fusion.48
  211.8 0.5 fusion.49
  212.3 0.6 fusion.50
  212.9 0.6 dynamic_slice.25
  214.2 2.2 constant_dynamic-slice_fusion.3
  216.4 0.6 fusion.48
  217.0 0.5 fusion.49
  217.5 0.6 fusion.50
  218.2 0.6 dynamic_slice.25
  219.5 2.2 constant_dynamic-slice_fusion.3
  221.7 0.6 fusion.48
  222.3 0.5 fusion.49
  222.8 0.6 fusion.50
  223.5 0.1 copy_bitcast_fusion.5
  223.6 32.3 %all_gather.7 = bf16[192,2048]{1,0:T(8,128)(2,1)S(1)} all-gather(bf16[192,256]{1,0:T(8,128)(2,1)S(1)} %copy_bitcast_fusion.5), channel_id=1, replica_groups=mesh['patch'=64,'head'=8] {'head'}, dimensions={1}, use_global_device_ids=true | all-gather | bytes 884736 | tf_op jit(solution)/shard_map/all_gather | solution.py:119
  255.9 1.2 fusion.16
  (46 shorter events, 0.5 us)
Async XLA Ops:
  7.2 248.7 %copy-start = (bf16[2048,384]{1,0:T(8,128)(2,1)S(1)}, bf16[2048,384]{1,0:T(8,128)(2,1)}, u32[]{:S(2)}) copy-start(bf16[2048,384]{1,0:T(8,128)(2,1)} %param.19) | copy-start | bytes 4718596
  7.2 144.5 %all-gather.2.cloned.1.call-start = ((), (), s32[]{:S(2)}) async-start(), calls=%async_computation | async-start | bytes 12779520 | tf_op jit(solution)/shard_map/all_gather | solution.py:103
  10.9 4.3 %copy-start.1 = (bf16[192,256]{1,0:T(8,128)(2,1)S(1)}, bf16[192,256]{1,0:T(8,128)(2,1)}, u32[]{:S(2)}) copy-start(bf16[192,256]{1,0:T(8,128)(2,1)} %param.13) | copy-start | bytes 294916
  181.3 74.6 %copy-start.2 = (f32[384]{0:T(512)S(1)}, f32[384]{0:T(512)}, u32[]{:S(2)}) copy-start(f32[384]{0:T(512)} %param.18) | copy-start | bytes 4612
Sparse Core Ops, SparseCore 0:
  10.1 141.5 all-gather.1
where the time goes:
time: 268 us; the launch traced here: 264 us
  waiting for transfers between devices  137 us (51%)
  local copies, waits for them, and re-layouts  55.4 us (21%)
  blocking collectives  32.3 us (12%)
  between operations  14.8 us (6%)
  matrix products  11.6 us (4%)
  other arithmetic  7.76 us (3%)
  loops' own time  5.29 us (2%)
    all_gather x1, waiting for transfers between devices, shards(): gathered = lax.all_gather(stale_pairs, 'patch', axis=1, tiled=True)  136 us
    all_gather x1, blocking collectives, shards(): lax.all_gather(attended, 'head', axis=1, tiled=True)  32.3 us
    dynamic_slice x16, local copies, waits for them, and re-layouts, absorb_rows(): lax.scan(advance, softmax_state, (key_blocks, value_blocks, jnp.arange(bl...  22.9 us
    slice x1, local copies, waits for them, and re-layouts, shards(): gathered[1].reshape(whole_rows, local_heads, head_width)  10.2 us
    another operation x1, local copies, waits for them, and re-layouts, absorb_rows(): key_rows.reshape(block_count, block_rows, key_rows.shape[1], key_rows.sha...  9.75 us
    another operation x1, local copies, waits for them, and re-layouts, absorb_rows(): value_rows.reshape(block_count, block_rows, value_rows.shape[1], value_ro...  9.72 us
    dot_general x9, matrix products, absorb(): jnp.einsum('qhk,khd->qhd', weights.astype(jnp.bfloat16), value_block, pre...  5.42 us
  transfers between devices with their start and end apart: 1, of which 1 were waited for; matrix products, arithmetic and copies ran while one was open for 3% of the time, Pallas kernels for 0%

commit v1 on v0

v1 whole, which is shorter than its diff:
```python
import functools

import jax
import jax.numpy as jnp
import numpy as np
from jax import lax
from jax.experimental import pallas as pl
from jax.experimental.pallas import tpu as pltpu
from jax.sharding import PartitionSpec as P

BF16 = jnp.bfloat16
F32 = jnp.float32
TOKENS = 192
HEAD = 128
WIDTH = 256
HEADS_HERE = 2
STAT_ROWS = 16
ROWS_SENT = TOKENS + STAT_ROWS
CHUNK = 4
LOG2E = 1.4426950408889634
VMEM_LIMIT = 48 * 1024 * 1024

QUERY_GROUPS = [
    [x * 32 + (2 * pair + z) * 2 + core for z in range(2) for x in range(2)]
    for pair in range(8)
    for core in range(2)
]
KEY_GROUPS = [
    [x * 32 + (2 * step + z) * 2 + core for step in range(8) for core in range(2)]
    for x in range(2)
    for z in range(2)
]


def place_in(groups):
    place = np.zeros(64, np.int32)
    for group in groups:
        for at, member in enumerate(group):
            place[member] = at
    return jnp.asarray(place)


def prepare_body(q_ref, k_ref, q_gain_ref, k_gain_ref, cos_ref, sin_ref, q_out, k_out):
    cosine, signed_sine = cos_ref[...], sin_ref[...]
    for raw, gain, out in ((q_ref, q_gain_ref, q_out), (k_ref, k_gain_ref, k_out)):
        for h in range(HEADS_HERE):
            cols = slice(h * HEAD, (h + 1) * HEAD)
            x = raw[:, cols].astype(F32)
            squares = jnp.mean(x * x, axis=-1, keepdims=True)
            n = x * lax.rsqrt(squares + 1e-06) * gain[...]
            out[:, cols] = (n * cosine + pltpu.roll(n, HEAD // 2, 1) * signed_sine).astype(BF16)


def prepare(query_raw, key_raw, query_gain, key_gain, cosine, signed_sine):
    shape = jax.ShapeDtypeStruct((TOKENS, WIDTH), BF16)
    return pl.pallas_call(
        prepare_body,
        out_shape=(shape, shape),
        name="norm_rotate",
    )(query_raw, key_raw, query_gain[None], key_gain[None], cosine, signed_sine)


def scores_of(q, k):
    return lax.dot_general(q, k, (((1,), (1,)), ((), ())), preferred_element_type=F32)


def attend_body(
    place_ref, q_ref, kv_ref, fresh_k_ref, fresh_v_ref, out_ref, peak_ref, total_ref, sum_ref
):
    step = pl.program_id(0)
    steps = pl.num_programs(0)
    scale = HEAD**-0.5 * LOG2E
    rows = q_ref.shape[0]
    keys = CHUNK * TOKENS
    block = 256

    def first(q, k, v):
        s = scores_of(q, k)
        peak = jnp.max(s, axis=-1, keepdims=True) * scale
        p = jnp.exp2(s * scale - peak)
        total = jnp.sum(p, axis=-1, keepdims=True)
        return peak, total, jnp.dot(p.astype(BF16), v, preferred_element_type=F32)

    def store(h, at, size, peak, total, acc):
        peak_ref[h, pl.ds(at, size), :] = jnp.broadcast_to(peak, (size, HEAD))
        total_ref[h, pl.ds(at, size), :] = jnp.broadcast_to(total, (size, HEAD))
        sum_ref[h, pl.ds(at, size), :] = acc

    @pl.when(step == 0)
    def _():
        mine = pl.multiple_of(place_ref[0] * TOKENS, TOKENS)
        slot = lax.rem(place_ref[1], CHUNK)
        for h in range(HEADS_HERE):
            cols = slice(h * HEAD, (h + 1) * HEAD)
            k = kv_ref[:, 0, :, cols].reshape(keys, HEAD)
            v = kv_ref[:, 1, :, cols].reshape(keys, HEAD)
            for r in range(rows // block):
                store(h, r * block, block, *first(q_ref[r * block : (r + 1) * block, cols], k, v))
            fresh_k, fresh_v = fresh_k_ref[:, cols], fresh_v_ref[:, cols]
            k = jnp.concatenate(
                [jnp.where(slot == t, fresh_k, kv_ref[t, 0, :, cols]) for t in range(CHUNK)]
            )
            v = jnp.concatenate(
                [jnp.where(slot == t, fresh_v, kv_ref[t, 1, :, cols]) for t in range(CHUNK)]
            )
            store(h, mine, TOKENS, *first(q_ref[pl.ds(mine, TOKENS), cols], k, v))

    @pl.when(step > 0)
    def _():
        for h in range(HEADS_HERE):
            cols = slice(h * HEAD, (h + 1) * HEAD)
            k = kv_ref[:, 0, :, cols].reshape(keys, HEAD)
            v = kv_ref[:, 1, :, cols].reshape(keys, HEAD)
            for r in range(rows // block):
                at = slice(r * block, (r + 1) * block)
                s = scores_of(q_ref[at, cols], k)
                before = peak_ref[h, at, :1]
                peak = jnp.maximum(before, jnp.max(s, axis=-1, keepdims=True) * scale)
                p = jnp.exp2(s * scale - peak)
                shrink = jnp.exp2(before - peak)
                total = total_ref[h, at, :1] * shrink + jnp.sum(p, axis=-1, keepdims=True)
                acc = sum_ref[h, at, :] * shrink + jnp.dot(
                    p.astype(BF16), v, preferred_element_type=F32
                )
                store(h, r * block, block, peak, total, acc)

    @pl.when(step == steps - 1)
    def _():
        lane = lax.broadcasted_iota(jnp.int32, (TOKENS, HEAD), 1)
        for g in range(rows // TOKENS):
            at = slice(g * TOKENS, (g + 1) * TOKENS)
            stats = jnp.zeros((TOKENS, HEAD), F32)
            for h in range(HEADS_HERE):
                cols = slice(h * HEAD, (h + 1) * HEAD)
                total = total_ref[h, at, :]
                out_ref[g, :TOKENS, cols] = (sum_ref[h, at, :] / total).astype(BF16)
                level = peak_ref[h, at, :] + jnp.log2(total)
                high = level.astype(BF16).astype(F32)
                middle = (level - high).astype(BF16).astype(F32)
                low = level - high - middle
                for piece, value in enumerate((high, middle, low)):
                    stats = jnp.where(lane == 3 * h + piece, value, stats)
            flat = jnp.transpose(stats)[:STAT_ROWS]
            out_ref[g, TOKENS:, :] = jnp.concatenate(
                [flat, jnp.zeros((STAT_ROWS, WIDTH - TOKENS), F32)], axis=1
            ).astype(BF16)


def attend(places, queries, pairs, fresh_keys, values_now):
    rows = queries.shape[0]
    steps = pairs.shape[0] // CHUNK
    whole = lambda i, place: (0, 0)
    return pl.pallas_call(
        attend_body,
        grid_spec=pltpu.PrefetchScalarGridSpec(
            num_scalar_prefetch=1,
            grid=(steps,),
            in_specs=[
                pl.BlockSpec((rows, WIDTH), whole),
                pl.BlockSpec(
                    (CHUNK, 2, TOKENS, WIDTH),
                    lambda i, place: (lax.rem(place[1] // CHUNK + i, steps), 0, 0, 0),
                ),
                pl.BlockSpec((TOKENS, WIDTH), whole),
                pl.BlockSpec((TOKENS, WIDTH), whole),
            ],
            out_specs=pl.BlockSpec(
                (rows // TOKENS, ROWS_SENT, WIDTH), lambda i, place: (0, 0, 0)
            ),
            scratch_shapes=[pltpu.VMEM((HEADS_HERE, rows, HEAD), F32)] * 3,
        ),
        out_shape=jax.ShapeDtypeStruct((rows // TOKENS, ROWS_SENT, WIDTH), BF16),
        compiler_params=pltpu.CompilerParams(vmem_limit_bytes=VMEM_LIMIT),
        name="attend",
    )(places, queries, pairs, fresh_keys, values_now)


def merge_body(parts_ref, out_ref):
    count = parts_ref.shape[0]
    levels = []
    for g in range(count):
        flat = parts_ref[g, TOKENS:, :].astype(F32)
        tall = jnp.concatenate([flat, jnp.zeros((HEAD - STAT_ROWS, WIDTH), F32)])
        levels.append(jnp.transpose(tall)[:TOKENS])
    for h in range(HEADS_HERE):
        cols = slice(h * HEAD, (h + 1) * HEAD)
        level = [
            s[:, 3 * h : 3 * h + 1] + s[:, 3 * h + 1 : 3 * h + 2] + s[:, 3 * h + 2 : 3 * h + 3]
            for s in levels
        ]
        top = functools.reduce(jnp.maximum, level)
        weights = [jnp.exp2(one - top) for one in level]
        acc = sum(
            w * parts_ref[g, :TOKENS, cols].astype(F32) for g, w in enumerate(weights)
        )
        merged = (acc / sum(weights)).astype(BF16)
        for copy in range(out_ref.shape[0]):
            out_ref[copy, :, cols] = merged


def merge(parts, copies):
    return pl.pallas_call(
        merge_body,
        out_shape=jax.ShapeDtypeStruct((copies, TOKENS, WIDTH), BF16),
        name="merge",
    )(parts)


def project_body(parts_ref, weight_ref, gate_ref, out_ref):
    acc = jnp.dot(parts_ref[0], weight_ref[:WIDTH], preferred_element_type=F32)
    for g in range(1, parts_ref.shape[0]):
        acc += jnp.dot(
            parts_ref[g], weight_ref[g * WIDTH : (g + 1) * WIDTH], preferred_element_type=F32
        )
    out_ref[...] = (acc * gate_ref[...]).astype(BF16)


def project(parts, out_weight, attn_gate):
    return pl.pallas_call(
        project_body,
        out_shape=jax.ShapeDtypeStruct((TOKENS, out_weight.shape[1]), BF16),
        compiler_params=pltpu.CompilerParams(vmem_limit_bytes=VMEM_LIMIT),
        name="project",
    )(parts, out_weight, attn_gate[None])


def shards(
    query_raw,
    key_raw,
    value_raw,
    stale_pairs,
    query_gain,
    key_gain,
    patch_offsets,
    attn_gate,
    out_weight,
):
    pairs = lax.all_gather(stale_pairs, "patch", axis=0, axis_index_groups=KEY_GROUPS)
    positions = patch_offsets[0] + jnp.arange(TOKENS, dtype=jnp.int32)
    frequency = jnp.exp(
        -(2.0 * jnp.arange(HEAD // 2, dtype=F32) / HEAD) * jnp.log(256.0)
    )
    angles = positions.astype(F32)[:, None] * frequency
    cosine, sine = jnp.cos(angles), jnp.sin(angles)
    queries, fresh_keys = prepare(
        query_raw,
        key_raw,
        query_gain,
        key_gain,
        jnp.concatenate([cosine, cosine], axis=1),
        jnp.concatenate([-sine, sine], axis=1),
    )
    group_queries = lax.all_gather(
        queries, "patch", axis=0, tiled=True, axis_index_groups=QUERY_GROUPS
    )
    me = lax.axis_index("patch")
    places = jnp.stack([place_in(QUERY_GROUPS)[me], place_in(KEY_GROUPS)[me]])
    parts = attend(places, group_queries, pairs, fresh_keys, value_raw)
    parts = lax.all_to_all(
        parts, "patch", split_axis=0, concat_axis=0, tiled=True, axis_index_groups=QUERY_GROUPS
    )
    copies = merge(parts, 8)
    all_heads = lax.all_to_all(copies, "head", split_axis=0, concat_axis=0, tiled=True)
    return (project(all_heads, out_weight, attn_gate), fresh_keys)


def solution(mesh):
    return jax.shard_map(
        shards,
        mesh=mesh,
        in_specs=(
            P("patch", "head"),
            P("patch", "head"),
            P("patch", "head"),
            P(None, "patch", "head"),
            P(),
            P(),
            P("patch"),
            P("head"),
            P(None, "head"),
        ),
        out_specs=(P("patch", "head"), P("patch", "head")),
        check_vma=False,
    )
```

time: 268 us -> 135 us (0.50); the launches traced: 264 us -> 134 us
  waiting for transfers between devices: 137 us -> 62.1 us
  local copies, waits for them, and re-layouts: 55.4 us -> 6.11 us
  Pallas kernels: 0 us -> 20.2 us
  matrix products: 11.6 us -> 0 us
  blocking collectives: 32.3 us -> 23.1 us
  other arithmetic: 7.76 us -> 2.44 us
  loops' own time: 5.29 us -> 0 us
  starting transfers between devices: 0.04 us -> 5.24 us
    all_gather x1, waiting for transfers between devices: 136 us -> 48.5 us  [shards(): lax.all_gather(stale_pairs, 'patch', axis=0, axis_index_groups=KEY_GROUPS)]
    all_gather x1, blocking collectives: 32.3 us -> 11.6 us  [shards(): lax.all_gather(queries, 'patch', axis=0, tiled=True, axis_index_groups=QU...]
    dynamic_slice x16 -> x2, local copies, waits for them, and re-layouts: 22.9 us -> 2.42 us  [shards(): places = jnp.stack([place_in(QUERY_GROUPS)[me], place_in(KEY_GROUPS)[me]])]
    pallas_call x0 -> x4, Pallas kernels: none -> 20.2 us  [the longest x1 14.2 us: attend(): pl.pallas_call(attend_body, grid_spec=pltpu.PrefetchScalarGridSpec(num_sc...]
    another operation x2 -> x0, local copies, waits for them, and re-layouts: 19.5 us -> none  [the longest x1 9.75 us: absorb_rows(): key_rows.reshape(block_count, block_rows, key_rows.shape[1], key_rows.sha...]
    all_to_all x0 -> x1, waiting for transfers between devices: none -> 12.9 us  [shards(): lax.all_to_all(copies, 'head', split_axis=0, concat_axis=0, tiled=True)]
    all_to_all x0 -> x1, blocking collectives: none -> 11.6 us  [shards(): lax.all_to_all(parts, 'patch', split_axis=0, concat_axis=0, tiled=True, a...]
    dot_general x19 -> x0, matrix products: 11.6 us -> none  [the longest x9 5.42 us: absorb(): jnp.einsum('qhk,khd->qhd', weights.astype(jnp.bfloat16), value_block, pre...]
  transfers between devices with their start and end apart: 1 -> 2, of which waited for: 1 -> 2; matrix products, arithmetic and copies ran while one was open for 3% -> 4% of each run, Pallas kernels for 0% -> 2%
where the time goes in v1:
time: 135 us; the launch traced here: 134 us
  waiting for transfers between devices  62.1 us (46%)
  blocking collectives  23.1 us (17%)
  Pallas kernels  20.2 us (15%)
  between operations  14.7 us (11%)
  local copies, waits for them, and re-layouts  6.11 us (5%)
  starting transfers between devices  5.24 us (4%)
  other arithmetic  2.44 us (2%)
    all_gather x1, waiting for transfers between devices, shards(): lax.all_gather(stale_pairs, 'patch', axis=0, axis_index_groups=KEY_GROUPS)  48.5 us
    pallas_call x1, Pallas kernels, attend(): pl.pallas_call(attend_body, grid_spec=pltpu.PrefetchScalarGridSpec(num_sc...  14.2 us
    all_to_all x1, waiting for transfers between devices, shards(): lax.all_to_all(copies, 'head', split_axis=0, concat_axis=0, tiled=True)  12.9 us
    all_gather x1, blocking collectives, shards(): lax.all_gather(queries, 'patch', axis=0, tiled=True, axis_index_groups=QU...  11.6 us
    all_to_all x1, blocking collectives, shards(): lax.all_to_all(parts, 'patch', split_axis=0, concat_axis=0, tiled=True, a...  11.6 us
    all_to_all x1, starting transfers between devices, shards(): lax.all_to_all(copies, 'head', split_axis=0, concat_axis=0, tiled=True)  5.21 us
    unnamed x10, local copies, waits for them, and re-layouts  3.68 us
  transfers between devices with their start and end apart: 2, of which 2 were waited for; matrix products, arithmetic and copies ran while one was open for 4% of the time, Pallas kernels for 2%

profile of v1, /device:TPU:1, one launch (start us, length us, event | category | flops | bytes accessed | tf_op | source)
XLA Modules:
  0.0 133.9 jit_solution(1556637896479949209)
XLA Ops:
  7.2 0.0 all-gather.3.cloned.1.call-start
  7.2 0.7 all-gather.3.cloned.1.call-update
  8.5 1.2 dynamic_slice.6
  9.8 1.2 dynamic_slice.7
  11.0 0.4 fusion
  11.4 0.8 pad_maximum_fusion
  12.2 2.2 %norm_rotate.1 = (bf16[192,256]{1,0:T(8,128)(2,1)}, bf16[192,256]{1,0:T(8,128)(2,1)}) custom-call(bf16[192,256]{1,0:T(8,128)(2,1)} %q_ref.1, bf16[192,256]{1,0:T(8,128)(2,1)} %k_ref.1, f32[1,128]{1,0:T(1,128)} %bitcast.6, f32[1,128]{1,0:T(1,128)} %bitcast.7, f32[192,128]{1,0:T(8,128)} %get-tuple-element.9.cos_ref, f32[192,128]{1,0:T(8,128)} %get-tuple-element.10.sin_ref), custom_call_target="tpu_custom_call" | custom-call | tf_op jit(solution)/shard_map/norm_rotate/pallas_call | solution.py:56
  14.5 1.2 pad_add_fusion.place_ref
  15.7 11.6 %all_gather.9.q_ref = bf16[768,256]{1,0:T(8,128)(2,1)S(1)} all-gather(bf16[192,256]{1,0:T(8,128)(2,1)} %get-tuple-element.4), channel_id=1, replica_groups={{0,256,16,272},{8,264,24,280},{32,288,48,304},{40,296,56,312},{64,320,8..., dimensions={0}, use_global_device_ids=true | all-gather | bytes 491520 | tf_op jit(solution)/shard_map/all_gather | solution.py:253
  27.2 48.5 %all-gather.3.cloned.1.call-done = bf16[32,192,256]{2,1,0:T(8,128)(2,1)} async-done(((bf16[2,192,256]{2,1,0:T(8,128)(2,1)}), bf16[32,192,256]{2,1,0:T(8,128)(2,1)}) %all-gather.3.cloned.1.call-update) | async-done | bytes 3145744 | tf_op jit(solution)/shard_map/all_gather | solution.py:238
  75.7 0.0 copy-start
  75.7 1.9 %copy-done = bf16[32,192,256]{2,1,0:T(8,128)(2,1)S(1)} copy-done((bf16[32,192,256]{2,1,0:T(8,128)(2,1)S(1)}, bf16[32,192,256]{2,1,0:T(8,128)(2,1)}, u32[]{:S(2)}) %copy-start) | copy-done | bytes 3145752
  77.6 0.0 copy-start.2
  77.6 0.9 copy-done.2
  78.5 0.0 copy-start.3
  78.5 0.9 copy-done.3
  79.4 0.0 copy-start.4
  79.4 0.0 copy-start.1
  79.4 14.2 %attend.1 = bf16[4,208,256]{2,1,0:T(8,128)(2,1)S(1)} custom-call(s32[2]{0:T(128)S(1)} %pad_add_fusion.place_ref, bf16[768,256]{1,0:T(8,128)(2,1)S(1)} %all_gather.9.q_ref, bf16[16,2,192,256]{3,2,1,0:T(8,128)(2,1)S(1)} %bitcast.5, bf16[192,256]{1,0:T(8,128)(2,1)S(1)} %copy-done.3, bf16[192,256]{1,0:T(8,128)(2,1)S(1)} %copy-done.2), custom_call_target="tpu_custom_call" | custom-call | tf_op jit(solution)/shard_map/attend/pallas_call | solution.py:153
  93.7 11.6 %all_to_all.10.parts_ref = bf16[4,208,256]{2,1,0:T(8,128)(2,1)} all-to-all(bf16[4,208,256]{2,1,0:T(8,128)(2,1)S(1)} %attend.1), channel_id=1, replica_groups={{0,256,16,272},{8,264,24,280},{32,288,48,304},{40,296,56,312},{64,320,8..., dimensions={0} | all-to-all | bytes 851968 | tf_op jit(solution)/shard_map/all_to_all | solution.py:259
  105.2 2.5 %merge.1 = bf16[8,192,256]{2,1,0:T(8,128)(2,1)} custom-call(bf16[4,208,256]{2,1,0:T(8,128)(2,1)} %all_to_all.10.parts_ref), custom_call_target="tpu_custom_call" | custom-call | tf_op jit(solution)/shard_map/merge/pallas_call | solution.py:202
  107.8 5.2 %all-to-all-start.1 = ((bf16[8,192,256]{2,1,0:T(8,128)(2,1)}), bf16[8,192,256]{2,1,0:T(8,128)(2,1)S(1)}, u32[]{:S(2)}, u32[]{:S(2)}) async-start(bf16[8,192,256]{2,1,0:T(8,128)(2,1)} %merge.1), calls=%async_computation.1 | async-start | bytes 1572864 | tf_op jit(solution)/shard_map/all_to_all | solution.py:263
  113.0 0.0 copy-done.4
  113.0 12.9 %all-to-all-done.1.parts_ref = bf16[8,192,256]{2,1,0:T(8,128)(2,1)S(1)} async-done(((bf16[8,192,256]{2,1,0:T(8,128)(2,1)}), bf16[8,192,256]{2,1,0:T(8,128)(2,1)S(1)}, u32[]{:S(2)}, u32[]{:S(2)}) %all-to-all-start.1) | async-done | bytes 786464 | tf_op jit(solution)/shard_map/all_to_all | solution.py:263
  125.9 0.0 copy-done.1
  125.9 1.2 project.1
  (3 shorter events, 0.0 us)
Async XLA Ops:
  7.2 68.6 %all-gather.3.cloned.1.call-start = ((), (), s32[]{:S(2)}) async-start(), calls=%async_computation.2 | async-start | bytes 3342336 | tf_op jit(solution)/shard_map/all_gather | solution.py:238
  75.7 1.9 %copy-start = (bf16[32,192,256]{2,1,0:T(8,128)(2,1)S(1)}, bf16[32,192,256]{2,1,0:T(8,128)(2,1)}, u32[]{:S(2)}) copy-start(bf16[32,192,256]{2,1,0:T(8,128)(2,1)} %all-gather.3.cloned.1.call-done) | copy-start | bytes 9437188
  77.6 0.9 copy-start.2
  78.5 0.9 copy-start.3
  79.4 33.5 %copy-start.4 = (f32[384]{0:T(512)S(1)}, f32[384]{0:T(512)}, u32[]{:S(2)}) copy-start(f32[384]{0:T(512)} %param.18) | copy-start | bytes 4612
  79.4 46.4 %copy-start.1 = (bf16[2048,384]{1,0:T(8,128)(2,1)S(1)}, bf16[2048,384]{1,0:T(8,128)(2,1)}, u32[]{:S(2)}) copy-start(bf16[2048,384]{1,0:T(8,128)(2,1)} %weight_ref.1) | copy-start | bytes 4718596
  107.8 18.1 %all-to-all-start.1 = ((bf16[8,192,256]{2,1,0:T(8,128)(2,1)}), bf16[8,192,256]{2,1,0:T(8,128)(2,1)S(1)}, u32[]{:S(2)}, u32[]{:S(2)}) async-start(bf16[8,192,256]{2,1,0:T(8,128)(2,1)} %merge.1), calls=%async_computation.1 | async-start | bytes 1572864 | tf_op jit(solution)/shard_map/all_to_all | solution.py:263
Sparse Core Ops, SparseCore 0:
  10.1 65.5 all-gather.2

commit v2 on v1

v2 whole, which is shorter than its diff:
```python
import functools

import jax
import jax.numpy as jnp
from jax import lax
from jax.experimental import pallas as pl
from jax.experimental.pallas import tpu as pltpu
from jax.sharding import PartitionSpec as P

BF16 = jnp.bfloat16
F32 = jnp.float32
TOKENS = 192
HEAD = 128
WIDTH = 256
HEADS_HERE = 2
STAT_ROWS = 16
ROWS_SENT = TOKENS + STAT_ROWS
LOG2E = 1.4426950408889634
VMEM_LIMIT = 48 * 1024 * 1024

PATCHES = 64
CORES = [[i, i + 1] for i in range(0, PATCHES, 2)]
QUERY_GROUPS = [
    [x * 32 + (2 * pair + z) * 2 + core for core in range(2) for x in range(2) for z in range(2)]
    for pair in range(8)
]


def swapped(bit):
    return [(i, i ^ bit) for i in range(PATCHES)]


def ring_swaps(first):
    pairs = []
    for i in range(PATCHES):
        z, core = i % 32 // 2, i % 2
        odd = z // 2 % 2
        by = 2 - 4 * odd if first == (core == 0) else 4 * odd - 2
        pairs.append((i, i // 32 * 32 + (z + by) % 16 * 2 + core))
    return pairs


def prepare_body(
    core_ref, q_ref, k_ref, v_ref, q_gain_ref, k_gain_ref, cos_ref, sin_ref, k_out, mine_out, send_out
):
    cosine, signed_sine = cos_ref[...], sin_ref[...]
    first = core_ref[0] == 0

    def put(part, heads):
        mine_out[part] = jnp.where(first, heads[0], heads[1])
        send_out[part] = jnp.where(first, heads[1], heads[0])

    for part, (raw, gain) in enumerate(((q_ref, q_gain_ref), (k_ref, k_gain_ref))):
        heads = []
        for h in range(HEADS_HERE):
            cols = slice(h * HEAD, (h + 1) * HEAD)
            x = raw[:, cols].astype(F32)
            squares = jnp.mean(x * x, axis=-1, keepdims=True)
            n = x * lax.rsqrt(squares + 1e-06) * gain[...]
            turned = (n * cosine + pltpu.roll(n, HEAD // 2, 1) * signed_sine).astype(BF16)
            heads.append(turned)
            if part == 1:
                k_out[:, cols] = turned
        put(part, heads)
    put(2, [v_ref[:, :HEAD], v_ref[:, HEAD:]])


def prepare(core, query_raw, key_raw, value_raw, query_gain, key_gain, cosine, signed_sine):
    halves = jax.ShapeDtypeStruct((3, TOKENS, HEAD), BF16)
    return pl.pallas_call(
        prepare_body,
        in_specs=[pl.BlockSpec(memory_space=pltpu.SMEM)]
        + [pl.BlockSpec(memory_space=pltpu.VMEM)] * 7,
        out_shape=(jax.ShapeDtypeStruct((TOKENS, WIDTH), BF16), halves, halves),
        name="norm_rotate",
    )(core, query_raw, key_raw, value_raw, query_gain[None], key_gain[None], cosine, signed_sine)


def attend_body(share_count, begins, ends, *refs):
    refs = list(refs)
    take = lambda count: [refs.pop(0) for _ in range(count)]
    scale = HEAD**-0.5 * LOG2E
    place_ref = take(1)[0] if begins or ends else None
    q_refs = take(2)
    fresh_refs = take(2) if begins else None
    before = None if begins else take(3)
    shares = take(share_count)
    half = q_refs[0].shape[0]

    def rows_of(part, patch=None):
        if ends:
            picked = [shares[part][core] for core in range(2)]
        else:
            picked = [share[part, core] for share in shares for core in range(2)]
        if patch is not None:
            at = jnp.bitwise_xor(place_ref[1], patch)
            new = fresh_refs[patch][1 + part]
            picked = [jnp.where(at == core, new, old) for core, old in enumerate(picked)]
        return jnp.concatenate(picked)

    size = 2 * TOKENS
    blocks = [(at, size, None) for at in range(0, 2 * half, size)]
    if begins:
        blocks[:1] = [(0, TOKENS, 0), (TOKENS, TOKENS, 1)]
    usual = rows_of(0), rows_of(1)

    def scores_of(block):
        at, size, patch = block
        k = usual[0] if patch is None else rows_of(0, patch)
        q = q_refs[at // half][at % half : at % half + size, :]
        return lax.dot_general(q, k, (((1,), (1,)), ((), ())), preferred_element_type=F32)

    def finish(at, size, peak, total, acc):
        total = jnp.sum(total, axis=-1, keepdims=True)
        level = peak + jnp.log2(total)
        high = level.astype(BF16).astype(F32)
        middle = (level - high).astype(BF16).astype(F32)
        low = level - high - middle
        lane = lax.broadcasted_iota(jnp.int32, (size, HEAD), 1)
        packed = jnp.where(lane == 0, high, jnp.where(lane == 1, middle, low))
        out = (acc / total).astype(BF16)
        for g in range(at // TOKENS, (at + size) // TOKENS):
            rows = slice(g * TOKENS - at, (g + 1) * TOKENS - at)
            to = jnp.bitwise_xor(place_ref[1], g % 2) * 4 + jnp.bitwise_xor(place_ref[0], g // 2)
            refs[0][to, :TOKENS, :] = out[rows]
            flat = jnp.transpose(packed[rows])[:8]
            rest = jnp.concatenate([flat[:, HEAD:], jnp.zeros((8, 2 * HEAD - TOKENS), F32)], axis=1)
            refs[0][to, TOKENS:, :] = jnp.concatenate([flat[:, :HEAD], rest]).astype(BF16)

    following = scores_of(blocks[0])
    for index, (at, size, patch) in enumerate(blocks):
        s = following
        if index + 1 < len(blocks):
            following = scores_of(blocks[index + 1])
        rows = slice(at, at + size)
        tiles = [s[:, t * HEAD : (t + 1) * HEAD] for t in range(s.shape[1] // HEAD)]
        peak = jnp.max(functools.reduce(jnp.maximum, tiles), axis=-1, keepdims=True) * scale
        if begins:
            peak = jnp.broadcast_to(peak, (size, HEAD))
        else:
            peak_before = before[0][rows, :]
            peak = jnp.maximum(peak_before, peak)
        tiles = [jnp.exp2(tile * scale - peak) for tile in tiles]
        total = functools.reduce(jnp.add, tiles)
        p = jnp.concatenate([tile.astype(BF16) for tile in tiles], axis=1)
        v = usual[1] if patch is None else rows_of(1, patch)
        acc = jnp.dot(p, v, preferred_element_type=F32)
        if not begins:
            shrink = jnp.exp2(peak_before - peak)
            total += before[1][rows, :] * shrink
            acc += before[2][rows, :] * shrink
        if ends:
            finish(at, size, peak, total, acc)
        else:
            for ref, value in zip(refs, (peak, total, acc), strict=True):
                ref[rows, :] = value


def attend(queries, shares, fresh=(), state=(), place=None, ends=False):
    rows = 2 * queries[0].shape[0]
    begins = bool(fresh)
    operands = [*queries, *fresh, *state, *shares]
    specs = [pl.BlockSpec(memory_space=pltpu.VMEM)] * len(operands)
    if begins or ends:
        operands.insert(0, place)
        specs.insert(0, pl.BlockSpec(memory_space=pltpu.SMEM))
    if ends:
        out_shape = jax.ShapeDtypeStruct((rows // TOKENS, ROWS_SENT, HEAD), BF16)
    else:
        out_shape = (jax.ShapeDtypeStruct((rows, HEAD), F32),) * 3
    key_count = 2 * TOKENS * (1 if ends else len(shares))
    return pl.pallas_call(
        functools.partial(attend_body, len(shares), begins, ends),
        in_specs=specs,
        out_shape=out_shape,
        compiler_params=pltpu.CompilerParams(vmem_limit_bytes=VMEM_LIMIT),
        cost_estimate=pl.CostEstimate(
            flops=4 * rows * key_count * HEAD,
            bytes_accessed=12 * rows * HEAD,
            transcendentals=rows * key_count,
        ),
        name="attend",
    )(*operands)


def merge_body(parts_ref, out_ref):
    count = parts_ref.shape[0]
    chips = count // HEADS_HERE
    weights = []
    for h in range(HEADS_HERE):
        levels = []
        for g in range(h * chips, (h + 1) * chips):
            flat = parts_ref[g, TOKENS:, :].astype(F32)
            wide = jnp.concatenate([flat[:8], flat[8:]], axis=1)
            levels.append(wide[0:1] + wide[1:2] + wide[2:3])
        top = functools.reduce(jnp.maximum, levels)
        weights += [jnp.exp2(one - top) for one in levels]
        whole = sum(weights[h * chips :])
        weights[h * chips :] = [one / whole for one in weights[h * chips :]]
    wide = jnp.concatenate(weights + [jnp.zeros((HEAD - count, 2 * HEAD), F32)])
    columns = jnp.transpose(wide)[:TOKENS]
    for h in range(HEADS_HERE):
        cols = slice(h * HEAD, (h + 1) * HEAD)
        merged = sum(
            columns[:, g : g + 1] * parts_ref[g, :TOKENS, :].astype(F32)
            for g in range(h * chips, (h + 1) * chips)
        ).astype(BF16)
        for copy in range(out_ref.shape[0]):
            out_ref[copy, :, cols] = merged


def merge(parts, copies):
    return pl.pallas_call(
        merge_body,
        out_shape=jax.ShapeDtypeStruct((copies, TOKENS, WIDTH), BF16),
        name="merge",
    )(parts)


def project_body(parts_ref, weight_ref, gate_ref, out_ref):
    acc = jnp.dot(parts_ref[0], weight_ref[:WIDTH], preferred_element_type=F32)
    for g in range(1, parts_ref.shape[0]):
        acc += jnp.dot(
            parts_ref[g], weight_ref[g * WIDTH : (g + 1) * WIDTH], preferred_element_type=F32
        )
    out_ref[...] = (acc * gate_ref[...]).astype(BF16)


def project(parts, out_weight, attn_gate):
    return pl.pallas_call(
        project_body,
        out_shape=jax.ShapeDtypeStruct((TOKENS, out_weight.shape[1]), BF16),
        compiler_params=pltpu.CompilerParams(vmem_limit_bytes=VMEM_LIMIT),
        name="project",
    )(parts, out_weight, attn_gate[None])


def shards(
    query_raw,
    key_raw,
    value_raw,
    stale_pairs,
    query_gain,
    key_gain,
    patch_offsets,
    attn_gate,
    out_weight,
):
    me = lax.axis_index("patch").astype(jnp.int32)
    core = me % 2

    def own_head(both):
        both = jnp.swapaxes(both, 0, 1)
        return lax.dynamic_slice_in_dim(both, core * HEAD, HEAD, axis=3)

    def over_cores(x):
        return lax.all_gather(x, "patch", axis=0, axis_index_groups=CORES)

    share = own_head(over_cores(stale_pairs))
    one, other = ring_swaps(True), ring_swaps(False)
    over_one, over_other = [share], [share]

    def step():
        block = over_other[-1]
        over_other.append(lax.ppermute(over_one[-1], "patch", other))
        over_one.append(lax.ppermute(block, "patch", one))

    step()
    step()
    step()
    positions = patch_offsets[0] + jnp.arange(TOKENS, dtype=jnp.int32)
    frequency = jnp.exp(
        -(2.0 * jnp.arange(HEAD // 2, dtype=F32) / HEAD) * jnp.log(256.0)
    )
    angles = positions.astype(F32)[:, None] * frequency
    cosine, sine = jnp.cos(angles), jnp.sin(angles)
    fresh_keys, mine, send = prepare(
        core[None],
        query_raw,
        key_raw,
        value_raw,
        query_gain,
        key_gain,
        jnp.concatenate([cosine, cosine], axis=1),
        jnp.concatenate([-sine, sine], axis=1),
    )
    theirs = lax.ppermute(send, "patch", swapped(1))
    near = jnp.concatenate([mine[0], theirs[0]])
    near = jnp.concatenate([near, lax.ppermute(near, "patch", swapped(2))])
    queries = (near, lax.ppermute(near, "patch", swapped(32)))
    place = jnp.stack([(me // 32) * 2 + (me // 2) % 2, core])
    state = attend(queries, [share], fresh=(mine, theirs), place=place)
    state = attend(queries, [over_one[1], over_other[1]], state=state)
    far_keys = lax.ppermute(over_other[3][0], "patch", one)
    far_values = lax.ppermute(over_one[3][1], "patch", other)
    state = attend(queries, [over_one[2], over_other[2]], state=state)
    state = attend(queries, [over_one[3], over_other[3]], state=state)
    parts = attend(queries, [far_keys, far_values], state=state, place=place, ends=True)
    parts = lax.all_to_all(
        parts, "patch", split_axis=0, concat_axis=0, tiled=True, axis_index_groups=QUERY_GROUPS
    )
    copies = merge(parts, 8)
    all_heads = lax.all_to_all(copies, "head", split_axis=0, concat_axis=0, tiled=True)
    return (project(all_heads, out_weight, attn_gate), fresh_keys)


def solution(mesh):
    return jax.shard_map(
        shards,
        mesh=mesh,
        in_specs=(
            P("patch", "head"),
            P("patch", "head"),
            P("patch", "head"),
            P(None, "patch", "head"),
            P(),
            P(),
            P("patch"),
            P("head"),
            P(None, "head"),
        ),
        out_specs=(P("patch", "head"), P("patch", "head")),
        check_vma=False,
    )
```

time: 135 us -> 109 us (0.81)
  waiting for transfers between devices: 62.1 us -> 20.6 us
  starting transfers between devices: 5.24 us -> 43.9 us
  between operations: 14.7 us -> 1.57 us
  local copies, waits for them, and re-layouts: 6.11 us -> 1.78 us
  Pallas kernels: 20.2 us -> 16.3 us
    all_gather x1 -> x0, waiting for transfers between devices: 48.5 us -> none  [shards(): lax.all_gather(stale_pairs, 'patch', axis=0, axis_index_groups=KEY_GROUPS)]
    ppermute x0 -> x11, starting transfers between devices: none -> 37.2 us  [the longest x3 13.1 us: step(): over_one.append(lax.ppermute(block, 'patch', one))]
    ppermute x0 -> x11, waiting for transfers between devices: none -> 7.06 us  [the longest x3 5.75 us: step(): over_other.append(lax.ppermute(over_one[-1], 'patch', other))]
    pallas_call x2 -> x6, Pallas kernels: 16.5 us -> 12.6 us  [the longest x5 10.2 us: attend(): pl.pallas_call(functools.partial(attend_body, len(shares), begins, ends),...]
    unnamed x10 -> x6, local copies, waits for them, and re-layouts: 3.68 us -> 0.91 us
    all_gather x1, blocking collectives: 11.6 us -> 8.81 us  [over_cores(): return lax.all_gather(x, 'patch', axis=0, axis_index_groups=CORES)]
    all_to_all x1, blocking collectives: 11.6 us -> 14.2 us  [shards(): lax.all_to_all(parts, 'patch', split_axis=0, concat_axis=0, tiled=True, a...]
    dynamic_slice x2 -> x1, local copies, waits for them, and re-layouts: 2.42 us -> 0.03 us  [own_head(): return lax.dynamic_slice_in_dim(both, core * HEAD, HEAD, axis=3)]
  transfers between devices with their start and end apart: 2 -> 12, of which waited for: 2 -> 5; matrix products, arithmetic and copies ran while one was open for 4% -> 2% of each run, Pallas kernels for 2% -> 10%
where the time goes in v2:
time: 109 us; the launch traced here: 108 us
  starting transfers between devices  43.9 us (40%)
  blocking collectives  23 us (21%)
  waiting for transfers between devices  20.6 us (19%)
  Pallas kernels  16.3 us (15%)
  local copies, waits for them, and re-layouts  1.78 us (2%)
  between operations  1.57 us (1%)
  other arithmetic  1.34 us (1%)
    all_to_all x1, blocking collectives, shards(): lax.all_to_all(parts, 'patch', split_axis=0, concat_axis=0, tiled=True, a...  14.2 us
    all_to_all x1, waiting for transfers between devices, shards(): lax.all_to_all(copies, 'head', split_axis=0, concat_axis=0, tiled=True)  13.5 us
    ppermute x3, starting transfers between devices, step(): over_one.append(lax.ppermute(block, 'patch', one))  13.1 us
    pallas_call x5, Pallas kernels, attend(): pl.pallas_call(functools.partial(attend_body, len(shares), begins, ends),...  10.2 us
    all_gather x1, blocking collectives, over_cores(): return lax.all_gather(x, 'patch', axis=0, axis_index_groups=CORES)  8.81 us
    ppermute x3, starting transfers between devices, step(): over_other.append(lax.ppermute(over_one[-1], 'patch', other))  8.45 us
    all_to_all x1, starting transfers between devices, shards(): lax.all_to_all(copies, 'head', split_axis=0, concat_axis=0, tiled=True)  6.66 us
    ppermute x3, waiting for transfers between devices, step(): over_other.append(lax.ppermute(over_one[-1], 'patch', other))  5.75 us
  transfers between devices with their start and end apart: 12, of which 5 were waited for; matrix products, arithmetic and copies ran while one was open for 2% of the time, Pallas kernels for 10%

profile of v2, /device:TPU:1, one launch (start us, length us, event | category | flops | bytes accessed | tf_op | source)
XLA Modules:
  0.0 108.5 jit_solution(12053304495101535791)
XLA Ops:
  0.6 8.8 %all-gather = bf16[4,192,256]{2,1,0:T(8,128)(2,1)S(1)} all-gather(bf16[2,192,256]{2,1,0:T(8,128)(2,1)} %param.12), channel_id=2, replica_groups={{0,8},{16,24},{32,40},{48,56},{64,72},{80,88},{96,104},{112,120},{128,1..., dimensions={0}, use_global_device_ids=true | all-gather | bytes 589824 | tf_op jit(solution)/shard_map/all_gather | solution.py:257
  9.5 6.2 %collective-permute-start.3 = (bf16[2,2,192,128]{3,2,1,0:T(8,128)(2,1)S(1)}, bf16[2,2,192,128]{3,2,1,0:T(8,128)(2,1)S(1)}, u32[]{:S(2)}, u32[]{:S(2)}) collective-permute-start(bf16[2,2,192,128]{3,2,1,0:T(8,128)(2,1)S(1)} %copy_bitcast_fusion.refs_5_), channel_id=1, source_target_pairs={{0,32},{8,232},{16,48},{24,248},{32,0},{40,72},{48,16},{56,88},{64... | collective-permute-start | bytes 589832 | tf_op jit(solution)/shard_map/ppermute | solution.py:266
  15.7 1.9 %collective-permute-start.4 = (bf16[2,2,192,128]{3,2,1,0:T(8,128)(2,1)S(1)}, bf16[2,2,192,128]{3,2,1,0:T(8,128)(2,1)S(1)}, u32[]{:S(2)}, u32[]{:S(2)}) collective-permute-start(bf16[2,2,192,128]{3,2,1,0:T(8,128)(2,1)S(1)} %copy_bitcast_fusion.refs_5_), channel_id=1, source_target_pairs={{0,224},{8,40},{16,240},{24,56},{32,64},{40,8},{48,80},{56,24},{64... | collective-permute-start | bytes 589832 | tf_op jit(solution)/shard_map/ppermute | solution.py:265
  18.3 0.4 fusion
  18.7 0.8 pad_maximum_fusion.1
  19.5 2.4 %norm_rotate.1 = (bf16[192,256]{1,0:T(8,128)(2,1)}, bf16[3,192,128]{2,1,0:T(8,128)(2,1)}, bf16[3,192,128]{2,1,0:T(8,128)(2,1)}) custom-call(s32[1]{0:T(128)} %bitcast.1.core_ref, bf16[192,256]{1,0:T(8,128)(2,1)} %q_ref.1, bf16[192,256]{1,0:T(8,128)(2,1)} %k_ref.1, bf16[192,256]{1,0:T(8,128)(2,1)} %v_ref.1, f32[1,128]{1,0:T(1,128)} %bitcast.18, ...), custom_call_target="tpu_custom_call" | custom-call | tf_op jit(solution)/shard_map/norm_rotate/pallas_call | solution.py:70
  21.9 4.0 %collective-permute-start = (bf16[3,192,128]{2,1,0:T(8,128)(2,1)}, bf16[3,192,128]{2,1,0:T(8,128)(2,1)S(1)}, u32[]{:S(2)}, u32[]{:S(2)}) collective-permute-start(bf16[3,192,128]{2,1,0:T(8,128)(2,1)} %get-tuple-element.18), channel_id=1, source_target_pairs={{0,8},{8,0},{16,24},{24,16},{32,40},{40,32},{48,56},{56,48},{64,72... | collective-permute-start | bytes 442376 | tf_op jit(solution)/shard_map/ppermute | solution.py:287
  25.9 0.8 slice_bitcast_fusion.3
  26.7 0.4 collective-permute-done.refs_4_
  27.1 2.6 %collective-permute-start.1 = (bf16[384,128]{1,0:T(8,128)(2,1)S(1)}, bf16[384,128]{1,0:T(8,128)(2,1)S(1)}, u32[]{:S(2)}, u32[]{:S(2)}) collective-permute-start(bf16[384,128]{1,0:T(8,128)(2,1)S(1)} %pad_maximum_fusion.3), channel_id=1, source_target_pairs={{0,16},{8,24},{16,0},{24,8},{32,48},{40,56},{48,32},{56,40},{64,80... | collective-permute-start | bytes 294920 | tf_op jit(solution)/shard_map/ppermute | solution.py:289
  29.8 0.0 collective-permute-done.4.refs_6_
  29.8 3.7 %collective-permute-start.5 = (bf16[2,2,192,128]{3,2,1,0:T(8,128)(2,1)S(1)}, bf16[2,2,192,128]{3,2,1,0:T(8,128)(2,1)S(1)}, u32[]{:S(2)}, u32[]{:S(2)}) collective-permute-start(bf16[2,2,192,128]{3,2,1,0:T(8,128)(2,1)S(1)} %collective-permute-done.4.refs_6_), channel_id=1, source_target_pairs={{0,32},{8,232},{16,48},{24,248},{32,0},{40,72},{48,16},{56,88},{64... | collective-permute-start | bytes 589832 | tf_op jit(solution)/shard_map/ppermute | solution.py:266
  33.5 0.0 collective-permute-done.3.refs_5_
  33.5 3.1 %collective-permute-start.6 = (bf16[2,2,192,128]{3,2,1,0:T(8,128)(2,1)S(1)}, bf16[2,2,192,128]{3,2,1,0:T(8,128)(2,1)S(1)}, u32[]{:S(2)}, u32[]{:S(2)}) collective-permute-start(bf16[2,2,192,128]{3,2,1,0:T(8,128)(2,1)S(1)} %collective-permute-done.3.refs_5_), channel_id=1, source_target_pairs={{0,224},{8,40},{16,240},{24,56},{32,64},{40,8},{48,80},{56,24},{64... | collective-permute-start | bytes 589832 | tf_op jit(solution)/shard_map/ppermute | solution.py:265
  36.6 0.0 collective-permute-done.1
  36.6 3.1 %collective-permute-start.2 = (bf16[768,128]{1,0:T(8,128)(2,1)S(1)}, bf16[768,128]{1,0:T(8,128)(2,1)S(1)}, u32[]{:S(2)}, u32[]{:S(2)}) collective-permute-start(bf16[768,128]{1,0:T(8,128)(2,1)S(1)} %pad_maximum_fusion.refs_1_.refs_0_), channel_id=1, source_target_pairs={{0,256},{8,264},{16,272},{24,280},{32,288},{40,296},{48,304},{56,3... | collective-permute-start | bytes 589832 | tf_op jit(solution)/shard_map/ppermute | solution.py:290
  39.8 4.7 %collective-permute-done.6.refs_6_ = bf16[2,2,192,128]{3,2,1,0:T(8,128)(2,1)S(1)} collective-permute-done((bf16[2,2,192,128]{3,2,1,0:T(8,128)(2,1)S(1)}, bf16[2,2,192,128]{3,2,1,0:T(8,128)(2,1)S(1)}, u32[]{:S(2)}, u32[]{:S(2)}) %collective-permute-start.6) | collective-permute-done | bytes 196640 | tf_op jit(solution)/shard_map/ppermute | solution.py:265
  44.5 3.1 %collective-permute-start.7 = (bf16[2,2,192,128]{3,2,1,0:T(8,128)(2,1)S(1)}, bf16[2,2,192,128]{3,2,1,0:T(8,128)(2,1)S(1)}, u32[]{:S(2)}, u32[]{:S(2)}) collective-permute-start(bf16[2,2,192,128]{3,2,1,0:T(8,128)(2,1)S(1)} %collective-permute-done.6.refs_6_), channel_id=1, source_target_pairs={{0,32},{8,232},{16,48},{24,248},{32,0},{40,72},{48,16},{56,88},{64... | collective-permute-start | bytes 589832 | tf_op jit(solution)/shard_map/ppermute | solution.py:266
  47.7 0.1 pad_add_fusion.refs_0_
  47.8 0.0 collective-permute-done.5.refs_5_
  47.8 3.4 %collective-permute-start.8 = (bf16[2,2,192,128]{3,2,1,0:T(8,128)(2,1)S(1)}, bf16[2,2,192,128]{3,2,1,0:T(8,128)(2,1)S(1)}, u32[]{:S(2)}, u32[]{:S(2)}) collective-permute-start(bf16[2,2,192,128]{3,2,1,0:T(8,128)(2,1)S(1)} %collective-permute-done.5.refs_5_), channel_id=1, source_target_pairs={{0,224},{8,40},{16,240},{24,56},{32,64},{40,8},{48,80},{56,24},{64... | collective-permute-start | bytes 589832 | tf_op jit(solution)/shard_map/ppermute | solution.py:265
  51.2 0.0 collective-permute-done.2.refs_2_.refs_1_
  51.2 0.0 copy-start.1
  51.2 0.9 copy-done.1
  52.1 1.7 %attend.5 = (f32[1536,128]{1,0:T(8,128)S(1)}, f32[1536,128]{1,0:T(8,128)S(1)}, f32[1536,128]{1,0:T(8,128)S(1)}) custom-call(s32[2]{0:T(128)S(1)} %pad_add_fusion.refs_0_, bf16[768,128]{1,0:T(8,128)(2,1)S(1)} %pad_maximum_fusion.refs_1_.refs_0_, bf16[768,128]{1,0:T(8,128)(2,1)S(1)} %collective-permute-done.2.refs_2_.refs_1_, ...), custom_call_target="tpu_custom_call" | custom-call | flops 301989888 | bytes 2359296 | tf_op jit(solution)/shard_map/attend/pallas_call | solution.py:172
  53.8 2.2 %attend.6 = (f32[1536,128]{1,0:T(8,128)S(1)}, f32[1536,128]{1,0:T(8,128)S(1)}, f32[1536,128]{1,0:T(8,128)S(1)}) custom-call(bf16[768,128]{1,0:T(8,128)(2,1)S(1)} %pad_maximum_fusion.refs_1_.refs_0_, bf16[768,128]{1,0:T(8,128)(2,1)S(1)} %collective-permute-done.2.refs_2_.refs_1_, f32[1536,128]{1,0:T(8,128)S(1)} %get-tuple-element.19.refs_2_, ...), custom_call_target="tpu_custom_call" | custom-call | flops 603979776 | bytes 2359296 | tf_op jit(solution)/shard_map/attend/pallas_call | solution.py:172
  56.0 0.0 collective-permute-done.7.refs_5_
  56.0 2.7 %collective-permute-start.10 = (bf16[2,192,128]{2,1,0:T(8,128)(2,1)S(1)}, bf16[2,192,128]{2,1,0:T(8,128)(2,1)S(1)}, u32[]{:S(2)}, u32[]{:S(2)}) collective-permute-start(bf16[2,192,128]{2,1,0:T(8,128)(2,1)S(1)} %slice_bitcast_fusion), channel_id=1, source_target_pairs={{0,224},{8,40},{16,240},{24,56},{32,64},{40,8},{48,80},{56,24},{64... | collective-permute-start | bytes 294920 | tf_op jit(solution)/shard_map/ppermute | solution.py:295
  58.7 1.0 collective-permute-done.8.refs_6_
  59.8 3.2 %collective-permute-start.9 = (bf16[2,192,128]{2,1,0:T(8,128)(2,1)S(1)}, bf16[2,192,128]{2,1,0:T(8,128)(2,1)S(1)}, u32[]{:S(2)}, u32[]{:S(2)}) collective-permute-start(bf16[2,192,128]{2,1,0:T(8,128)(2,1)S(1)} %slice_bitcast_fusion.1), channel_id=1, source_target_pairs={{0,32},{8,232},{16,48},{24,248},{32,0},{40,72},{48,16},{56,88},{64... | collective-permute-start | bytes 294920 | tf_op jit(solution)/shard_map/ppermute | solution.py:294
  63.0 2.2 %attend.7 = (f32[1536,128]{1,0:T(8,128)S(1)}, f32[1536,128]{1,0:T(8,128)S(1)}, f32[1536,128]{1,0:T(8,128)S(1)}) custom-call(bf16[768,128]{1,0:T(8,128)(2,1)S(1)} %pad_maximum_fusion.refs_1_.refs_0_, bf16[768,128]{1,0:T(8,128)(2,1)S(1)} %collective-permute-done.2.refs_2_.refs_1_, f32[1536,128]{1,0:T(8,128)S(1)} %get-tuple-element.22.refs_2_, ...), custom_call_target="tpu_custom_call" | custom-call | flops 603979776 | bytes 2359296 | tf_op jit(solution)/shard_map/attend/pallas_call | solution.py:172
  65.2 2.2 %attend.8 = (f32[1536,128]{1,0:T(8,128)S(1)}, f32[1536,128]{1,0:T(8,128)S(1)}, f32[1536,128]{1,0:T(8,128)S(1)}) custom-call(bf16[768,128]{1,0:T(8,128)(2,1)S(1)} %pad_maximum_fusion.refs_1_.refs_0_, bf16[768,128]{1,0:T(8,128)(2,1)S(1)} %collective-permute-done.2.refs_2_.refs_1_, f32[1536,128]{1,0:T(8,128)S(1)} %get-tuple-element.25.refs_2_, ...), custom_call_target="tpu_custom_call" | custom-call | flops 603979776 | bytes 2359296 | tf_op jit(solution)/shard_map/attend/pallas_call | solution.py:172
  67.4 0.0 collective-permute-done.10.refs_7_
  67.4 0.9 collective-permute-done.9.refs_6_
  68.3 2.1 %attend.9 = bf16[8,208,128]{2,1,0:T(8,128)(2,1)S(1)} custom-call(s32[2]{0:T(128)S(1)} %pad_add_fusion.refs_0_, bf16[768,128]{1,0:T(8,128)(2,1)S(1)} %pad_maximum_fusion.refs_1_.refs_0_, bf16[768,128]{1,0:T(8,128)(2,1)S(1)} %collective-permute-done.2.refs_2_.refs_1_, f32[1536,128]{1,0:T(8,128)S(1)} %get-tuple-element.28.refs_3_, ...), custom_call_target="tpu_custom_call" | custom-call | flops 301989888 | bytes 2359296 | tf_op jit(solution)/shard_map/attend/pallas_call | solution.py:172
  70.3 14.2 %all_to_all.10.parts_ref = bf16[8,208,128]{2,1,0:T(8,128)(2,1)} all-to-all(bf16[8,208,128]{2,1,0:T(8,128)(2,1)S(1)} %attend.9), channel_id=1, replica_groups={{0,16,256,272,8,24,264,280},{32,48,288,304,40,56,296,312},{64,80,320,33..., dimensions={0} | all-to-all | bytes 851968 | tf_op jit(solution)/shard_map/all_to_all | solution.py:299
  84.5 0.0 copy-start.2
  84.5 0.0 copy-start
  84.6 2.5 %merge.1 = bf16[8,192,256]{2,1,0:T(8,128)(2,1)} custom-call(bf16[8,208,128]{2,1,0:T(8,128)(2,1)} %all_to_all.10.parts_ref), custom_call_target="tpu_custom_call" | custom-call | tf_op jit(solution)/shard_map/merge/pallas_call | solution.py:213
  87.1 6.7 %all-to-all-start.1 = ((bf16[8,192,256]{2,1,0:T(8,128)(2,1)}), bf16[8,192,256]{2,1,0:T(8,128)(2,1)S(1)}, u32[]{:S(2)}, u32[]{:S(2)}) async-start(bf16[8,192,256]{2,1,0:T(8,128)(2,1)} %merge.1), calls=%async_computation.1 | async-start | bytes 1572864 | tf_op jit(solution)/shard_map/all_to_all | solution.py:303
  93.7 0.0 copy-done.2
  93.7 13.5 %all-to-all-done.1.parts_ref = bf16[8,192,256]{2,1,0:T(8,128)(2,1)S(1)} async-done(((bf16[8,192,256]{2,1,0:T(8,128)(2,1)}), bf16[8,192,256]{2,1,0:T(8,128)(2,1)S(1)}, u32[]{:S(2)}, u32[]{:S(2)}) %all-to-all-start.1) | async-done | bytes 786464 | tf_op jit(solution)/shard_map/all_to_all | solution.py:303
  107.2 0.0 copy-done
  107.2 1.2 %project.1 = bf16[192,384]{1,0:T(8,128)(2,1)} custom-call(bf16[8,192,256]{2,1,0:T(8,128)(2,1)S(1)} %all-to-all-done.1.parts_ref, bf16[2048,384]{1,0:T(8,128)(2,1)S(1)} %copy-done, f32[1,384]{1,0:T(1,128)S(1)} %broadcast_in_dim.14.gate_ref), custom_call_target="tpu_custom_call" | custom-call | tf_op jit(solution)/shard_map/project/pallas_call | solution.py:230
  (9 shorter events, 0.1 us)
Async XLA Ops:
  9.5 24.0 %collective-permute-start.3 = (bf16[2,2,192,128]{3,2,1,0:T(8,128)(2,1)S(1)}, bf16[2,2,192,128]{3,2,1,0:T(8,128)(2,1)S(1)}, u32[]{:S(2)}, u32[]{:S(2)}) collective-permute-start(bf16[2,2,192,128]{3,2,1,0:T(8,128)(2,1)S(1)} %copy_bitcast_fusion.refs_5_), channel_id=1, source_target_pairs={{0,32},{8,232},{16,48},{24,248},{32,0},{40,72},{48,16},{56,88},{64... | collective-permute-start | bytes 589832 | tf_op jit(solution)/shard_map/ppermute | solution.py:266
  15.7 14.1 %collective-permute-start.4 = (bf16[2,2,192,128]{3,2,1,0:T(8,128)(2,1)S(1)}, bf16[2,2,192,128]{3,2,1,0:T(8,128)(2,1)S(1)}, u32[]{:S(2)}, u32[]{:S(2)}) collective-permute-start(bf16[2,2,192,128]{3,2,1,0:T(8,128)(2,1)S(1)} %copy_bitcast_fusion.refs_5_), channel_id=1, source_target_pairs={{0,224},{8,40},{16,240},{24,56},{32,64},{40,8},{48,80},{56,24},{64... | collective-permute-start | bytes 589832 | tf_op jit(solution)/shard_map/ppermute | solution.py:265
  21.9 5.2 %collective-permute-start = (bf16[3,192,128]{2,1,0:T(8,128)(2,1)}, bf16[3,192,128]{2,1,0:T(8,128)(2,1)S(1)}, u32[]{:S(2)}, u32[]{:S(2)}) collective-permute-start(bf16[3,192,128]{2,1,0:T(8,128)(2,1)} %get-tuple-element.18), channel_id=1, source_target_pairs={{0,8},{8,0},{16,24},{24,16},{32,40},{40,32},{48,56},{56,48},{64,72... | collective-permute-start | bytes 442376 | tf_op jit(solution)/shard_map/ppermute | solution.py:287
  27.1 9.5 %collective-permute-start.1 = (bf16[384,128]{1,0:T(8,128)(2,1)S(1)}, bf16[384,128]{1,0:T(8,128)(2,1)S(1)}, u32[]{:S(2)}, u32[]{:S(2)}) collective-permute-start(bf16[384,128]{1,0:T(8,128)(2,1)S(1)} %pad_maximum_fusion.3), channel_id=1, source_target_pairs={{0,16},{8,24},{16,0},{24,8},{32,48},{40,56},{48,32},{56,40},{64,80... | collective-permute-start | bytes 294920 | tf_op jit(solution)/shard_map/ppermute | solution.py:289
  29.8 18.0 %collective-permute-start.5 = (bf16[2,2,192,128]{3,2,1,0:T(8,128)(2,1)S(1)}, bf16[2,2,192,128]{3,2,1,0:T(8,128)(2,1)S(1)}, u32[]{:S(2)}, u32[]{:S(2)}) collective-permute-start(bf16[2,2,192,128]{3,2,1,0:T(8,128)(2,1)S(1)} %collective-permute-done.4.refs_6_), channel_id=1, source_target_pairs={{0,32},{8,232},{16,48},{24,248},{32,0},{40,72},{48,16},{56,88},{64... | collective-permute-start | bytes 589832 | tf_op jit(solution)/shard_map/ppermute | solution.py:266
  33.5 11.0 %collective-permute-start.6 = (bf16[2,2,192,128]{3,2,1,0:T(8,128)(2,1)S(1)}, bf16[2,2,192,128]{3,2,1,0:T(8,128)(2,1)S(1)}, u32[]{:S(2)}, u32[]{:S(2)}) collective-permute-start(bf16[2,2,192,128]{3,2,1,0:T(8,128)(2,1)S(1)} %collective-permute-done.3.refs_5_), channel_id=1, source_target_pairs={{0,224},{8,40},{16,240},{24,56},{32,64},{40,8},{48,80},{56,24},{64... | collective-permute-start | bytes 589832 | tf_op jit(solution)/shard_map/ppermute | solution.py:265
  36.6 14.6 %collective-permute-start.2 = (bf16[768,128]{1,0:T(8,128)(2,1)S(1)}, bf16[768,128]{1,0:T(8,128)(2,1)S(1)}, u32[]{:S(2)}, u32[]{:S(2)}) collective-permute-start(bf16[768,128]{1,0:T(8,128)(2,1)S(1)} %pad_maximum_fusion.refs_1_.refs_0_), channel_id=1, source_target_pairs={{0,256},{8,264},{16,272},{24,280},{32,288},{40,296},{48,304},{56,3... | collective-permute-start | bytes 589832 | tf_op jit(solution)/shard_map/ppermute | solution.py:290
  44.5 11.4 %collective-permute-start.7 = (bf16[2,2,192,128]{3,2,1,0:T(8,128)(2,1)S(1)}, bf16[2,2,192,128]{3,2,1,0:T(8,128)(2,1)S(1)}, u32[]{:S(2)}, u32[]{:S(2)}) collective-permute-start(bf16[2,2,192,128]{3,2,1,0:T(8,128)(2,1)S(1)} %collective-permute-done.6.refs_6_), channel_id=1, source_target_pairs={{0,32},{8,232},{16,48},{24,248},{32,0},{40,72},{48,16},{56,88},{64... | collective-permute-start | bytes 589832 | tf_op jit(solution)/shard_map/ppermute | solution.py:266
  47.8 12.0 %collective-permute-start.8 = (bf16[2,2,192,128]{3,2,1,0:T(8,128)(2,1)S(1)}, bf16[2,2,192,128]{3,2,1,0:T(8,128)(2,1)S(1)}, u32[]{:S(2)}, u32[]{:S(2)}) collective-permute-start(bf16[2,2,192,128]{3,2,1,0:T(8,128)(2,1)S(1)} %collective-permute-done.5.refs_5_), channel_id=1, source_target_pairs={{0,224},{8,40},{16,240},{24,56},{32,64},{40,8},{48,80},{56,24},{64... | collective-permute-start | bytes 589832 | tf_op jit(solution)/shard_map/ppermute | solution.py:265
  51.2 0.9 copy-start.1
  56.0 11.4 %collective-permute-start.10 = (bf16[2,192,128]{2,1,0:T(8,128)(2,1)S(1)}, bf16[2,192,128]{2,1,0:T(8,128)(2,1)S(1)}, u32[]{:S(2)}, u32[]{:S(2)}) collective-permute-start(bf16[2,192,128]{2,1,0:T(8,128)(2,1)S(1)} %slice_bitcast_fusion), channel_id=1, source_target_pairs={{0,224},{8,40},{16,240},{24,56},{32,64},{40,8},{48,80},{56,24},{64... | collective-permute-start | bytes 294920 | tf_op jit(solution)/shard_map/ppermute | solution.py:295
  59.8 8.5 %collective-permute-start.9 = (bf16[2,192,128]{2,1,0:T(8,128)(2,1)S(1)}, bf16[2,192,128]{2,1,0:T(8,128)(2,1)S(1)}, u32[]{:S(2)}, u32[]{:S(2)}) collective-permute-start(bf16[2,192,128]{2,1,0:T(8,128)(2,1)S(1)} %slice_bitcast_fusion.1), channel_id=1, source_target_pairs={{0,32},{8,232},{16,48},{24,248},{32,0},{40,72},{48,16},{56,88},{64... | collective-permute-start | bytes 294920 | tf_op jit(solution)/shard_map/ppermute | solution.py:294
  84.5 9.2 %copy-start.2 = (f32[384]{0:T(512)S(1)}, f32[384]{0:T(512)}, u32[]{:S(2)}) copy-start(f32[384]{0:T(512)} %param.16) | copy-start | bytes 4612
  84.5 22.7 %copy-start = (bf16[2048,384]{1,0:T(8,128)(2,1)S(1)}, bf16[2048,384]{1,0:T(8,128)(2,1)}, u32[]{:S(2)}) copy-start(bf16[2048,384]{1,0:T(8,128)(2,1)} %weight_ref.1) | copy-start | bytes 4718596
  87.1 20.2 %all-to-all-start.1 = ((bf16[8,192,256]{2,1,0:T(8,128)(2,1)}), bf16[8,192,256]{2,1,0:T(8,128)(2,1)S(1)}, u32[]{:S(2)}, u32[]{:S(2)}) async-start(bf16[8,192,256]{2,1,0:T(8,128)(2,1)} %merge.1), calls=%async_computation.1 | async-start | bytes 1572864 | tf_op jit(solution)/shard_map/all_to_all | solution.py:303

commit v3 on v2

--- a/solution.py
+++ b/solution.py
@@ -16,7 +16,7 @@
 STAT_ROWS = 16
 ROWS_SENT = TOKENS + STAT_ROWS
 LOG2E = 1.4426950408889634
-VMEM_LIMIT = 48 * 1024 * 1024
+VMEM_LIMIT = 20 * 1024 * 1024
 
 PATCHES = 64
 CORES = [[i, i + 1] for i in range(0, PATCHES, 2)]
@@ -258,16 +258,7 @@
 
     share = own_head(over_cores(stale_pairs))
     one, other = ring_swaps(True), ring_swaps(False)
-    over_one, over_other = [share], [share]
-
-    def step():
-        block = over_other[-1]
-        over_other.append(lax.ppermute(over_one[-1], "patch", other))
-        over_one.append(lax.ppermute(block, "patch", one))
-
-    step()
-    step()
-    step()
+    first = lax.ppermute(share, "patch", other)
     positions = patch_offsets[0] + jnp.arange(TOKENS, dtype=jnp.int32)
     frequency = jnp.exp(
         -(2.0 * jnp.arange(HEAD // 2, dtype=F32) / HEAD) * jnp.log(256.0)
@@ -285,16 +276,24 @@
         jnp.concatenate([-sine, sine], axis=1),
     )
     theirs = lax.ppermute(send, "patch", swapped(1))
+    share_later, theirs = lax.optimization_barrier((share, theirs))
+    second = lax.ppermute(share_later, "patch", one)
     near = jnp.concatenate([mine[0], theirs[0]])
     near = jnp.concatenate([near, lax.ppermute(near, "patch", swapped(2))])
+    third = lax.ppermute(first, "patch", one)
+    fourth = lax.ppermute(second, "patch", other)
     queries = (near, lax.ppermute(near, "patch", swapped(32)))
+    fifth = lax.ppermute(third, "patch", other)
     place = jnp.stack([(me // 32) * 2 + (me // 2) % 2, core])
     state = attend(queries, [share], fresh=(mine, theirs), place=place)
-    state = attend(queries, [over_one[1], over_other[1]], state=state)
-    far_keys = lax.ppermute(over_other[3][0], "patch", one)
-    far_values = lax.ppermute(over_one[3][1], "patch", other)
-    state = attend(queries, [over_one[2], over_other[2]], state=state)
-    state = attend(queries, [over_one[3], over_other[3]], state=state)
+    state = attend(queries, [first, second], state=state)
+    fourth, state = lax.optimization_barrier((fourth, state))
+    sixth = lax.ppermute(fourth, "patch", one)
+    state = attend(queries, [third, fourth], state=state)
+    fifth, state = lax.optimization_barrier((fifth, state))
+    far_keys = lax.ppermute(fifth[0], "patch", one)
+    far_values = lax.ppermute(sixth[1], "patch", other)
+    state = attend(queries, [fifth, sixth], state=state)
     parts = attend(queries, [far_keys, far_values], state=state, place=place, ends=True)
     parts = lax.all_to_all(
         parts, "patch", split_axis=0, concat_axis=0, tiled=True, axis_index_groups=QUERY_GROUPS

time: 109 us -> 108 us (level)
  starting transfers between devices: 43.9 us -> 47.8 us
  blocking collectives: 23 us -> 19.4 us
    all_gather x1, blocking collectives: 8.81 us -> 2.3 us  [over_cores(): return lax.all_gather(x, 'patch', axis=0, axis_index_groups=CORES)]
    ppermute x1, starting transfers between devices: 3.99 us -> 8.91 us  [shards(): theirs = lax.ppermute(send, 'patch', swapped(1))]
    all_to_all x1, blocking collectives: 14.2 us -> 17.1 us  [shards(): lax.all_to_all(parts, 'patch', split_axis=0, concat_axis=0, tiled=True, a...]
  transfers between devices with their start and end apart: 12 -> 12, of which waited for: 5 -> 4; matrix products, arithmetic and copies ran while one was open for 2% -> 1% of each run, Pallas kernels for 10% -> 8%
where the time goes in v3:
time: 108 us; the launch traced here: 107 us
  starting transfers between devices  47.8 us (44%)
  waiting for transfers between devices  20.1 us (19%)
  blocking collectives  19.4 us (18%)
  Pallas kernels  16.3 us (15%)
  between operations  1.58 us (1%)
  other arithmetic  1.34 us (1%)
    all_to_all x1, blocking collectives, shards(): lax.all_to_all(parts, 'patch', split_axis=0, concat_axis=0, tiled=True, a...  17.1 us
    all_to_all x1, waiting for transfers between devices, shards(): lax.all_to_all(copies, 'head', split_axis=0, concat_axis=0, tiled=True)  13.5 us
    pallas_call x5, Pallas kernels, attend(): pl.pallas_call(functools.partial(attend_body, len(shares), begins, ends),...  10.2 us
    ppermute x1, starting transfers between devices, shards(): theirs = lax.ppermute(send, 'patch', swapped(1))  8.91 us
    ppermute x1, starting transfers between devices, shards(): second = lax.ppermute(share_later, 'patch', one)  8.08 us
    all_to_all x1, starting transfers between devices, shards(): lax.all_to_all(copies, 'head', split_axis=0, concat_axis=0, tiled=True)  6.49 us
    ppermute x1, starting transfers between devices, shards(): sixth = lax.ppermute(fourth, 'patch', one)  4.14 us
    ppermute x1, waiting for transfers between devices, shards(): third = lax.ppermute(first, 'patch', one)  3.97 us
  transfers between devices with their start and end apart: 12, of which 4 were waited for; matrix products, arithmetic and copies ran while one was open for 1% of the time, Pallas kernels for 8%

profile of v3, /device:TPU:1, one launch (start us, length us, event | category | flops | bytes accessed | tf_op | source)
XLA Modules:
  0.0 107.5 jit_solution(10106867229734108925)
XLA Ops:
  1.3 0.4 fusion
  1.8 0.8 pad_maximum_fusion.1
  2.6 2.4 %norm_rotate.1 = (bf16[192,256]{1,0:T(8,128)(2,1)}, bf16[3,192,128]{2,1,0:T(8,128)(2,1)}, bf16[3,192,128]{2,1,0:T(8,128)(2,1)}) custom-call(s32[1]{0:T(128)} %bitcast.1.core_ref, bf16[192,256]{1,0:T(8,128)(2,1)} %q_ref.1, bf16[192,256]{1,0:T(8,128)(2,1)} %k_ref.1, bf16[192,256]{1,0:T(8,128)(2,1)} %v_ref.1, f32[1,128]{1,0:T(1,128)} %bitcast.18, ...), custom_call_target="tpu_custom_call" | custom-call | tf_op jit(solution)/shard_map/norm_rotate/pallas_call | solution.py:70
  4.9 0.0 copy-start.1
  4.9 8.9 %collective-permute-start = (bf16[3,192,128]{2,1,0:T(8,128)(2,1)}, bf16[3,192,128]{2,1,0:T(8,128)(2,1)S(1)}, u32[]{:S(2)}, u32[]{:S(2)}) collective-permute-start(bf16[3,192,128]{2,1,0:T(8,128)(2,1)} %get-tuple-element.28), channel_id=1, source_target_pairs={{0,8},{8,0},{16,24},{24,16},{32,40},{40,32},{48,56},{56,48},{64,72... | collective-permute-start | bytes 442376 | tf_op jit(solution)/shard_map/ppermute | solution.py:278
  13.8 2.3 %all-gather = bf16[4,192,256]{2,1,0:T(8,128)(2,1)S(1)} all-gather(bf16[2,192,256]{2,1,0:T(8,128)(2,1)} %param.12), channel_id=2, replica_groups={{0,8},{16,24},{32,40},{48,56},{64,72},{80,88},{96,104},{112,120},{128,1..., dimensions={0}, use_global_device_ids=true | all-gather | bytes 589824 | tf_op jit(solution)/shard_map/all_gather | solution.py:257
  16.2 1.9 %collective-permute-start.3 = (bf16[2,2,192,128]{3,2,1,0:T(8,128)(2,1)S(1)}, bf16[2,2,192,128]{3,2,1,0:T(8,128)(2,1)S(1)}, u32[]{:S(2)}, u32[]{:S(2)}) collective-permute-start(bf16[2,2,192,128]{3,2,1,0:T(8,128)(2,1)S(1)} %copy_bitcast_fusion.refs_5_), channel_id=1, source_target_pairs={{0,224},{8,40},{16,240},{24,56},{32,64},{40,8},{48,80},{56,24},{64... | collective-permute-start | bytes 589832 | tf_op jit(solution)/shard_map/ppermute | solution.py:261
  18.1 0.8 slice_bitcast_fusion.3
  18.9 0.0 collective-permute-done.refs_4_
  18.9 1.9 %collective-permute-start.1 = (bf16[384,128]{1,0:T(8,128)(2,1)S(1)}, bf16[384,128]{1,0:T(8,128)(2,1)S(1)}, u32[]{:S(2)}, u32[]{:S(2)}) collective-permute-start(bf16[384,128]{1,0:T(8,128)(2,1)S(1)} %pad_maximum_fusion.3), channel_id=1, source_target_pairs={{0,16},{8,24},{16,0},{24,8},{32,48},{40,56},{48,32},{56,40},{64,80... | collective-permute-start | bytes 294920 | tf_op jit(solution)/shard_map/ppermute | solution.py:282
  20.9 8.1 %collective-permute-start.6 = (bf16[2,2,192,128]{3,2,1,0:T(8,128)(2,1)S(1)}, bf16[2,2,192,128]{3,2,1,0:T(8,128)(2,1)S(1)}, u32[]{:S(2)}, u32[]{:S(2)}) collective-permute-start(bf16[2,2,192,128]{3,2,1,0:T(8,128)(2,1)S(1)} %copy_bitcast_fusion.refs_5_), channel_id=1, source_target_pairs={{0,32},{8,232},{16,48},{24,248},{32,0},{40,72},{48,16},{56,88},{64... | collective-permute-start | bytes 589832 | tf_op jit(solution)/shard_map/ppermute | solution.py:280
  29.0 0.0 collective-permute-done.3.refs_5_
  29.0 1.9 %collective-permute-start.4 = (bf16[2,2,192,128]{3,2,1,0:T(8,128)(2,1)S(1)}, bf16[2,2,192,128]{3,2,1,0:T(8,128)(2,1)S(1)}, u32[]{:S(2)}, u32[]{:S(2)}) collective-permute-start(bf16[2,2,192,128]{3,2,1,0:T(8,128)(2,1)S(1)} %collective-permute-done.3.refs_5_), channel_id=1, source_target_pairs={{0,32},{8,232},{16,48},{24,248},{32,0},{40,72},{48,16},{56,88},{64... | collective-permute-start | bytes 589832 | tf_op jit(solution)/shard_map/ppermute | solution.py:283
  30.9 0.0 collective-permute-done.1
  30.9 3.1 %collective-permute-start.2 = (bf16[768,128]{1,0:T(8,128)(2,1)S(1)}, bf16[768,128]{1,0:T(8,128)(2,1)S(1)}, u32[]{:S(2)}, u32[]{:S(2)}) collective-permute-start(bf16[768,128]{1,0:T(8,128)(2,1)S(1)} %pad_maximum_fusion.refs_1_.refs_0_), channel_id=1, source_target_pairs={{0,256},{8,264},{16,272},{24,280},{32,288},{40,296},{48,304},{56,3... | collective-permute-start | bytes 589832 | tf_op jit(solution)/shard_map/ppermute | solution.py:285
  34.1 0.0 collective-permute-done.6.refs_6_
  34.1 2.3 %collective-permute-start.7 = (bf16[2,2,192,128]{3,2,1,0:T(8,128)(2,1)S(1)}, bf16[2,2,192,128]{3,2,1,0:T(8,128)(2,1)S(1)}, u32[]{:S(2)}, u32[]{:S(2)}) collective-permute-start(bf16[2,2,192,128]{3,2,1,0:T(8,128)(2,1)S(1)} %collective-permute-done.6.refs_6_), channel_id=1, source_target_pairs={{0,224},{8,40},{16,240},{24,56},{32,64},{40,8},{48,80},{56,24},{64... | collective-permute-start | bytes 589832 | tf_op jit(solution)/shard_map/ppermute | solution.py:284
  36.4 4.0 %collective-permute-done.4.refs_5_ = bf16[2,2,192,128]{3,2,1,0:T(8,128)(2,1)S(1)} collective-permute-done((bf16[2,2,192,128]{3,2,1,0:T(8,128)(2,1)S(1)}, bf16[2,2,192,128]{3,2,1,0:T(8,128)(2,1)S(1)}, u32[]{:S(2)}, u32[]{:S(2)}) %collective-permute-start.4) | collective-permute-done | bytes 196640 | tf_op jit(solution)/shard_map/ppermute | solution.py:283
  40.3 1.9 %collective-permute-start.5 = (bf16[2,2,192,128]{3,2,1,0:T(8,128)(2,1)S(1)}, bf16[2,2,192,128]{3,2,1,0:T(8,128)(2,1)S(1)}, u32[]{:S(2)}, u32[]{:S(2)}) collective-permute-start(bf16[2,2,192,128]{3,2,1,0:T(8,128)(2,1)S(1)} %collective-permute-done.4.refs_5_), channel_id=1, source_target_pairs={{0,224},{8,40},{16,240},{24,56},{32,64},{40,8},{48,80},{56,24},{64... | collective-permute-start | bytes 589832 | tf_op jit(solution)/shard_map/ppermute | solution.py:286
  42.3 0.1 pad_add_fusion.refs_0_
  42.3 0.0 collective-permute-done.2.refs_2_.refs_1_
  42.3 0.0 copy-done.1
  42.3 1.6 %attend.5 = (f32[1536,128]{1,0:T(8,128)S(1)}, f32[1536,128]{1,0:T(8,128)S(1)}, f32[1536,128]{1,0:T(8,128)S(1)}) custom-call(s32[2]{0:T(128)S(1)} %pad_add_fusion.refs_0_, bf16[768,128]{1,0:T(8,128)(2,1)S(1)} %pad_maximum_fusion.refs_1_.refs_0_, bf16[768,128]{1,0:T(8,128)(2,1)S(1)} %collective-permute-done.2.refs_2_.refs_1_, ...), custom_call_target="tpu_custom_call" | custom-call | flops 301989888 | bytes 2359296 | tf_op jit(solution)/shard_map/attend/pallas_call | solution.py:172
  44.0 2.2 %attend.6 = (f32[1536,128]{1,0:T(8,128)S(1)}, f32[1536,128]{1,0:T(8,128)S(1)}, f32[1536,128]{1,0:T(8,128)S(1)}) custom-call(bf16[768,128]{1,0:T(8,128)(2,1)S(1)} %pad_maximum_fusion.refs_1_.refs_0_, bf16[768,128]{1,0:T(8,128)(2,1)S(1)} %collective-permute-done.2.refs_2_.refs_1_, f32[1536,128]{1,0:T(8,128)S(1)} %get-tuple-element.31.refs_2_, ...), custom_call_target="tpu_custom_call" | custom-call | flops 603979776 | bytes 2359296 | tf_op jit(solution)/shard_map/attend/pallas_call | solution.py:172
  46.2 0.3 collective-permute-done.7.refs_6_
  46.5 4.1 %collective-permute-start.8 = (bf16[2,2,192,128]{3,2,1,0:T(8,128)(2,1)S(1)}, bf16[2,2,192,128]{3,2,1,0:T(8,128)(2,1)S(1)}, u32[]{:S(2)}, u32[]{:S(2)}) collective-permute-start(bf16[2,2,192,128]{3,2,1,0:T(8,128)(2,1)S(1)} %collective-permute-done.7.refs_6_), channel_id=1, source_target_pairs={{0,32},{8,232},{16,48},{24,248},{32,0},{40,72},{48,16},{56,88},{64... | collective-permute-start | bytes 589832 | tf_op jit(solution)/shard_map/ppermute | solution.py:291
  50.7 2.2 %attend.7 = (f32[1536,128]{1,0:T(8,128)S(1)}, f32[1536,128]{1,0:T(8,128)S(1)}, f32[1536,128]{1,0:T(8,128)S(1)}) custom-call(bf16[768,128]{1,0:T(8,128)(2,1)S(1)} %pad_maximum_fusion.refs_1_.refs_0_, bf16[768,128]{1,0:T(8,128)(2,1)S(1)} %collective-permute-done.2.refs_2_.refs_1_, f32[1536,128]{1,0:T(8,128)S(1)} %get-tuple-element.37.refs_2_, ...), custom_call_target="tpu_custom_call" | custom-call | flops 603979776 | bytes 2359296 | tf_op jit(solution)/shard_map/attend/pallas_call | solution.py:172
  52.8 0.0 collective-permute-done.5.refs_5_
  52.9 3.2 %collective-permute-start.9 = (bf16[2,192,128]{2,1,0:T(8,128)(2,1)S(1)}, bf16[2,192,128]{2,1,0:T(8,128)(2,1)S(1)}, u32[]{:S(2)}, u32[]{:S(2)}) collective-permute-start(bf16[2,192,128]{2,1,0:T(8,128)(2,1)S(1)} %slice_bitcast_fusion.1), channel_id=1, source_target_pairs={{0,32},{8,232},{16,48},{24,248},{32,0},{40,72},{48,16},{56,88},{64... | collective-permute-start | bytes 294920 | tf_op jit(solution)/shard_map/ppermute | solution.py:294
  56.1 0.0 collective-permute-done.8.refs_6_
  56.1 3.9 %collective-permute-start.10 = (bf16[2,192,128]{2,1,0:T(8,128)(2,1)S(1)}, bf16[2,192,128]{2,1,0:T(8,128)(2,1)S(1)}, u32[]{:S(2)}, u32[]{:S(2)}) collective-permute-start(bf16[2,192,128]{2,1,0:T(8,128)(2,1)S(1)} %slice_bitcast_fusion), channel_id=1, source_target_pairs={{0,224},{8,40},{16,240},{24,56},{32,64},{40,8},{48,80},{56,24},{64... | collective-permute-start | bytes 294920 | tf_op jit(solution)/shard_map/ppermute | solution.py:295
  60.1 2.2 %attend.8 = (f32[1536,128]{1,0:T(8,128)S(1)}, f32[1536,128]{1,0:T(8,128)S(1)}, f32[1536,128]{1,0:T(8,128)S(1)}) custom-call(bf16[768,128]{1,0:T(8,128)(2,1)S(1)} %pad_maximum_fusion.refs_1_.refs_0_, bf16[768,128]{1,0:T(8,128)(2,1)S(1)} %collective-permute-done.2.refs_2_.refs_1_, f32[1536,128]{1,0:T(8,128)S(1)} %get-tuple-element.44.refs_2_, ...), custom_call_target="tpu_custom_call" | custom-call | flops 603979776 | bytes 2359296 | tf_op jit(solution)/shard_map/attend/pallas_call | solution.py:172
  62.3 0.0 collective-permute-done.9.refs_6_
  62.3 2.3 %collective-permute-done.10.refs_7_ = bf16[2,192,128]{2,1,0:T(8,128)(2,1)S(1)} collective-permute-done((bf16[2,192,128]{2,1,0:T(8,128)(2,1)S(1)}, bf16[2,192,128]{2,1,0:T(8,128)(2,1)S(1)}, u32[]{:S(2)}, u32[]{:S(2)}) %collective-permute-start.10) | collective-permute-done | bytes 98336 | tf_op jit(solution)/shard_map/ppermute | solution.py:295
  64.6 2.1 %attend.9 = bf16[8,208,128]{2,1,0:T(8,128)(2,1)S(1)} custom-call(s32[2]{0:T(128)S(1)} %pad_add_fusion.refs_0_, bf16[768,128]{1,0:T(8,128)(2,1)S(1)} %pad_maximum_fusion.refs_1_.refs_0_, bf16[768,128]{1,0:T(8,128)(2,1)S(1)} %collective-permute-done.2.refs_2_.refs_1_, f32[1536,128]{1,0:T(8,128)S(1)} %get-tuple-element.48.refs_3_, ...), custom_call_target="tpu_custom_call" | custom-call | flops 301989888 | bytes 2359296 | tf_op jit(solution)/shard_map/attend/pallas_call | solution.py:172
  66.6 17.1 %all_to_all.10.parts_ref = bf16[8,208,128]{2,1,0:T(8,128)(2,1)} all-to-all(bf16[8,208,128]{2,1,0:T(8,128)(2,1)S(1)} %attend.9), channel_id=1, replica_groups={{0,16,256,272,8,24,264,280},{32,48,288,304,40,56,296,312},{64,80,320,33..., dimensions={0} | all-to-all | bytes 851968 | tf_op jit(solution)/shard_map/all_to_all | solution.py:298
  83.7 0.0 copy-start.2
  83.7 0.0 copy-start
  83.7 2.5 %merge.1 = bf16[8,192,256]{2,1,0:T(8,128)(2,1)} custom-call(bf16[8,208,128]{2,1,0:T(8,128)(2,1)} %all_to_all.10.parts_ref), custom_call_target="tpu_custom_call" | custom-call | tf_op jit(solution)/shard_map/merge/pallas_call | solution.py:213
  86.2 6.5 %all-to-all-start.1 = ((bf16[8,192,256]{2,1,0:T(8,128)(2,1)}), bf16[8,192,256]{2,1,0:T(8,128)(2,1)S(1)}, u32[]{:S(2)}, u32[]{:S(2)}) async-start(bf16[8,192,256]{2,1,0:T(8,128)(2,1)} %merge.1), calls=%async_computation.1 | async-start | bytes 1572864 | tf_op jit(solution)/shard_map/all_to_all | solution.py:302
  92.7 0.0 copy-done.2
  92.7 13.5 %all-to-all-done.1.parts_ref = bf16[8,192,256]{2,1,0:T(8,128)(2,1)S(1)} async-done(((bf16[8,192,256]{2,1,0:T(8,128)(2,1)}), bf16[8,192,256]{2,1,0:T(8,128)(2,1)S(1)}, u32[]{:S(2)}, u32[]{:S(2)}) %all-to-all-start.1) | async-done | bytes 786464 | tf_op jit(solution)/shard_map/all_to_all | solution.py:302
  106.2 0.0 copy-done
  106.2 1.2 %project.1 = bf16[192,384]{1,0:T(8,128)(2,1)} custom-call(bf16[8,192,256]{2,1,0:T(8,128)(2,1)S(1)} %all-to-all-done.1.parts_ref, bf16[2048,384]{1,0:T(8,128)(2,1)S(1)} %copy-done, f32[1,384]{1,0:T(1,128)S(1)} %broadcast_in_dim.14.gate_ref), custom_call_target="tpu_custom_call" | custom-call | tf_op jit(solution)/shard_map/project/pallas_call | solution.py:230
  (9 shorter events, 0.1 us)
Async XLA Ops:
  4.9 37.4 %copy-start.1 = (bf16[3,192,128]{2,1,0:T(8,128)(2,1)S(1)}, bf16[3,192,128]{2,1,0:T(8,128)(2,1)}, u32[]{:S(2)}) copy-start(bf16[3,192,128]{2,1,0:T(8,128)(2,1)} %get-tuple-element.27.refs_3_) | copy-start | bytes 442372
  4.9 14.0 %collective-permute-start = (bf16[3,192,128]{2,1,0:T(8,128)(2,1)}, bf16[3,192,128]{2,1,0:T(8,128)(2,1)S(1)}, u32[]{:S(2)}, u32[]{:S(2)}) collective-permute-start(bf16[3,192,128]{2,1,0:T(8,128)(2,1)} %get-tuple-element.28), channel_id=1, source_target_pairs={{0,8},{8,0},{16,24},{24,16},{32,40},{40,32},{48,56},{56,48},{64,72... | collective-permute-start | bytes 442376 | tf_op jit(solution)/shard_map/ppermute | solution.py:278
  16.2 12.8 %collective-permute-start.3 = (bf16[2,2,192,128]{3,2,1,0:T(8,128)(2,1)S(1)}, bf16[2,2,192,128]{3,2,1,0:T(8,128)(2,1)S(1)}, u32[]{:S(2)}, u32[]{:S(2)}) collective-permute-start(bf16[2,2,192,128]{3,2,1,0:T(8,128)(2,1)S(1)} %copy_bitcast_fusion.refs_5_), channel_id=1, source_target_pairs={{0,224},{8,40},{16,240},{24,56},{32,64},{40,8},{48,80},{56,24},{64... | collective-permute-start | bytes 589832 | tf_op jit(solution)/shard_map/ppermute | solution.py:261
  18.9 12.0 %collective-permute-start.1 = (bf16[384,128]{1,0:T(8,128)(2,1)S(1)}, bf16[384,128]{1,0:T(8,128)(2,1)S(1)}, u32[]{:S(2)}, u32[]{:S(2)}) collective-permute-start(bf16[384,128]{1,0:T(8,128)(2,1)S(1)} %pad_maximum_fusion.3), channel_id=1, source_target_pairs={{0,16},{8,24},{16,0},{24,8},{32,48},{40,56},{48,32},{56,40},{64,80... | collective-permute-start | bytes 294920 | tf_op jit(solution)/shard_map/ppermute | solution.py:282
  20.9 13.2 %collective-permute-start.6 = (bf16[2,2,192,128]{3,2,1,0:T(8,128)(2,1)S(1)}, bf16[2,2,192,128]{3,2,1,0:T(8,128)(2,1)S(1)}, u32[]{:S(2)}, u32[]{:S(2)}) collective-permute-start(bf16[2,2,192,128]{3,2,1,0:T(8,128)(2,1)S(1)} %copy_bitcast_fusion.refs_5_), channel_id=1, source_target_pairs={{0,32},{8,232},{16,48},{24,248},{32,0},{40,72},{48,16},{56,88},{64... | collective-permute-start | bytes 589832 | tf_op jit(solution)/shard_map/ppermute | solution.py:280
  29.0 11.4 %collective-permute-start.4 = (bf16[2,2,192,128]{3,2,1,0:T(8,128)(2,1)S(1)}, bf16[2,2,192,128]{3,2,1,0:T(8,128)(2,1)S(1)}, u32[]{:S(2)}, u32[]{:S(2)}) collective-permute-start(bf16[2,2,192,128]{3,2,1,0:T(8,128)(2,1)S(1)} %collective-permute-done.3.refs_5_), channel_id=1, source_target_pairs={{0,32},{8,232},{16,48},{24,248},{32,0},{40,72},{48,16},{56,88},{64... | collective-permute-start | bytes 589832 | tf_op jit(solution)/shard_map/ppermute | solution.py:283
  30.9 11.4 %collective-permute-start.2 = (bf16[768,128]{1,0:T(8,128)(2,1)S(1)}, bf16[768,128]{1,0:T(8,128)(2,1)S(1)}, u32[]{:S(2)}, u32[]{:S(2)}) collective-permute-start(bf16[768,128]{1,0:T(8,128)(2,1)S(1)} %pad_maximum_fusion.refs_1_.refs_0_), channel_id=1, source_target_pairs={{0,256},{8,264},{16,272},{24,280},{32,288},{40,296},{48,304},{56,3... | collective-permute-start | bytes 589832 | tf_op jit(solution)/shard_map/ppermute | solution.py:285
  34.1 12.4 %collective-permute-start.7 = (bf16[2,2,192,128]{3,2,1,0:T(8,128)(2,1)S(1)}, bf16[2,2,192,128]{3,2,1,0:T(8,128)(2,1)S(1)}, u32[]{:S(2)}, u32[]{:S(2)}) collective-permute-start(bf16[2,2,192,128]{3,2,1,0:T(8,128)(2,1)S(1)} %collective-permute-done.6.refs_6_), channel_id=1, source_target_pairs={{0,224},{8,40},{16,240},{24,56},{32,64},{40,8},{48,80},{56,24},{64... | collective-permute-start | bytes 589832 | tf_op jit(solution)/shard_map/ppermute | solution.py:284
  40.3 12.5 %collective-permute-start.5 = (bf16[2,2,192,128]{3,2,1,0:T(8,128)(2,1)S(1)}, bf16[2,2,192,128]{3,2,1,0:T(8,128)(2,1)S(1)}, u32[]{:S(2)}, u32[]{:S(2)}) collective-permute-start(bf16[2,2,192,128]{3,2,1,0:T(8,128)(2,1)S(1)} %collective-permute-done.4.refs_5_), channel_id=1, source_target_pairs={{0,224},{8,40},{16,240},{24,56},{32,64},{40,8},{48,80},{56,24},{64... | collective-permute-start | bytes 589832 | tf_op jit(solution)/shard_map/ppermute | solution.py:286
  46.5 9.6 %collective-permute-start.8 = (bf16[2,2,192,128]{3,2,1,0:T(8,128)(2,1)S(1)}, bf16[2,2,192,128]{3,2,1,0:T(8,128)(2,1)S(1)}, u32[]{:S(2)}, u32[]{:S(2)}) collective-permute-start(bf16[2,2,192,128]{3,2,1,0:T(8,128)(2,1)S(1)} %collective-permute-done.7.refs_6_), channel_id=1, source_target_pairs={{0,32},{8,232},{16,48},{24,248},{32,0},{40,72},{48,16},{56,88},{64... | collective-permute-start | bytes 589832 | tf_op jit(solution)/shard_map/ppermute | solution.py:291
  52.9 9.4 %collective-permute-start.9 = (bf16[2,192,128]{2,1,0:T(8,128)(2,1)S(1)}, bf16[2,192,128]{2,1,0:T(8,128)(2,1)S(1)}, u32[]{:S(2)}, u32[]{:S(2)}) collective-permute-start(bf16[2,192,128]{2,1,0:T(8,128)(2,1)S(1)} %slice_bitcast_fusion.1), channel_id=1, source_target_pairs={{0,32},{8,232},{16,48},{24,248},{32,0},{40,72},{48,16},{56,88},{64... | collective-permute-start | bytes 294920 | tf_op jit(solution)/shard_map/ppermute | solution.py:294
  56.1 8.4 %collective-permute-start.10 = (bf16[2,192,128]{2,1,0:T(8,128)(2,1)S(1)}, bf16[2,192,128]{2,1,0:T(8,128)(2,1)S(1)}, u32[]{:S(2)}, u32[]{:S(2)}) collective-permute-start(bf16[2,192,128]{2,1,0:T(8,128)(2,1)S(1)} %slice_bitcast_fusion), channel_id=1, source_target_pairs={{0,224},{8,40},{16,240},{24,56},{32,64},{40,8},{48,80},{56,24},{64... | collective-permute-start | bytes 294920 | tf_op jit(solution)/shard_map/ppermute | solution.py:295
  83.7 9.0 %copy-start.2 = (f32[384]{0:T(512)S(1)}, f32[384]{0:T(512)}, u32[]{:S(2)}) copy-start(f32[384]{0:T(512)} %param.16) | copy-start | bytes 4612
  83.7 22.5 %copy-start = (bf16[2048,384]{1,0:T(8,128)(2,1)S(1)}, bf16[2048,384]{1,0:T(8,128)(2,1)}, u32[]{:S(2)}) copy-start(bf16[2048,384]{1,0:T(8,128)(2,1)} %weight_ref.1) | copy-start | bytes 4718596
  86.2 20.0 %all-to-all-start.1 = ((bf16[8,192,256]{2,1,0:T(8,128)(2,1)}), bf16[8,192,256]{2,1,0:T(8,128)(2,1)S(1)}, u32[]{:S(2)}, u32[]{:S(2)}) async-start(bf16[8,192,256]{2,1,0:T(8,128)(2,1)} %merge.1), calls=%async_computation.1 | async-start | bytes 1572864 | tf_op jit(solution)/shard_map/all_to_all | solution.py:302

commit v4 on v3

--- a/solution.py
+++ b/solution.py
@@ -19,7 +19,6 @@
 VMEM_LIMIT = 20 * 1024 * 1024
 
 PATCHES = 64
-CORES = [[i, i + 1] for i in range(0, PATCHES, 2)]
 QUERY_GROUPS = [
     [x * 32 + (2 * pair + z) * 2 + core for core in range(2) for x in range(2) for z in range(2)]
     for pair in range(8)
@@ -41,9 +40,10 @@
 
 
 def prepare_body(
-    core_ref, q_ref, k_ref, v_ref, q_gain_ref, k_gain_ref, cos_ref, sin_ref, k_out, mine_out, send_out
+    core_ref, q_ref, k_ref, v_ref, stale_ref, q_gain_ref, k_gain_ref, cos_ref, sin_ref, k_out, mine_out, send_out
 ):
-    cosine, signed_sine = cos_ref[...], sin_ref[...]
+    cosine = jnp.concatenate([cos_ref[...], cos_ref[...]], axis=1)
+    signed_sine = jnp.concatenate([-sin_ref[...], sin_ref[...]], axis=1)
     first = core_ref[0] == 0
 
     def put(part, heads):
@@ -63,17 +63,29 @@
                 k_out[:, cols] = turned
         put(part, heads)
     put(2, [v_ref[:, :HEAD], v_ref[:, HEAD:]])
-
-
-def prepare(core, query_raw, key_raw, value_raw, query_gain, key_gain, cosine, signed_sine):
-    halves = jax.ShapeDtypeStruct((3, TOKENS, HEAD), BF16)
+    for part in range(2):
+        put(3 + part, [stale_ref[part, :, :HEAD], stale_ref[part, :, HEAD:]])
+
+
+def prepare(core, query_raw, key_raw, value_raw, stale_pairs, query_gain, key_gain, cosine, sine):
+    halves = jax.ShapeDtypeStruct((5, TOKENS, HEAD), BF16)
     return pl.pallas_call(
         prepare_body,
         in_specs=[pl.BlockSpec(memory_space=pltpu.SMEM)]
-        + [pl.BlockSpec(memory_space=pltpu.VMEM)] * 7,
+        + [pl.BlockSpec(memory_space=pltpu.VMEM)] * 8,
         out_shape=(jax.ShapeDtypeStruct((TOKENS, WIDTH), BF16), halves, halves),
         name="norm_rotate",
-    )(core, query_raw, key_raw, value_raw, query_gain[None], key_gain[None], cosine, signed_sine)
+    )(
+        core,
+        query_raw,
+        key_raw,
+        value_raw,
+        stale_pairs,
+        query_gain[None],
+        key_gain[None],
+        cosine,
+        sine,
+    )
 
 
 def attend_body(share_count, begins, ends, *refs):
@@ -88,14 +100,9 @@
     half = q_refs[0].shape[0]
 
     def rows_of(part, patch=None):
-        if ends:
-            picked = [shares[part][core] for core in range(2)]
-        else:
-            picked = [share[part, core] for share in shares for core in range(2)]
+        picked = [share[part, core] for share in shares for core in range(2)]
         if patch is not None:
-            at = jnp.bitwise_xor(place_ref[1], patch)
-            new = fresh_refs[patch][1 + part]
-            picked = [jnp.where(at == core, new, old) for core, old in enumerate(picked)]
+            picked[patch] = fresh_refs[patch][1 + part]
         return jnp.concatenate(picked)
 
     size = 2 * TOKENS
@@ -168,7 +175,7 @@
         out_shape = jax.ShapeDtypeStruct((rows // TOKENS, ROWS_SENT, HEAD), BF16)
     else:
         out_shape = (jax.ShapeDtypeStruct((rows, HEAD), F32),) * 3
-    key_count = 2 * TOKENS * (1 if ends else len(shares))
+    key_count = 2 * TOKENS * len(shares)
     return pl.pallas_call(
         functools.partial(attend_body, len(shares), begins, ends),
         in_specs=specs,
@@ -249,16 +256,6 @@
     me = lax.axis_index("patch").astype(jnp.int32)
     core = me % 2
 
-    def own_head(both):
-        both = jnp.swapaxes(both, 0, 1)
-        return lax.dynamic_slice_in_dim(both, core * HEAD, HEAD, axis=3)
-
-    def over_cores(x):
-        return lax.all_gather(x, "patch", axis=0, axis_index_groups=CORES)
-
-    share = own_head(over_cores(stale_pairs))
-    one, other = ring_swaps(True), ring_swaps(False)
-    first = lax.ppermute(share, "patch", other)
     positions = patch_offsets[0] + jnp.arange(TOKENS, dtype=jnp.int32)
     frequency = jnp.exp(
         -(2.0 * jnp.arange(HEAD // 2, dtype=F32) / HEAD) * jnp.log(256.0)
@@ -270,14 +267,17 @@
         query_raw,
         key_raw,
         value_raw,
+        stale_pairs,
         query_gain,
         key_gain,
-        jnp.concatenate([cosine, cosine], axis=1),
-        jnp.concatenate([-sine, sine], axis=1),
+        cosine,
+        sine,
     )
     theirs = lax.ppermute(send, "patch", swapped(1))
-    share_later, theirs = lax.optimization_barrier((share, theirs))
-    second = lax.ppermute(share_later, "patch", one)
+    share = jnp.stack([mine[3:], theirs[3:]], axis=1)
+    one, other = ring_swaps(True), ring_swaps(False)
+    first = lax.ppermute(share, "patch", other)
+    second = lax.ppermute(share, "patch", one)
     near = jnp.concatenate([mine[0], theirs[0]])
     near = jnp.concatenate([near, lax.ppermute(near, "patch", swapped(2))])
     third = lax.ppermute(first, "patch", one)
@@ -291,10 +291,9 @@
     sixth = lax.ppermute(fourth, "patch", one)
     state = attend(queries, [third, fourth], state=state)
     fifth, state = lax.optimization_barrier((fifth, state))
-    far_keys = lax.ppermute(fifth[0], "patch", one)
-    far_values = lax.ppermute(sixth[1], "patch", other)
+    far = lax.ppermute(fifth, "patch", one)
     state = attend(queries, [fifth, sixth], state=state)
-    parts = attend(queries, [far_keys, far_values], state=state, place=place, ends=True)
+    parts = attend(queries, [far], state=state, place=place, ends=True)
     parts = lax.all_to_all(
         parts, "patch", split_axis=0, concat_axis=0, tiled=True, axis_index_groups=QUERY_GROUPS
     )

time: 108 us -> 102 us (0.944)
  blocking collectives: 19.4 us -> 15.7 us
  starting transfers between devices: 47.8 us -> 44.4 us
    ppermute x3 -> x2, starting transfers between devices: 15.3 us -> 11.4 us  [the longest x1 8.08 us: shards(): second = lax.ppermute(share, 'patch', one)]
    all_gather x1 -> x0, blocking collectives: 2.3 us -> none  [over_cores(): return lax.all_gather(x, 'patch', axis=0, axis_index_groups=CORES)]
    all_to_all x1, blocking collectives: 17.1 us -> 15.7 us  [shards(): lax.all_to_all(parts, 'patch', split_axis=0, concat_axis=0, tiled=True, a...]
    ppermute x3 -> x2, waiting for transfers between devices: 2.27 us -> 3.66 us  [the longest x1 3.66 us: shards(): far = lax.ppermute(fifth, 'patch', one)]
    ppermute x1, waiting for transfers between devices: 3.97 us -> 2.7 us  [shards(): third = lax.ppermute(first, 'patch', one)]
    sin x0 -> x1, other arithmetic: none -> 1.1 us  [shards(): cosine, sine = (jnp.cos(angles), jnp.sin(angles))]
  transfers between devices with their start and end apart: 12 -> 11, of which waited for: 4 -> 4; matrix products, arithmetic and copies ran while one was open for 1% -> 2% of each run, Pallas kernels for 8% -> 8%
where the time goes in v4:
time: 102 us
  starting transfers between devices  44.4 us (44%)
  waiting for transfers between devices  20.3 us (20%)
  Pallas kernels  16.6 us (16%)
  blocking collectives  15.7 us (15%)
  local copies, waits for them, and re-layouts  1.73 us (2%)
  between operations  1.56 us (2%)
  other arithmetic  1.24 us (1%)
    all_to_all x1, blocking collectives, shards(): lax.all_to_all(parts, 'patch', split_axis=0, concat_axis=0, tiled=True, a...  15.7 us
    all_to_all x1, waiting for transfers between devices, shards(): lax.all_to_all(copies, 'head', split_axis=0, concat_axis=0, tiled=True)  13.5 us
    pallas_call x5, Pallas kernels, attend(): pl.pallas_call(functools.partial(attend_body, len(shares), begins, ends),...  10.2 us
    ppermute x1, starting transfers between devices, shards(): theirs = lax.ppermute(send, 'patch', swapped(1))  8.91 us
    ppermute x1, starting transfers between devices, shards(): second = lax.ppermute(share, 'patch', one)  8.08 us
    all_to_all x1, starting transfers between devices, shards(): lax.all_to_all(copies, 'head', split_axis=0, concat_axis=0, tiled=True)  6.15 us
    ppermute x1, starting transfers between devices, shards(): sixth = lax.ppermute(fourth, 'patch', one)  4.02 us
    ppermute x1, waiting for transfers between devices, shards(): far = lax.ppermute(fifth, 'patch', one)  3.66 us
  transfers between devices with their start and end apart: 11, of which 4 were waited for; matrix products, arithmetic and copies ran while one was open for 2% of the time, Pallas kernels for 8%

profile of v4, /device:TPU:1, one launch (start us, length us, event | category | flops | bytes accessed | tf_op | source)
XLA Modules:
  0.0 101.5 jit_solution(7579239837409088774)
XLA Ops:
  1.3 1.1 %multiply_sine_fusion = (f32[192,64]{1,0:T(8,128)}, f32[192,64]{1,0:T(8,128)}) fusion(f32[64]{0:T(128)S(1)} %multiply_exponential_fusion, f32[192]{0:T(256)S(1)} %add_convert_fusion), kind=kLoop, calls=%fused_computation.2 | loop fusion | flops 12288 | bytes 99328 | tf_op jit(solution)/shard_map/sin | solution.py:264
  2.4 2.6 %norm_rotate.1 = (bf16[192,256]{1,0:T(8,128)(2,1)}, bf16[5,192,128]{2,1,0:T(8,128)(2,1)}, bf16[5,192,128]{2,1,0:T(8,128)(2,1)}) custom-call(s32[1]{0:T(128)} %bitcast.1.core_ref, bf16[192,256]{1,0:T(8,128)(2,1)} %q_ref.1, bf16[192,256]{1,0:T(8,128)(2,1)} %k_ref.1, bf16[192,256]{1,0:T(8,128)(2,1)} %v_ref.1, bf16[2,192,256]{2,1,0:T(8,128)(2,1)} %stale_ref.1, ...), custom_call_target="tpu_custom_call" | custom-call | tf_op jit(solution)/shard_map/norm_rotate/pallas_call | solution.py:72
  5.0 0.0 copy-start.1
  5.0 8.9 %collective-permute-start = (bf16[5,192,128]{2,1,0:T(8,128)(2,1)}, bf16[5,192,128]{2,1,0:T(8,128)(2,1)S(1)}, u32[]{:S(2)}, u32[]{:S(2)}) collective-permute-start(bf16[5,192,128]{2,1,0:T(8,128)(2,1)} %get-tuple-element.26), channel_id=1, source_target_pairs={{0,8},{8,0},{16,24},{24,16},{32,40},{40,32},{48,56},{56,48},{64,72... | collective-permute-start | bytes 737288 | tf_op jit(solution)/shard_map/ppermute | solution.py:276
  14.0 0.8 slice_bitcast_fusion.3
  14.8 0.9 slice_bitcast_fusion.1
  15.7 0.0 collective-permute-done.refs_4_
  15.7 1.9 %collective-permute-start.3 = (bf16[2,2,192,128]{3,2,1,0:T(8,128)(2,1)S(1)}, bf16[2,2,192,128]{3,2,1,0:T(8,128)(2,1)S(1)}, u32[]{:S(2)}, u32[]{:S(2)}) collective-permute-start(bf16[2,2,192,128]{3,2,1,0:T(8,128)(2,1)S(1)} %pad_maximum_fusion.1.refs_5_), channel_id=1, source_target_pairs={{0,224},{8,40},{16,240},{24,56},{32,64},{40,8},{48,80},{56,24},{64... | collective-permute-start | bytes 589832 | tf_op jit(solution)/shard_map/ppermute | solution.py:279
  17.7 1.9 %collective-permute-start.1 = (bf16[384,128]{1,0:T(8,128)(2,1)S(1)}, bf16[384,128]{1,0:T(8,128)(2,1)S(1)}, u32[]{:S(2)}, u32[]{:S(2)}) collective-permute-start(bf16[384,128]{1,0:T(8,128)(2,1)S(1)} %pad_maximum_fusion.2), channel_id=1, source_target_pairs={{0,16},{8,24},{16,0},{24,8},{32,48},{40,56},{48,32},{56,40},{64,80... | collective-permute-start | bytes 294920 | tf_op jit(solution)/shard_map/ppermute | solution.py:282
  19.6 8.1 %collective-permute-start.6 = (bf16[2,2,192,128]{3,2,1,0:T(8,128)(2,1)S(1)}, bf16[2,2,192,128]{3,2,1,0:T(8,128)(2,1)S(1)}, u32[]{:S(2)}, u32[]{:S(2)}) collective-permute-start(bf16[2,2,192,128]{3,2,1,0:T(8,128)(2,1)S(1)} %pad_maximum_fusion.1.refs_5_), channel_id=1, source_target_pairs={{0,32},{8,232},{16,48},{24,248},{32,0},{40,72},{48,16},{56,88},{64... | collective-permute-start | bytes 589832 | tf_op jit(solution)/shard_map/ppermute | solution.py:280
  27.7 0.0 collective-permute-done.3.refs_5_
  27.7 2.0 %collective-permute-start.4 = (bf16[2,2,192,128]{3,2,1,0:T(8,128)(2,1)S(1)}, bf16[2,2,192,128]{3,2,1,0:T(8,128)(2,1)S(1)}, u32[]{:S(2)}, u32[]{:S(2)}) collective-permute-start(bf16[2,2,192,128]{3,2,1,0:T(8,128)(2,1)S(1)} %collective-permute-done.3.refs_5_), channel_id=1, source_target_pairs={{0,32},{8,232},{16,48},{24,248},{32,0},{40,72},{48,16},{56,88},{64... | collective-permute-start | bytes 589832 | tf_op jit(solution)/shard_map/ppermute | solution.py:283
  29.7 0.0 collective-permute-done.1
  29.8 3.1 %collective-permute-start.2 = (bf16[768,128]{1,0:T(8,128)(2,1)S(1)}, bf16[768,128]{1,0:T(8,128)(2,1)S(1)}, u32[]{:S(2)}, u32[]{:S(2)}) collective-permute-start(bf16[768,128]{1,0:T(8,128)(2,1)S(1)} %pad_maximum_fusion.refs_1_.refs_0_), channel_id=1, source_target_pairs={{0,256},{8,264},{16,272},{24,280},{32,288},{40,296},{48,304},{56,3... | collective-permute-start | bytes 589832 | tf_op jit(solution)/shard_map/ppermute | solution.py:285
  32.9 0.0 collective-permute-done.6.refs_6_
  32.9 2.2 %collective-permute-start.7 = (bf16[2,2,192,128]{3,2,1,0:T(8,128)(2,1)S(1)}, bf16[2,2,192,128]{3,2,1,0:T(8,128)(2,1)S(1)}, u32[]{:S(2)}, u32[]{:S(2)}) collective-permute-start(bf16[2,2,192,128]{3,2,1,0:T(8,128)(2,1)S(1)} %collective-permute-done.6.refs_6_), channel_id=1, source_target_pairs={{0,224},{8,40},{16,240},{24,56},{32,64},{40,8},{48,80},{56,24},{64... | collective-permute-start | bytes 589832 | tf_op jit(solution)/shard_map/ppermute | solution.py:284
  35.1 2.7 %collective-permute-done.4.refs_5_ = bf16[2,2,192,128]{3,2,1,0:T(8,128)(2,1)S(1)} collective-permute-done((bf16[2,2,192,128]{3,2,1,0:T(8,128)(2,1)S(1)}, bf16[2,2,192,128]{3,2,1,0:T(8,128)(2,1)S(1)}, u32[]{:S(2)}, u32[]{:S(2)}) %collective-permute-start.4) | collective-permute-done | bytes 196640 | tf_op jit(solution)/shard_map/ppermute | solution.py:283
  37.8 2.8 %collective-permute-start.5 = (bf16[2,2,192,128]{3,2,1,0:T(8,128)(2,1)S(1)}, bf16[2,2,192,128]{3,2,1,0:T(8,128)(2,1)S(1)}, u32[]{:S(2)}, u32[]{:S(2)}) collective-permute-start(bf16[2,2,192,128]{3,2,1,0:T(8,128)(2,1)S(1)} %collective-permute-done.4.refs_5_), channel_id=1, source_target_pairs={{0,224},{8,40},{16,240},{24,56},{32,64},{40,8},{48,80},{56,24},{64... | collective-permute-start | bytes 589832 | tf_op jit(solution)/shard_map/ppermute | solution.py:286
  40.6 0.1 pad_add_fusion.refs_0_
  40.6 0.0 collective-permute-done.2.refs_2_.refs_1_
  40.6 0.0 copy-done.1
  40.6 1.6 %attend.5 = (f32[1536,128]{1,0:T(8,128)S(1)}, f32[1536,128]{1,0:T(8,128)S(1)}, f32[1536,128]{1,0:T(8,128)S(1)}) custom-call(s32[2]{0:T(128)S(1)} %pad_add_fusion.refs_0_, bf16[768,128]{1,0:T(8,128)(2,1)S(1)} %pad_maximum_fusion.refs_1_.refs_0_, bf16[768,128]{1,0:T(8,128)(2,1)S(1)} %collective-permute-done.2.refs_2_.refs_1_, ...), custom_call_target="tpu_custom_call" | custom-call | flops 301989888 | bytes 2359296 | tf_op jit(solution)/shard_map/attend/pallas_call | solution.py:179
  42.3 2.2 %attend.6 = (f32[1536,128]{1,0:T(8,128)S(1)}, f32[1536,128]{1,0:T(8,128)S(1)}, f32[1536,128]{1,0:T(8,128)S(1)}) custom-call(bf16[768,128]{1,0:T(8,128)(2,1)S(1)} %pad_maximum_fusion.refs_1_.refs_0_, bf16[768,128]{1,0:T(8,128)(2,1)S(1)} %collective-permute-done.2.refs_2_.refs_1_, f32[1536,128]{1,0:T(8,128)S(1)} %get-tuple-element.27.refs_2_, ...), custom_call_target="tpu_custom_call" | custom-call | flops 603979776 | bytes 2359296 | tf_op jit(solution)/shard_map/attend/pallas_call | solution.py:179
  44.5 0.0 collective-permute-done.7.refs_6_
  44.5 4.0 %collective-permute-start.8 = (bf16[2,2,192,128]{3,2,1,0:T(8,128)(2,1)S(1)}, bf16[2,2,192,128]{3,2,1,0:T(8,128)(2,1)S(1)}, u32[]{:S(2)}, u32[]{:S(2)}) collective-permute-start(bf16[2,2,192,128]{3,2,1,0:T(8,128)(2,1)S(1)} %collective-permute-done.7.refs_6_), channel_id=1, source_target_pairs={{0,32},{8,232},{16,48},{24,248},{32,0},{40,72},{48,16},{56,88},{64... | collective-permute-start | bytes 589832 | tf_op jit(solution)/shard_map/ppermute | solution.py:291
  48.5 2.2 %attend.7 = (f32[1536,128]{1,0:T(8,128)S(1)}, f32[1536,128]{1,0:T(8,128)S(1)}, f32[1536,128]{1,0:T(8,128)S(1)}) custom-call(bf16[768,128]{1,0:T(8,128)(2,1)S(1)} %pad_maximum_fusion.refs_1_.refs_0_, bf16[768,128]{1,0:T(8,128)(2,1)S(1)} %collective-permute-done.2.refs_2_.refs_1_, f32[1536,128]{1,0:T(8,128)S(1)} %get-tuple-element.33.refs_2_, ...), custom_call_target="tpu_custom_call" | custom-call | flops 603979776 | bytes 2359296 | tf_op jit(solution)/shard_map/attend/pallas_call | solution.py:179
  50.7 0.0 collective-permute-done.5.refs_5_
  50.7 3.4 %collective-permute-start.9 = (bf16[2,2,192,128]{3,2,1,0:T(8,128)(2,1)S(1)}, bf16[2,2,192,128]{3,2,1,0:T(8,128)(2,1)S(1)}, u32[]{:S(2)}, u32[]{:S(2)}) collective-permute-start(bf16[2,2,192,128]{3,2,1,0:T(8,128)(2,1)S(1)} %collective-permute-done.5.refs_5_), channel_id=1, source_target_pairs={{0,32},{8,232},{16,48},{24,248},{32,0},{40,72},{48,16},{56,88},{64... | collective-permute-start | bytes 589832 | tf_op jit(solution)/shard_map/ppermute | solution.py:294
  54.1 0.5 collective-permute-done.8.refs_6_
  54.6 2.2 %attend.8 = (f32[1536,128]{1,0:T(8,128)S(1)}, f32[1536,128]{1,0:T(8,128)S(1)}, f32[1536,128]{1,0:T(8,128)S(1)}) custom-call(bf16[768,128]{1,0:T(8,128)(2,1)S(1)} %pad_maximum_fusion.refs_1_.refs_0_, bf16[768,128]{1,0:T(8,128)(2,1)S(1)} %collective-permute-done.2.refs_2_.refs_1_, f32[1536,128]{1,0:T(8,128)S(1)} %get-tuple-element.40.refs_2_, ...), custom_call_target="tpu_custom_call" | custom-call | flops 603979776 | bytes 2359296 | tf_op jit(solution)/shard_map/attend/pallas_call | solution.py:179
  56.7 3.7 %collective-permute-done.9.refs_6_ = bf16[2,2,192,128]{3,2,1,0:T(8,128)(2,1)S(1)} collective-permute-done((bf16[2,2,192,128]{3,2,1,0:T(8,128)(2,1)S(1)}, bf16[2,2,192,128]{3,2,1,0:T(8,128)(2,1)S(1)}, u32[]{:S(2)}, u32[]{:S(2)}) %collective-permute-start.9) | collective-permute-done | bytes 196640 | tf_op jit(solution)/shard_map/ppermute | solution.py:294
  60.4 2.1 %attend.9 = bf16[8,208,128]{2,1,0:T(8,128)(2,1)S(1)} custom-call(s32[2]{0:T(128)S(1)} %pad_add_fusion.refs_0_, bf16[768,128]{1,0:T(8,128)(2,1)S(1)} %pad_maximum_fusion.refs_1_.refs_0_, bf16[768,128]{1,0:T(8,128)(2,1)S(1)} %collective-permute-done.2.refs_2_.refs_1_, f32[1536,128]{1,0:T(8,128)S(1)} %get-tuple-element.44.refs_3_, ...), custom_call_target="tpu_custom_call" | custom-call | flops 301989888 | bytes 2359296 | tf_op jit(solution)/shard_map/attend/pallas_call | solution.py:179
  62.5 15.7 %all_to_all.10.parts_ref = bf16[8,208,128]{2,1,0:T(8,128)(2,1)} all-to-all(bf16[8,208,128]{2,1,0:T(8,128)(2,1)S(1)} %attend.9), channel_id=1, replica_groups={{0,16,256,272,8,24,264,280},{32,48,288,304,40,56,296,312},{64,80,320,33..., dimensions={0} | all-to-all | bytes 851968 | tf_op jit(solution)/shard_map/all_to_all | solution.py:297
  78.1 0.0 copy-start.2
  78.1 0.0 copy-start
  78.1 2.5 %merge.1 = bf16[8,192,256]{2,1,0:T(8,128)(2,1)} custom-call(bf16[8,208,128]{2,1,0:T(8,128)(2,1)} %all_to_all.10.parts_ref), custom_call_target="tpu_custom_call" | custom-call | tf_op jit(solution)/shard_map/merge/pallas_call | solution.py:220
  80.6 6.1 %all-to-all-start.1 = ((bf16[8,192,256]{2,1,0:T(8,128)(2,1)}), bf16[8,192,256]{2,1,0:T(8,128)(2,1)S(1)}, u32[]{:S(2)}, u32[]{:S(2)}) async-start(bf16[8,192,256]{2,1,0:T(8,128)(2,1)} %merge.1), calls=%async_computation.1 | async-start | bytes 1572864 | tf_op jit(solution)/shard_map/all_to_all | solution.py:301
  86.8 0.0 copy-done.2
  86.8 13.5 %all-to-all-done.1.parts_ref = bf16[8,192,256]{2,1,0:T(8,128)(2,1)S(1)} async-done(((bf16[8,192,256]{2,1,0:T(8,128)(2,1)}), bf16[8,192,256]{2,1,0:T(8,128)(2,1)S(1)}, u32[]{:S(2)}, u32[]{:S(2)}) %all-to-all-start.1) | async-done | bytes 786464 | tf_op jit(solution)/shard_map/all_to_all | solution.py:301
  100.3 0.0 copy-done
  100.3 1.2 %project.1 = bf16[192,384]{1,0:T(8,128)(2,1)} custom-call(bf16[8,192,256]{2,1,0:T(8,128)(2,1)S(1)} %all-to-all-done.1.parts_ref, bf16[2048,384]{1,0:T(8,128)(2,1)S(1)} %copy-done, f32[1,384]{1,0:T(1,128)S(1)} %broadcast_in_dim.14.gate_ref), custom_call_target="tpu_custom_call" | custom-call | tf_op jit(solution)/shard_map/project/pallas_call | solution.py:237
  (8 shorter events, 0.1 us)
Async XLA Ops:
  5.0 35.6 %copy-start.1 = (bf16[5,192,128]{2,1,0:T(8,128)(2,1)S(1)}, bf16[5,192,128]{2,1,0:T(8,128)(2,1)}, u32[]{:S(2)}) copy-start(bf16[5,192,128]{2,1,0:T(8,128)(2,1)} %get-tuple-element.25.refs_3_) | copy-start | bytes 737284
  5.0 10.6 %collective-permute-start = (bf16[5,192,128]{2,1,0:T(8,128)(2,1)}, bf16[5,192,128]{2,1,0:T(8,128)(2,1)S(1)}, u32[]{:S(2)}, u32[]{:S(2)}) collective-permute-start(bf16[5,192,128]{2,1,0:T(8,128)(2,1)} %get-tuple-element.26), channel_id=1, source_target_pairs={{0,8},{8,0},{16,24},{24,16},{32,40},{40,32},{48,56},{56,48},{64,72... | collective-permute-start | bytes 737288 | tf_op jit(solution)/shard_map/ppermute | solution.py:276
  15.7 12.0 %collective-permute-start.3 = (bf16[2,2,192,128]{3,2,1,0:T(8,128)(2,1)S(1)}, bf16[2,2,192,128]{3,2,1,0:T(8,128)(2,1)S(1)}, u32[]{:S(2)}, u32[]{:S(2)}) collective-permute-start(bf16[2,2,192,128]{3,2,1,0:T(8,128)(2,1)S(1)} %pad_maximum_fusion.1.refs_5_), channel_id=1, source_target_pairs={{0,224},{8,40},{16,240},{24,56},{32,64},{40,8},{48,80},{56,24},{64... | collective-permute-start | bytes 589832 | tf_op jit(solution)/shard_map/ppermute | solution.py:279
  17.7 12.1 %collective-permute-start.1 = (bf16[384,128]{1,0:T(8,128)(2,1)S(1)}, bf16[384,128]{1,0:T(8,128)(2,1)S(1)}, u32[]{:S(2)}, u32[]{:S(2)}) collective-permute-start(bf16[384,128]{1,0:T(8,128)(2,1)S(1)} %pad_maximum_fusion.2), channel_id=1, source_target_pairs={{0,16},{8,24},{16,0},{24,8},{32,48},{40,56},{48,32},{56,40},{64,80... | collective-permute-start | bytes 294920 | tf_op jit(solution)/shard_map/ppermute | solution.py:282
  19.6 13.3 %collective-permute-start.6 = (bf16[2,2,192,128]{3,2,1,0:T(8,128)(2,1)S(1)}, bf16[2,2,192,128]{3,2,1,0:T(8,128)(2,1)S(1)}, u32[]{:S(2)}, u32[]{:S(2)}) collective-permute-start(bf16[2,2,192,128]{3,2,1,0:T(8,128)(2,1)S(1)} %pad_maximum_fusion.1.refs_5_), channel_id=1, source_target_pairs={{0,32},{8,232},{16,48},{24,248},{32,0},{40,72},{48,16},{56,88},{64... | collective-permute-start | bytes 589832 | tf_op jit(solution)/shard_map/ppermute | solution.py:280
  27.7 10.1 %collective-permute-start.4 = (bf16[2,2,192,128]{3,2,1,0:T(8,128)(2,1)S(1)}, bf16[2,2,192,128]{3,2,1,0:T(8,128)(2,1)S(1)}, u32[]{:S(2)}, u32[]{:S(2)}) collective-permute-start(bf16[2,2,192,128]{3,2,1,0:T(8,128)(2,1)S(1)} %collective-permute-done.3.refs_5_), channel_id=1, source_target_pairs={{0,32},{8,232},{16,48},{24,248},{32,0},{40,72},{48,16},{56,88},{64... | collective-permute-start | bytes 589832 | tf_op jit(solution)/shard_map/ppermute | solution.py:283
  29.8 10.9 %collective-permute-start.2 = (bf16[768,128]{1,0:T(8,128)(2,1)S(1)}, bf16[768,128]{1,0:T(8,128)(2,1)S(1)}, u32[]{:S(2)}, u32[]{:S(2)}) collective-permute-start(bf16[768,128]{1,0:T(8,128)(2,1)S(1)} %pad_maximum_fusion.refs_1_.refs_0_), channel_id=1, source_target_pairs={{0,256},{8,264},{16,272},{24,280},{32,288},{40,296},{48,304},{56,3... | collective-permute-start | bytes 589832 | tf_op jit(solution)/shard_map/ppermute | solution.py:285
  32.9 11.5 %collective-permute-start.7 = (bf16[2,2,192,128]{3,2,1,0:T(8,128)(2,1)S(1)}, bf16[2,2,192,128]{3,2,1,0:T(8,128)(2,1)S(1)}, u32[]{:S(2)}, u32[]{:S(2)}) collective-permute-start(bf16[2,2,192,128]{3,2,1,0:T(8,128)(2,1)S(1)} %collective-permute-done.6.refs_6_), channel_id=1, source_target_pairs={{0,224},{8,40},{16,240},{24,56},{32,64},{40,8},{48,80},{56,24},{64... | collective-permute-start | bytes 589832 | tf_op jit(solution)/shard_map/ppermute | solution.py:284
  37.8 12.9 %collective-permute-start.5 = (bf16[2,2,192,128]{3,2,1,0:T(8,128)(2,1)S(1)}, bf16[2,2,192,128]{3,2,1,0:T(8,128)(2,1)S(1)}, u32[]{:S(2)}, u32[]{:S(2)}) collective-permute-start(bf16[2,2,192,128]{3,2,1,0:T(8,128)(2,1)S(1)} %collective-permute-done.4.refs_5_), channel_id=1, source_target_pairs={{0,224},{8,40},{16,240},{24,56},{32,64},{40,8},{48,80},{56,24},{64... | collective-permute-start | bytes 589832 | tf_op jit(solution)/shard_map/ppermute | solution.py:286
  44.5 10.1 %collective-permute-start.8 = (bf16[2,2,192,128]{3,2,1,0:T(8,128)(2,1)S(1)}, bf16[2,2,192,128]{3,2,1,0:T(8,128)(2,1)S(1)}, u32[]{:S(2)}, u32[]{:S(2)}) collective-permute-start(bf16[2,2,192,128]{3,2,1,0:T(8,128)(2,1)S(1)} %collective-permute-done.7.refs_6_), channel_id=1, source_target_pairs={{0,32},{8,232},{16,48},{24,248},{32,0},{40,72},{48,16},{56,88},{64... | collective-permute-start | bytes 589832 | tf_op jit(solution)/shard_map/ppermute | solution.py:291
  50.7 9.7 %collective-permute-start.9 = (bf16[2,2,192,128]{3,2,1,0:T(8,128)(2,1)S(1)}, bf16[2,2,192,128]{3,2,1,0:T(8,128)(2,1)S(1)}, u32[]{:S(2)}, u32[]{:S(2)}) collective-permute-start(bf16[2,2,192,128]{3,2,1,0:T(8,128)(2,1)S(1)} %collective-permute-done.5.refs_5_), channel_id=1, source_target_pairs={{0,32},{8,232},{16,48},{24,248},{32,0},{40,72},{48,16},{56,88},{64... | collective-permute-start | bytes 589832 | tf_op jit(solution)/shard_map/ppermute | solution.py:294
  78.1 8.7 %copy-start.2 = (f32[384]{0:T(512)S(1)}, f32[384]{0:T(512)}, u32[]{:S(2)}) copy-start(f32[384]{0:T(512)} %param.16) | copy-start | bytes 4612
  78.1 22.2 %copy-start = (bf16[2048,384]{1,0:T(8,128)(2,1)S(1)}, bf16[2048,384]{1,0:T(8,128)(2,1)}, u32[]{:S(2)}) copy-start(bf16[2048,384]{1,0:T(8,128)(2,1)} %weight_ref.1) | copy-start | bytes 4718596
  80.6 19.7 %all-to-all-start.1 = ((bf16[8,192,256]{2,1,0:T(8,128)(2,1)}), bf16[8,192,256]{2,1,0:T(8,128)(2,1)S(1)}, u32[]{:S(2)}, u32[]{:S(2)}) async-start(bf16[8,192,256]{2,1,0:T(8,128)(2,1)} %merge.1), calls=%async_computation.1 | async-start | bytes 1572864 | tf_op jit(solution)/shard_map/all_to_all | solution.py:301

commit v5 on v4

--- a/solution.py
+++ b/solution.py
@@ -17,8 +17,10 @@
 ROWS_SENT = TOKENS + STAT_ROWS
 LOG2E = 1.4426950408889634
 VMEM_LIMIT = 20 * 1024 * 1024
+SMALL = pltpu.CompilerParams(vmem_limit_bytes=8 * 1024 * 1024)
 
 PATCHES = 64
+CORES = [[i, i + 1] for i in range(0, PATCHES, 2)]
 QUERY_GROUPS = [
     [x * 32 + (2 * pair + z) * 2 + core for core in range(2) for x in range(2) for z in range(2)]
     for pair in range(8)
@@ -40,43 +42,33 @@
 
 
 def prepare_body(
-    core_ref, q_ref, k_ref, v_ref, stale_ref, q_gain_ref, k_gain_ref, cos_ref, sin_ref, k_out, mine_out, send_out
+    q_ref, k_ref, v_ref, stale_ref, q_gain_ref, k_gain_ref, cos_ref, sin_ref, k_out, all_out
 ):
     cosine = jnp.concatenate([cos_ref[...], cos_ref[...]], axis=1)
     signed_sine = jnp.concatenate([-sin_ref[...], sin_ref[...]], axis=1)
-    first = core_ref[0] == 0
-
-    def put(part, heads):
-        mine_out[part] = jnp.where(first, heads[0], heads[1])
-        send_out[part] = jnp.where(first, heads[1], heads[0])
-
     for part, (raw, gain) in enumerate(((q_ref, q_gain_ref), (k_ref, k_gain_ref))):
-        heads = []
         for h in range(HEADS_HERE):
             cols = slice(h * HEAD, (h + 1) * HEAD)
             x = raw[:, cols].astype(F32)
             squares = jnp.mean(x * x, axis=-1, keepdims=True)
             n = x * lax.rsqrt(squares + 1e-06) * gain[...]
             turned = (n * cosine + pltpu.roll(n, HEAD // 2, 1) * signed_sine).astype(BF16)
-            heads.append(turned)
+            all_out[part, :, cols] = turned
             if part == 1:
                 k_out[:, cols] = turned
-        put(part, heads)
-    put(2, [v_ref[:, :HEAD], v_ref[:, HEAD:]])
-    for part in range(2):
-        put(3 + part, [stale_ref[part, :, :HEAD], stale_ref[part, :, HEAD:]])
-
-
-def prepare(core, query_raw, key_raw, value_raw, stale_pairs, query_gain, key_gain, cosine, sine):
-    halves = jax.ShapeDtypeStruct((5, TOKENS, HEAD), BF16)
+    all_out[2] = v_ref[...]
+    all_out[3:] = stale_ref[...]
+
+
+def prepare(query_raw, key_raw, value_raw, stale_pairs, query_gain, key_gain, cosine, sine):
     return pl.pallas_call(
         prepare_body,
-        in_specs=[pl.BlockSpec(memory_space=pltpu.SMEM)]
-        + [pl.BlockSpec(memory_space=pltpu.VMEM)] * 8,
-        out_shape=(jax.ShapeDtypeStruct((TOKENS, WIDTH), BF16), halves, halves),
+        out_shape=(
+            jax.ShapeDtypeStruct((TOKENS, WIDTH), BF16),
+            jax.ShapeDtypeStruct((5, TOKENS, WIDTH), BF16),
+        ),
         name="norm_rotate",
     )(
-        core,
         query_raw,
         key_raw,
         value_raw,
@@ -92,9 +84,9 @@
     refs = list(refs)
     take = lambda count: [refs.pop(0) for _ in range(count)]
     scale = HEAD**-0.5 * LOG2E
-    place_ref = take(1)[0] if begins or ends else None
+    place_ref = take(1)[0] if ends else None
     q_refs = take(2)
-    fresh_refs = take(2) if begins else None
+    fresh_ref = take(1)[0] if begins else None
     before = None if begins else take(3)
     shares = take(share_count)
     half = q_refs[0].shape[0]
@@ -102,7 +94,7 @@
     def rows_of(part, patch=None):
         picked = [share[part, core] for share in shares for core in range(2)]
         if patch is not None:
-            picked[patch] = fresh_refs[patch][1 + part]
+            picked[patch] = fresh_ref[part, patch]
         return jnp.concatenate(picked)
 
     size = 2 * TOKENS
@@ -128,7 +120,7 @@
         out = (acc / total).astype(BF16)
         for g in range(at // TOKENS, (at + size) // TOKENS):
             rows = slice(g * TOKENS - at, (g + 1) * TOKENS - at)
-            to = jnp.bitwise_xor(place_ref[1], g % 2) * 4 + jnp.bitwise_xor(place_ref[0], g // 2)
+            to = (g % 2) * 4 + jnp.bitwise_xor(place_ref[0], g // 2)
             refs[0][to, :TOKENS, :] = out[rows]
             flat = jnp.transpose(packed[rows])[:8]
             rest = jnp.concatenate([flat[:, HEAD:], jnp.zeros((8, 2 * HEAD - TOKENS), F32)], axis=1)
@@ -163,15 +155,14 @@
                 ref[rows, :] = value
 
 
-def attend(queries, shares, fresh=(), state=(), place=None, ends=False):
+def attend(queries, shares, fresh=None, state=(), place=None):
     rows = 2 * queries[0].shape[0]
-    begins = bool(fresh)
-    operands = [*queries, *fresh, *state, *shares]
+    begins, ends = fresh is not None, place is not None
+    operands = [*queries, *([fresh] if begins else []), *state, *shares]
     specs = [pl.BlockSpec(memory_space=pltpu.VMEM)] * len(operands)
-    if begins or ends:
+    if ends:
         operands.insert(0, place)
         specs.insert(0, pl.BlockSpec(memory_space=pltpu.SMEM))
-    if ends:
         out_shape = jax.ShapeDtypeStruct((rows // TOKENS, ROWS_SENT, HEAD), BF16)
     else:
         out_shape = (jax.ShapeDtypeStruct((rows, HEAD), F32),) * 3
@@ -220,6 +211,7 @@
     return pl.pallas_call(
         merge_body,
         out_shape=jax.ShapeDtypeStruct((copies, TOKENS, WIDTH), BF16),
+        compiler_params=SMALL,
         name="merge",
     )(parts)
 
@@ -237,7 +229,7 @@
     return pl.pallas_call(
         project_body,
         out_shape=jax.ShapeDtypeStruct((TOKENS, out_weight.shape[1]), BF16),
-        compiler_params=pltpu.CompilerParams(vmem_limit_bytes=VMEM_LIMIT),
+        compiler_params=SMALL,
         name="project",
     )(parts, out_weight, attn_gate[None])
 
@@ -262,30 +254,23 @@
     )
     angles = positions.astype(F32)[:, None] * frequency
     cosine, sine = jnp.cos(angles), jnp.sin(angles)
-    fresh_keys, mine, send = prepare(
-        core[None],
-        query_raw,
-        key_raw,
-        value_raw,
-        stale_pairs,
-        query_gain,
-        key_gain,
-        cosine,
-        sine,
-    )
-    theirs = lax.ppermute(send, "patch", swapped(1))
-    share = jnp.stack([mine[3:], theirs[3:]], axis=1)
+    fresh_keys, prepared = prepare(
+        query_raw, key_raw, value_raw, stale_pairs, query_gain, key_gain, cosine, sine
+    )
+    rows = lax.all_gather(prepared, "patch", axis=0, axis_index_groups=CORES)
+    rows = jnp.swapaxes(rows, 0, 1)
+    rows = lax.dynamic_slice_in_dim(rows, core * HEAD, HEAD, axis=3)
+    near, fresh, share = rows[0].reshape(2 * TOKENS, HEAD), rows[1:3], rows[3:]
     one, other = ring_swaps(True), ring_swaps(False)
     first = lax.ppermute(share, "patch", other)
     second = lax.ppermute(share, "patch", one)
-    near = jnp.concatenate([mine[0], theirs[0]])
     near = jnp.concatenate([near, lax.ppermute(near, "patch", swapped(2))])
     third = lax.ppermute(first, "patch", one)
     fourth = lax.ppermute(second, "patch", other)
     queries = (near, lax.ppermute(near, "patch", swapped(32)))
     fifth = lax.ppermute(third, "patch", other)
-    place = jnp.stack([(me // 32) * 2 + (me // 2) % 2, core])
-    state = attend(queries, [share], fresh=(mine, theirs), place=place)
+    place = ((me // 32) * 2 + (me // 2) % 2)[None]
+    state = attend(queries, [share], fresh=fresh)
     state = attend(queries, [first, second], state=state)
     fourth, state = lax.optimization_barrier((fourth, state))
     sixth = lax.ppermute(fourth, "patch", one)
@@ -293,7 +278,7 @@
     fifth, state = lax.optimization_barrier((fifth, state))
     far = lax.ppermute(fifth, "patch", one)
     state = attend(queries, [fifth, sixth], state=state)
-    parts = attend(queries, [far], state=state, place=place, ends=True)
+    parts = attend(queries, [far], state=state, place=place)
     parts = lax.all_to_all(
         parts, "patch", split_axis=0, concat_axis=0, tiled=True, axis_index_groups=QUERY_GROUPS
     )

time: 102 us -> 100 us (0.980)
  blocking collectives: 15.7 us -> 25.7 us
  starting transfers between devices: 44.4 us -> 36.9 us
  Pallas kernels: 16.6 us -> 13.6 us
  local copies, waits for them, and re-layouts: 1.73 us -> 0.13 us
    all_gather x0 -> x1, blocking collectives: none -> 9.21 us  [shards(): rows = lax.all_gather(prepared, 'patch', axis=0, axis_index_groups=CORES)]
    ppermute x1 -> x0, starting transfers between devices: 8.91 us -> none  [shards(): theirs = lax.ppermute(send, 'patch', swapped(1))]
    ppermute x1, waiting for transfers between devices: 2.7 us -> 0.39 us  [shards(): third = lax.ppermute(first, 'patch', one)]
    ppermute x1, waiting for transfers between devices: 0.47 us -> 2.49 us  [shards(): sixth = lax.ppermute(fourth, 'patch', one)]
    pallas_call x5, Pallas kernels: 10.2 us -> 8.4 us  [attend(): pl.pallas_call(functools.partial(attend_body, len(shares), begins, ends),...]
    ppermute x1, waiting for transfers between devices: 0.01 us -> 1.39 us  [shards(): second = lax.ppermute(share, 'patch', one)]
    ppermute x1, waiting for transfers between devices: 3.66 us -> 2.43 us  [shards(): far = lax.ppermute(fifth, 'patch', one)]
    ppermute x1, starting transfers between devices: 2.75 us -> 3.95 us  [shards(): fifth = lax.ppermute(third, 'patch', other)]
  transfers between devices with their start and end apart: 11 -> 10, of which waited for: 4 -> 6; matrix products, arithmetic and copies ran while one was open for 2% -> 0% of each run, Pallas kernels for 8% -> 7%
where the time goes in v5:
time: 100 us; the launch traced here: 99.8 us
  starting transfers between devices  36.9 us (37%)
  blocking collectives  25.7 us (26%)
  waiting for transfers between devices  20.7 us (21%)
  Pallas kernels  13.6 us (14%)
  between operations  1.53 us (2%)
  other arithmetic  1.12 us (1%)
    all_to_all x1, blocking collectives, shards(): lax.all_to_all(parts, 'patch', split_axis=0, concat_axis=0, tiled=True, a...  16.5 us
    all_to_all x1, waiting for transfers between devices, shards(): lax.all_to_all(copies, 'head', split_axis=0, concat_axis=0, tiled=True)  13.5 us
    all_gather x1, blocking collectives, shards(): rows = lax.all_gather(prepared, 'patch', axis=0, axis_index_groups=CORES)  9.21 us
    pallas_call x5, Pallas kernels, attend(): pl.pallas_call(functools.partial(attend_body, len(shares), begins, ends),...  8.4 us
    ppermute x1, starting transfers between devices, shards(): second = lax.ppermute(share, 'patch', one)  8.08 us
    all_to_all x1, starting transfers between devices, shards(): lax.all_to_all(copies, 'head', split_axis=0, concat_axis=0, tiled=True)  6.57 us
    ppermute x1, starting transfers between devices, shards(): fifth = lax.ppermute(third, 'patch', other)  3.95 us
    ppermute x1, starting transfers between devices, shards(): far = lax.ppermute(fifth, 'patch', one)  3.83 us
  transfers between devices with their start and end apart: 10, of which 6 were waited for; matrix products, arithmetic and copies ran while one was open for 0% of the time, Pallas kernels for 7%

profile of v5, /device:TPU:1, one launch (start us, length us, event | category | flops | bytes accessed | tf_op | source)
XLA Modules:
  0.0 99.8 jit_solution(6546901154694369112)
XLA Ops:
  1.3 1.1 %multiply_sine_fusion = (f32[192,64]{1,0:T(8,128)}, f32[192,64]{1,0:T(8,128)}) fusion(f32[64]{0:T(128)S(1)} %multiply_exponential_fusion, f32[192]{0:T(256)S(1)} %add_convert_fusion), kind=kLoop, calls=%fused_computation.2 | loop fusion | flops 12288 | bytes 99328 | tf_op jit(solution)/shard_map/sin | solution.py:256
  2.4 2.6 %norm_rotate.1 = (bf16[192,256]{1,0:T(8,128)(2,1)}, bf16[5,192,256]{2,1,0:T(8,128)(2,1)}) custom-call(bf16[192,256]{1,0:T(8,128)(2,1)} %q_ref.1, bf16[192,256]{1,0:T(8,128)(2,1)} %k_ref.1, bf16[192,256]{1,0:T(8,128)(2,1)} %v_ref.1, bf16[2,192,256]{2,1,0:T(8,128)(2,1)} %stale_ref.1, f32[1,128]{1,0:T(1,128)} %bitcast.12, f32[1,128]{1,0:T(1,128)} %bitcast.13, ...), custom_call_target="tpu_custom_call" | custom-call | tf_op jit(solution)/shard_map/norm_rotate/pallas_call | solution.py:64
  5.0 9.2 %all-gather = bf16[10,192,256]{2,1,0:T(8,128)(2,1)S(1)} all-gather(bf16[5,192,256]{2,1,0:T(8,128)(2,1)} %get-tuple-element.24), channel_id=2, replica_groups={{0,8},{16,24},{32,40},{48,56},{64,72},{80,88},{96,104},{112,120},{128,1..., dimensions={0}, use_global_device_ids=true | all-gather | bytes 1474560 | tf_op jit(solution)/shard_map/all_gather | solution.py:260
  14.3 0.1 copy_bitcast_fusion
  14.4 1.9 %collective-permute-start.2 = (bf16[2,2,192,128]{3,2,1,0:T(8,128)(2,1)S(1)}, bf16[2,2,192,128]{3,2,1,0:T(8,128)(2,1)S(1)}, u32[]{:S(2)}, u32[]{:S(2)}) collective-permute-start(bf16[2,2,192,128]{3,2,1,0:T(8,128)(2,1)S(1)} %get-tuple-element.47.refs_3_), channel_id=1, source_target_pairs={{0,224},{8,40},{16,240},{24,56},{32,64},{40,8},{48,80},{56,24},{64... | collective-permute-start | bytes 589832 | tf_op jit(solution)/shard_map/ppermute | solution.py:265
  16.3 1.9 %collective-permute-start = (bf16[384,128]{1,0:T(8,128)(2,1)S(1)}, bf16[384,128]{1,0:T(8,128)(2,1)S(1)}, u32[]{:S(2)}, u32[]{:S(2)}) collective-permute-start(bf16[384,128]{1,0:T(8,128)(2,1)S(1)} %bitcast.10), channel_id=1, source_target_pairs={{0,16},{8,24},{16,0},{24,8},{32,48},{40,56},{48,32},{56,40},{64,80... | collective-permute-start | bytes 294920 | tf_op jit(solution)/shard_map/ppermute | solution.py:267
  18.3 8.1 %collective-permute-start.5 = (bf16[2,2,192,128]{3,2,1,0:T(8,128)(2,1)S(1)}, bf16[2,2,192,128]{3,2,1,0:T(8,128)(2,1)S(1)}, u32[]{:S(2)}, u32[]{:S(2)}) collective-permute-start(bf16[2,2,192,128]{3,2,1,0:T(8,128)(2,1)S(1)} %get-tuple-element.47.refs_3_), channel_id=1, source_target_pairs={{0,32},{8,232},{16,48},{24,248},{32,0},{40,72},{48,16},{56,88},{64... | collective-permute-start | bytes 589832 | tf_op jit(solution)/shard_map/ppermute | solution.py:266
  26.3 0.0 collective-permute-done.2.refs_5_
  26.4 2.0 %collective-permute-start.3 = (bf16[2,2,192,128]{3,2,1,0:T(8,128)(2,1)S(1)}, bf16[2,2,192,128]{3,2,1,0:T(8,128)(2,1)S(1)}, u32[]{:S(2)}, u32[]{:S(2)}) collective-permute-start(bf16[2,2,192,128]{3,2,1,0:T(8,128)(2,1)S(1)} %collective-permute-done.2.refs_5_), channel_id=1, source_target_pairs={{0,32},{8,232},{16,48},{24,248},{32,0},{40,72},{48,16},{56,88},{64... | collective-permute-start | bytes 589832 | tf_op jit(solution)/shard_map/ppermute | solution.py:268
  28.4 0.0 collective-permute-done
  28.4 3.1 %collective-permute-start.1 = (bf16[768,128]{1,0:T(8,128)(2,1)S(1)}, bf16[768,128]{1,0:T(8,128)(2,1)S(1)}, u32[]{:S(2)}, u32[]{:S(2)}) collective-permute-start(bf16[768,128]{1,0:T(8,128)(2,1)S(1)} %pad_maximum_fusion.refs_0_.refs_1_), channel_id=1, source_target_pairs={{0,256},{8,264},{16,272},{24,280},{32,288},{40,296},{48,304},{56,3... | collective-permute-start | bytes 589832 | tf_op jit(solution)/shard_map/ppermute | solution.py:270
  31.6 1.4 %collective-permute-done.5.refs_6_ = bf16[2,2,192,128]{3,2,1,0:T(8,128)(2,1)S(1)} collective-permute-done((bf16[2,2,192,128]{3,2,1,0:T(8,128)(2,1)S(1)}, bf16[2,2,192,128]{3,2,1,0:T(8,128)(2,1)S(1)}, u32[]{:S(2)}, u32[]{:S(2)}) %collective-permute-start.5) | collective-permute-done | bytes 196640 | tf_op jit(solution)/shard_map/ppermute | solution.py:266
  33.0 1.9 %collective-permute-start.6 = (bf16[2,2,192,128]{3,2,1,0:T(8,128)(2,1)S(1)}, bf16[2,2,192,128]{3,2,1,0:T(8,128)(2,1)S(1)}, u32[]{:S(2)}, u32[]{:S(2)}) collective-permute-start(bf16[2,2,192,128]{3,2,1,0:T(8,128)(2,1)S(1)} %collective-permute-done.5.refs_6_), channel_id=1, source_target_pairs={{0,224},{8,40},{16,240},{24,56},{32,64},{40,8},{48,80},{56,24},{64... | collective-permute-start | bytes 589832 | tf_op jit(solution)/shard_map/ppermute | solution.py:269
  34.9 0.4 collective-permute-done.3.refs_5_
  35.3 4.0 %collective-permute-start.4 = (bf16[2,2,192,128]{3,2,1,0:T(8,128)(2,1)S(1)}, bf16[2,2,192,128]{3,2,1,0:T(8,128)(2,1)S(1)}, u32[]{:S(2)}, u32[]{:S(2)}) collective-permute-start(bf16[2,2,192,128]{3,2,1,0:T(8,128)(2,1)S(1)} %collective-permute-done.3.refs_5_), channel_id=1, source_target_pairs={{0,224},{8,40},{16,240},{24,56},{32,64},{40,8},{48,80},{56,24},{64... | collective-permute-start | bytes 589832 | tf_op jit(solution)/shard_map/ppermute | solution.py:271
  39.2 0.0 collective-permute-done.1.refs_1_.refs_2_
  39.2 1.1 %attend.5 = (f32[1536,128]{1,0:T(8,128)S(1)}, f32[1536,128]{1,0:T(8,128)S(1)}, f32[1536,128]{1,0:T(8,128)S(1)}) custom-call(bf16[768,128]{1,0:T(8,128)(2,1)S(1)} %pad_maximum_fusion.refs_0_.refs_1_, bf16[768,128]{1,0:T(8,128)(2,1)S(1)} %collective-permute-done.1.refs_1_.refs_2_, bf16[2,2,192,128]{3,2,1,0:T(8,128)(2,1)S(1)} %get-tuple-element.46.refs_2_, ...), custom_call_target="tpu_custom_call" | custom-call | flops 301989888 | bytes 2359296 | tf_op jit(solution)/shard_map/attend/pallas_call | solution.py:170
  40.3 2.0 %attend.6 = (f32[1536,128]{1,0:T(8,128)S(1)}, f32[1536,128]{1,0:T(8,128)S(1)}, f32[1536,128]{1,0:T(8,128)S(1)}) custom-call(bf16[768,128]{1,0:T(8,128)(2,1)S(1)} %pad_maximum_fusion.refs_0_.refs_1_, bf16[768,128]{1,0:T(8,128)(2,1)S(1)} %collective-permute-done.1.refs_1_.refs_2_, f32[1536,128]{1,0:T(8,128)S(1)} %get-tuple-element.25.refs_2_, ...), custom_call_target="tpu_custom_call" | custom-call | flops 603979776 | bytes 2359296 | tf_op jit(solution)/shard_map/attend/pallas_call | solution.py:170
  42.3 0.5 collective-permute-done.6.refs_6_
  42.8 3.5 %collective-permute-start.7 = (bf16[2,2,192,128]{3,2,1,0:T(8,128)(2,1)S(1)}, bf16[2,2,192,128]{3,2,1,0:T(8,128)(2,1)S(1)}, u32[]{:S(2)}, u32[]{:S(2)}) collective-permute-start(bf16[2,2,192,128]{3,2,1,0:T(8,128)(2,1)S(1)} %collective-permute-done.6.refs_6_), channel_id=1, source_target_pairs={{0,32},{8,232},{16,48},{24,248},{32,0},{40,72},{48,16},{56,88},{64... | collective-permute-start | bytes 589832 | tf_op jit(solution)/shard_map/ppermute | solution.py:276
  46.4 2.0 %attend.7 = (f32[1536,128]{1,0:T(8,128)S(1)}, f32[1536,128]{1,0:T(8,128)S(1)}, f32[1536,128]{1,0:T(8,128)S(1)}) custom-call(bf16[768,128]{1,0:T(8,128)(2,1)S(1)} %pad_maximum_fusion.refs_0_.refs_1_, bf16[768,128]{1,0:T(8,128)(2,1)S(1)} %collective-permute-done.1.refs_1_.refs_2_, f32[1536,128]{1,0:T(8,128)S(1)} %get-tuple-element.31.refs_2_, ...), custom_call_target="tpu_custom_call" | custom-call | flops 603979776 | bytes 2359296 | tf_op jit(solution)/shard_map/attend/pallas_call | solution.py:170
  48.3 0.0 collective-permute-done.4.refs_5_
  48.3 3.8 %collective-permute-start.8 = (bf16[2,2,192,128]{3,2,1,0:T(8,128)(2,1)S(1)}, bf16[2,2,192,128]{3,2,1,0:T(8,128)(2,1)S(1)}, u32[]{:S(2)}, u32[]{:S(2)}) collective-permute-start(bf16[2,2,192,128]{3,2,1,0:T(8,128)(2,1)S(1)} %collective-permute-done.4.refs_5_), channel_id=1, source_target_pairs={{0,32},{8,232},{16,48},{24,248},{32,0},{40,72},{48,16},{56,88},{64... | collective-permute-start | bytes 589832 | tf_op jit(solution)/shard_map/ppermute | solution.py:279
  52.2 2.5 %collective-permute-done.7.refs_6_ = bf16[2,2,192,128]{3,2,1,0:T(8,128)(2,1)S(1)} collective-permute-done((bf16[2,2,192,128]{3,2,1,0:T(8,128)(2,1)S(1)}, bf16[2,2,192,128]{3,2,1,0:T(8,128)(2,1)S(1)}, u32[]{:S(2)}, u32[]{:S(2)}) %collective-permute-start.7) | collective-permute-done | bytes 196640 | tf_op jit(solution)/shard_map/ppermute | solution.py:276
  54.7 2.0 %attend.8 = (f32[1536,128]{1,0:T(8,128)S(1)}, f32[1536,128]{1,0:T(8,128)S(1)}, f32[1536,128]{1,0:T(8,128)S(1)}) custom-call(bf16[768,128]{1,0:T(8,128)(2,1)S(1)} %pad_maximum_fusion.refs_0_.refs_1_, bf16[768,128]{1,0:T(8,128)(2,1)S(1)} %collective-permute-done.1.refs_1_.refs_2_, f32[1536,128]{1,0:T(8,128)S(1)} %get-tuple-element.38.refs_2_, ...), custom_call_target="tpu_custom_call" | custom-call | flops 603979776 | bytes 2359296 | tf_op jit(solution)/shard_map/attend/pallas_call | solution.py:170
  56.7 2.4 %collective-permute-done.8.refs_6_ = bf16[2,2,192,128]{3,2,1,0:T(8,128)(2,1)S(1)} collective-permute-done((bf16[2,2,192,128]{3,2,1,0:T(8,128)(2,1)S(1)}, bf16[2,2,192,128]{3,2,1,0:T(8,128)(2,1)S(1)}, u32[]{:S(2)}, u32[]{:S(2)}) %collective-permute-start.8) | collective-permute-done | bytes 196640 | tf_op jit(solution)/shard_map/ppermute | solution.py:279
  59.1 1.4 %attend.9 = bf16[8,208,128]{2,1,0:T(8,128)(2,1)S(1)} custom-call(s32[1]{0:T(128)} %bitcast.refs_0_, bf16[768,128]{1,0:T(8,128)(2,1)S(1)} %pad_maximum_fusion.refs_0_.refs_1_, bf16[768,128]{1,0:T(8,128)(2,1)S(1)} %collective-permute-done.1.refs_1_.refs_2_, f32[1536,128]{1,0:T(8,128)S(1)} %get-tuple-element.42.refs_3_, ...), custom_call_target="tpu_custom_call" | custom-call | flops 301989888 | bytes 2359296 | tf_op jit(solution)/shard_map/attend/pallas_call | solution.py:170
  60.5 16.5 %all_to_all.10.parts_ref = bf16[8,208,128]{2,1,0:T(8,128)(2,1)S(1)} all-to-all(bf16[8,208,128]{2,1,0:T(8,128)(2,1)S(1)} %attend.9), channel_id=1, replica_groups={{0,16,256,272,8,24,264,280},{32,48,288,304,40,56,296,312},{64,80,320,33..., dimensions={0} | all-to-all | bytes 851968 | tf_op jit(solution)/shard_map/all_to_all | solution.py:282
  77.0 0.0 copy-start.1
  77.1 0.0 copy-start
  77.1 1.4 %merge.1 = bf16[8,192,256]{2,1,0:T(8,128)(2,1)} custom-call(bf16[8,208,128]{2,1,0:T(8,128)(2,1)S(1)} %all_to_all.10.parts_ref), custom_call_target="tpu_custom_call" | custom-call | tf_op jit(solution)/shard_map/merge/pallas_call | solution.py:211
  78.4 6.6 %all-to-all-start.1 = ((bf16[8,192,256]{2,1,0:T(8,128)(2,1)}), bf16[8,192,256]{2,1,0:T(8,128)(2,1)S(1)}, u32[]{:S(2)}, u32[]{:S(2)}) async-start(bf16[8,192,256]{2,1,0:T(8,128)(2,1)} %merge.1), calls=%async_computation.1 | async-start | bytes 1572864 | tf_op jit(solution)/shard_map/all_to_all | solution.py:286
  85.0 0.0 copy-done.1
  85.0 13.5 %all-to-all-done.1.parts_ref = bf16[8,192,256]{2,1,0:T(8,128)(2,1)S(1)} async-done(((bf16[8,192,256]{2,1,0:T(8,128)(2,1)}), bf16[8,192,256]{2,1,0:T(8,128)(2,1)S(1)}, u32[]{:S(2)}, u32[]{:S(2)}) %all-to-all-start.1) | async-done | bytes 786464 | tf_op jit(solution)/shard_map/all_to_all | solution.py:286
  98.5 0.0 copy-done
  98.5 1.2 %project.1 = bf16[192,384]{1,0:T(8,128)(2,1)} custom-call(bf16[8,192,256]{2,1,0:T(8,128)(2,1)S(1)} %all-to-all-done.1.parts_ref, bf16[2048,384]{1,0:T(8,128)(2,1)S(1)} %copy-done, f32[1,384]{1,0:T(1,128)S(1)} %broadcast_in_dim.17.gate_ref), custom_call_target="tpu_custom_call" | custom-call | tf_op jit(solution)/shard_map/project/pallas_call | solution.py:229
  (6 shorter events, 0.1 us)
Async XLA Ops:
  14.4 12.0 %collective-permute-start.2 = (bf16[2,2,192,128]{3,2,1,0:T(8,128)(2,1)S(1)}, bf16[2,2,192,128]{3,2,1,0:T(8,128)(2,1)S(1)}, u32[]{:S(2)}, u32[]{:S(2)}) collective-permute-start(bf16[2,2,192,128]{3,2,1,0:T(8,128)(2,1)S(1)} %get-tuple-element.47.refs_3_), channel_id=1, source_target_pairs={{0,224},{8,40},{16,240},{24,56},{32,64},{40,8},{48,80},{56,24},{64... | collective-permute-start | bytes 589832 | tf_op jit(solution)/shard_map/ppermute | solution.py:265
  16.3 12.1 %collective-permute-start = (bf16[384,128]{1,0:T(8,128)(2,1)S(1)}, bf16[384,128]{1,0:T(8,128)(2,1)S(1)}, u32[]{:S(2)}, u32[]{:S(2)}) collective-permute-start(bf16[384,128]{1,0:T(8,128)(2,1)S(1)} %bitcast.10), channel_id=1, source_target_pairs={{0,16},{8,24},{16,0},{24,8},{32,48},{40,56},{48,32},{56,40},{64,80... | collective-permute-start | bytes 294920 | tf_op jit(solution)/shard_map/ppermute | solution.py:267
  18.3 14.7 %collective-permute-start.5 = (bf16[2,2,192,128]{3,2,1,0:T(8,128)(2,1)S(1)}, bf16[2,2,192,128]{3,2,1,0:T(8,128)(2,1)S(1)}, u32[]{:S(2)}, u32[]{:S(2)}) collective-permute-start(bf16[2,2,192,128]{3,2,1,0:T(8,128)(2,1)S(1)} %get-tuple-element.47.refs_3_), channel_id=1, source_target_pairs={{0,32},{8,232},{16,48},{24,248},{32,0},{40,72},{48,16},{56,88},{64... | collective-permute-start | bytes 589832 | tf_op jit(solution)/shard_map/ppermute | solution.py:266
  26.4 8.9 %collective-permute-start.3 = (bf16[2,2,192,128]{3,2,1,0:T(8,128)(2,1)S(1)}, bf16[2,2,192,128]{3,2,1,0:T(8,128)(2,1)S(1)}, u32[]{:S(2)}, u32[]{:S(2)}) collective-permute-start(bf16[2,2,192,128]{3,2,1,0:T(8,128)(2,1)S(1)} %collective-permute-done.2.refs_5_), channel_id=1, source_target_pairs={{0,32},{8,232},{16,48},{24,248},{32,0},{40,72},{48,16},{56,88},{64... | collective-permute-start | bytes 589832 | tf_op jit(solution)/shard_map/ppermute | solution.py:268
  28.4 10.8 %collective-permute-start.1 = (bf16[768,128]{1,0:T(8,128)(2,1)S(1)}, bf16[768,128]{1,0:T(8,128)(2,1)S(1)}, u32[]{:S(2)}, u32[]{:S(2)}) collective-permute-start(bf16[768,128]{1,0:T(8,128)(2,1)S(1)} %pad_maximum_fusion.refs_0_.refs_1_), channel_id=1, source_target_pairs={{0,256},{8,264},{16,272},{24,280},{32,288},{40,296},{48,304},{56,3... | collective-permute-start | bytes 589832 | tf_op jit(solution)/shard_map/ppermute | solution.py:270
  33.0 9.8 %collective-permute-start.6 = (bf16[2,2,192,128]{3,2,1,0:T(8,128)(2,1)S(1)}, bf16[2,2,192,128]{3,2,1,0:T(8,128)(2,1)S(1)}, u32[]{:S(2)}, u32[]{:S(2)}) collective-permute-start(bf16[2,2,192,128]{3,2,1,0:T(8,128)(2,1)S(1)} %collective-permute-done.5.refs_6_), channel_id=1, source_target_pairs={{0,224},{8,40},{16,240},{24,56},{32,64},{40,8},{48,80},{56,24},{64... | collective-permute-start | bytes 589832 | tf_op jit(solution)/shard_map/ppermute | solution.py:269
  35.3 13.1 %collective-permute-start.4 = (bf16[2,2,192,128]{3,2,1,0:T(8,128)(2,1)S(1)}, bf16[2,2,192,128]{3,2,1,0:T(8,128)(2,1)S(1)}, u32[]{:S(2)}, u32[]{:S(2)}) collective-permute-start(bf16[2,2,192,128]{3,2,1,0:T(8,128)(2,1)S(1)} %collective-permute-done.3.refs_5_), channel_id=1, source_target_pairs={{0,224},{8,40},{16,240},{24,56},{32,64},{40,8},{48,80},{56,24},{64... | collective-permute-start | bytes 589832 | tf_op jit(solution)/shard_map/ppermute | solution.py:271
  42.8 11.9 %collective-permute-start.7 = (bf16[2,2,192,128]{3,2,1,0:T(8,128)(2,1)S(1)}, bf16[2,2,192,128]{3,2,1,0:T(8,128)(2,1)S(1)}, u32[]{:S(2)}, u32[]{:S(2)}) collective-permute-start(bf16[2,2,192,128]{3,2,1,0:T(8,128)(2,1)S(1)} %collective-permute-done.6.refs_6_), channel_id=1, source_target_pairs={{0,32},{8,232},{16,48},{24,248},{32,0},{40,72},{48,16},{56,88},{64... | collective-permute-start | bytes 589832 | tf_op jit(solution)/shard_map/ppermute | solution.py:276
  48.3 10.8 %collective-permute-start.8 = (bf16[2,2,192,128]{3,2,1,0:T(8,128)(2,1)S(1)}, bf16[2,2,192,128]{3,2,1,0:T(8,128)(2,1)S(1)}, u32[]{:S(2)}, u32[]{:S(2)}) collective-permute-start(bf16[2,2,192,128]{3,2,1,0:T(8,128)(2,1)S(1)} %collective-permute-done.4.refs_5_), channel_id=1, source_target_pairs={{0,32},{8,232},{16,48},{24,248},{32,0},{40,72},{48,16},{56,88},{64... | collective-permute-start | bytes 589832 | tf_op jit(solution)/shard_map/ppermute | solution.py:279
  77.0 8.0 %copy-start.1 = (f32[384]{0:T(512)S(1)}, f32[384]{0:T(512)}, u32[]{:S(2)}) copy-start(f32[384]{0:T(512)} %param.16) | copy-start | bytes 4612
  77.1 21.5 %copy-start = (bf16[2048,384]{1,0:T(8,128)(2,1)S(1)}, bf16[2048,384]{1,0:T(8,128)(2,1)}, u32[]{:S(2)}) copy-start(bf16[2048,384]{1,0:T(8,128)(2,1)} %weight_ref.1) | copy-start | bytes 4718596
  78.4 20.1 %all-to-all-start.1 = ((bf16[8,192,256]{2,1,0:T(8,128)(2,1)}), bf16[8,192,256]{2,1,0:T(8,128)(2,1)S(1)}, u32[]{:S(2)}, u32[]{:S(2)}) async-start(bf16[8,192,256]{2,1,0:T(8,128)(2,1)} %merge.1), calls=%async_computation.1 | async-start | bytes 1572864 | tf_op jit(solution)/shard_map/all_to_all | solution.py:286

commit v6 on v5

--- a/solution.py
+++ b/solution.py
@@ -2,6 +2,7 @@
 
 import jax
 import jax.numpy as jnp
+import numpy as np
 from jax import lax
 from jax.experimental import pallas as pl
 from jax.experimental.pallas import tpu as pltpu
@@ -42,10 +43,16 @@
 
 
 def prepare_body(
-    q_ref, k_ref, v_ref, stale_ref, q_gain_ref, k_gain_ref, cos_ref, sin_ref, k_out, all_out
+    offset_ref, q_ref, k_ref, v_ref, stale_ref, q_gain_ref, k_gain_ref, k_out, all_out
 ):
-    cosine = jnp.concatenate([cos_ref[...], cos_ref[...]], axis=1)
-    signed_sine = jnp.concatenate([-sin_ref[...], sin_ref[...]], axis=1)
+    half = HEAD // 2
+    lane = lax.broadcasted_iota(jnp.int32, (TOKENS, HEAD), 1)
+    place = jnp.where(lane < half, lane, lane - half).astype(F32)
+    frequency = jnp.exp(-(2.0 * place / HEAD) * np.float32(np.log(256.0)))
+    positions = offset_ref[0] + lax.broadcasted_iota(jnp.int32, (TOKENS, HEAD), 0)
+    angles = positions.astype(F32) * frequency
+    cosine, sine = jnp.cos(angles), jnp.sin(angles)
+    signed_sine = jnp.where(lane < half, -sine, sine)
     for part, (raw, gain) in enumerate(((q_ref, q_gain_ref), (k_ref, k_gain_ref))):
         for h in range(HEADS_HERE):
             cols = slice(h * HEAD, (h + 1) * HEAD)
@@ -60,23 +67,24 @@
     all_out[3:] = stale_ref[...]
 
 
-def prepare(query_raw, key_raw, value_raw, stale_pairs, query_gain, key_gain, cosine, sine):
+def prepare(patch_offsets, query_raw, key_raw, value_raw, stale_pairs, query_gain, key_gain):
     return pl.pallas_call(
         prepare_body,
+        in_specs=[pl.BlockSpec(memory_space=pltpu.SMEM)]
+        + [pl.BlockSpec(memory_space=pltpu.VMEM)] * 6,
         out_shape=(
             jax.ShapeDtypeStruct((TOKENS, WIDTH), BF16),
             jax.ShapeDtypeStruct((5, TOKENS, WIDTH), BF16),
         ),
         name="norm_rotate",
     )(
+        patch_offsets,
         query_raw,
         key_raw,
         value_raw,
         stale_pairs,
         query_gain[None],
         key_gain[None],
-        cosine,
-        sine,
     )
 
 
@@ -248,14 +256,8 @@
     me = lax.axis_index("patch").astype(jnp.int32)
     core = me % 2
 
-    positions = patch_offsets[0] + jnp.arange(TOKENS, dtype=jnp.int32)
-    frequency = jnp.exp(
-        -(2.0 * jnp.arange(HEAD // 2, dtype=F32) / HEAD) * jnp.log(256.0)
-    )
-    angles = positions.astype(F32)[:, None] * frequency
-    cosine, sine = jnp.cos(angles), jnp.sin(angles)
     fresh_keys, prepared = prepare(
-        query_raw, key_raw, value_raw, stale_pairs, query_gain, key_gain, cosine, sine
+        patch_offsets, query_raw, key_raw, value_raw, stale_pairs, query_gain, key_gain
     )
     rows = lax.all_gather(prepared, "patch", axis=0, axis_index_groups=CORES)
     rows = jnp.swapaxes(rows, 0, 1)

time: 100 us -> 99.1 us (level)
  other arithmetic: 1.12 us -> 0.02 us
    sin x1 -> x0, other arithmetic: 1.09 us -> none  [shards(): cosine, sine = (jnp.cos(angles), jnp.sin(angles))]
where the time goes in v6:
time: 99.1 us; the launch traced here: 98.7 us
  starting transfers between devices  36.9 us (37%)
  blocking collectives  25.7 us (26%)
  waiting for transfers between devices  20.7 us (21%)
  Pallas kernels  13.7 us (14%)
  between operations  1.51 us (2%)
    all_to_all x1, blocking collectives, shards(): lax.all_to_all(parts, 'patch', split_axis=0, concat_axis=0, tiled=True, a...  16.5 us
    all_to_all x1, waiting for transfers between devices, shards(): lax.all_to_all(copies, 'head', split_axis=0, concat_axis=0, tiled=True)  13.5 us
    all_gather x1, blocking collectives, shards(): rows = lax.all_gather(prepared, 'patch', axis=0, axis_index_groups=CORES)  9.21 us
    pallas_call x5, Pallas kernels, attend(): pl.pallas_call(functools.partial(attend_body, len(shares), begins, ends),...  8.4 us
    ppermute x1, starting transfers between devices, shards(): second = lax.ppermute(share, 'patch', one)  8.08 us
    all_to_all x1, starting transfers between devices, shards(): lax.all_to_all(copies, 'head', split_axis=0, concat_axis=0, tiled=True)  6.58 us
    ppermute x1, starting transfers between devices, shards(): fifth = lax.ppermute(third, 'patch', other)  3.95 us
    ppermute x1, starting transfers between devices, shards(): far = lax.ppermute(fifth, 'patch', one)  3.82 us
  transfers between devices with their start and end apart: 10, of which 6 were waited for; matrix products, arithmetic and copies ran while one was open for 0% of the time, Pallas kernels for 7%

profile of v6, /device:TPU:1, one launch (start us, length us, event | category | flops | bytes accessed | tf_op | source)
XLA Modules:
  0.0 98.7 jit_solution(1769395978706395107)
XLA Ops:
  1.3 2.6 %norm_rotate.1 = (bf16[192,256]{1,0:T(8,128)(2,1)}, bf16[5,192,256]{2,1,0:T(8,128)(2,1)}) custom-call(s32[1]{0:T(128)S(6)} %copy.15.offset_ref, bf16[192,256]{1,0:T(8,128)(2,1)} %q_ref.1, bf16[192,256]{1,0:T(8,128)(2,1)} %k_ref.1, bf16[192,256]{1,0:T(8,128)(2,1)} %v_ref.1, bf16[2,192,256]{2,1,0:T(8,128)(2,1)} %stale_ref.1, f32[1,128]{1,0:T(1,128)} %bitcast.10, ...), custom_call_target="tpu_custom_call" | custom-call | tf_op jit(solution)/shard_map/norm_rotate/pallas_call | solution.py:71
  3.9 9.2 %all-gather = bf16[10,192,256]{2,1,0:T(8,128)(2,1)S(1)} all-gather(bf16[5,192,256]{2,1,0:T(8,128)(2,1)} %get-tuple-element.24), channel_id=2, replica_groups={{0,8},{16,24},{32,40},{48,56},{64,72},{80,88},{96,104},{112,120},{128,1..., dimensions={0}, use_global_device_ids=true | all-gather | bytes 1474560 | tf_op jit(solution)/shard_map/all_gather | solution.py:262
  13.1 0.1 copy_bitcast_fusion
  13.3 1.9 %collective-permute-start.2 = (bf16[2,2,192,128]{3,2,1,0:T(8,128)(2,1)S(1)}, bf16[2,2,192,128]{3,2,1,0:T(8,128)(2,1)S(1)}, u32[]{:S(2)}, u32[]{:S(2)}) collective-permute-start(bf16[2,2,192,128]{3,2,1,0:T(8,128)(2,1)S(1)} %get-tuple-element.47.refs_3_), channel_id=1, source_target_pairs={{0,224},{8,40},{16,240},{24,56},{32,64},{40,8},{48,80},{56,24},{64... | collective-permute-start | bytes 589832 | tf_op jit(solution)/shard_map/ppermute | solution.py:267
  15.2 1.9 %collective-permute-start = (bf16[384,128]{1,0:T(8,128)(2,1)S(1)}, bf16[384,128]{1,0:T(8,128)(2,1)S(1)}, u32[]{:S(2)}, u32[]{:S(2)}) collective-permute-start(bf16[384,128]{1,0:T(8,128)(2,1)S(1)} %bitcast.8), channel_id=1, source_target_pairs={{0,16},{8,24},{16,0},{24,8},{32,48},{40,56},{48,32},{56,40},{64,80... | collective-permute-start | bytes 294920 | tf_op jit(solution)/shard_map/ppermute | solution.py:269
  17.1 8.1 %collective-permute-start.5 = (bf16[2,2,192,128]{3,2,1,0:T(8,128)(2,1)S(1)}, bf16[2,2,192,128]{3,2,1,0:T(8,128)(2,1)S(1)}, u32[]{:S(2)}, u32[]{:S(2)}) collective-permute-start(bf16[2,2,192,128]{3,2,1,0:T(8,128)(2,1)S(1)} %get-tuple-element.47.refs_3_), channel_id=1, source_target_pairs={{0,32},{8,232},{16,48},{24,248},{32,0},{40,72},{48,16},{56,88},{64... | collective-permute-start | bytes 589832 | tf_op jit(solution)/shard_map/ppermute | solution.py:268
  25.2 0.0 collective-permute-done.2.refs_5_
  25.2 2.0 %collective-permute-start.3 = (bf16[2,2,192,128]{3,2,1,0:T(8,128)(2,1)S(1)}, bf16[2,2,192,128]{3,2,1,0:T(8,128)(2,1)S(1)}, u32[]{:S(2)}, u32[]{:S(2)}) collective-permute-start(bf16[2,2,192,128]{3,2,1,0:T(8,128)(2,1)S(1)} %collective-permute-done.2.refs_5_), channel_id=1, source_target_pairs={{0,32},{8,232},{16,48},{24,248},{32,0},{40,72},{48,16},{56,88},{64... | collective-permute-start | bytes 589832 | tf_op jit(solution)/shard_map/ppermute | solution.py:270
  27.3 0.0 collective-permute-done
  27.3 3.1 %collective-permute-start.1 = (bf16[768,128]{1,0:T(8,128)(2,1)S(1)}, bf16[768,128]{1,0:T(8,128)(2,1)S(1)}, u32[]{:S(2)}, u32[]{:S(2)}) collective-permute-start(bf16[768,128]{1,0:T(8,128)(2,1)S(1)} %pad_maximum_fusion.refs_0_.refs_1_), channel_id=1, source_target_pairs={{0,256},{8,264},{16,272},{24,280},{32,288},{40,296},{48,304},{56,3... | collective-permute-start | bytes 589832 | tf_op jit(solution)/shard_map/ppermute | solution.py:272
  30.5 1.4 %collective-permute-done.5.refs_6_ = bf16[2,2,192,128]{3,2,1,0:T(8,128)(2,1)S(1)} collective-permute-done((bf16[2,2,192,128]{3,2,1,0:T(8,128)(2,1)S(1)}, bf16[2,2,192,128]{3,2,1,0:T(8,128)(2,1)S(1)}, u32[]{:S(2)}, u32[]{:S(2)}) %collective-permute-start.5) | collective-permute-done | bytes 196640 | tf_op jit(solution)/shard_map/ppermute | solution.py:268
  31.8 1.9 %collective-permute-start.6 = (bf16[2,2,192,128]{3,2,1,0:T(8,128)(2,1)S(1)}, bf16[2,2,192,128]{3,2,1,0:T(8,128)(2,1)S(1)}, u32[]{:S(2)}, u32[]{:S(2)}) collective-permute-start(bf16[2,2,192,128]{3,2,1,0:T(8,128)(2,1)S(1)} %collective-permute-done.5.refs_6_), channel_id=1, source_target_pairs={{0,224},{8,40},{16,240},{24,56},{32,64},{40,8},{48,80},{56,24},{64... | collective-permute-start | bytes 589832 | tf_op jit(solution)/shard_map/ppermute | solution.py:271
  33.8 0.4 collective-permute-done.3.refs_5_
  34.1 4.0 %collective-permute-start.4 = (bf16[2,2,192,128]{3,2,1,0:T(8,128)(2,1)S(1)}, bf16[2,2,192,128]{3,2,1,0:T(8,128)(2,1)S(1)}, u32[]{:S(2)}, u32[]{:S(2)}) collective-permute-start(bf16[2,2,192,128]{3,2,1,0:T(8,128)(2,1)S(1)} %collective-permute-done.3.refs_5_), channel_id=1, source_target_pairs={{0,224},{8,40},{16,240},{24,56},{32,64},{40,8},{48,80},{56,24},{64... | collective-permute-start | bytes 589832 | tf_op jit(solution)/shard_map/ppermute | solution.py:273
  38.1 0.0 collective-permute-done.1.refs_1_.refs_2_
  38.1 1.1 %attend.5 = (f32[1536,128]{1,0:T(8,128)S(1)}, f32[1536,128]{1,0:T(8,128)S(1)}, f32[1536,128]{1,0:T(8,128)S(1)}) custom-call(bf16[768,128]{1,0:T(8,128)(2,1)S(1)} %pad_maximum_fusion.refs_0_.refs_1_, bf16[768,128]{1,0:T(8,128)(2,1)S(1)} %collective-permute-done.1.refs_1_.refs_2_, bf16[2,2,192,128]{3,2,1,0:T(8,128)(2,1)S(1)} %get-tuple-element.46.refs_2_, ...), custom_call_target="tpu_custom_call" | custom-call | flops 301989888 | bytes 2359296 | tf_op jit(solution)/shard_map/attend/pallas_call | solution.py:178
  39.2 2.0 %attend.6 = (f32[1536,128]{1,0:T(8,128)S(1)}, f32[1536,128]{1,0:T(8,128)S(1)}, f32[1536,128]{1,0:T(8,128)S(1)}) custom-call(bf16[768,128]{1,0:T(8,128)(2,1)S(1)} %pad_maximum_fusion.refs_0_.refs_1_, bf16[768,128]{1,0:T(8,128)(2,1)S(1)} %collective-permute-done.1.refs_1_.refs_2_, f32[1536,128]{1,0:T(8,128)S(1)} %get-tuple-element.25.refs_2_, ...), custom_call_target="tpu_custom_call" | custom-call | flops 603979776 | bytes 2359296 | tf_op jit(solution)/shard_map/attend/pallas_call | solution.py:178
  41.2 0.5 collective-permute-done.6.refs_6_
  41.7 3.6 %collective-permute-start.7 = (bf16[2,2,192,128]{3,2,1,0:T(8,128)(2,1)S(1)}, bf16[2,2,192,128]{3,2,1,0:T(8,128)(2,1)S(1)}, u32[]{:S(2)}, u32[]{:S(2)}) collective-permute-start(bf16[2,2,192,128]{3,2,1,0:T(8,128)(2,1)S(1)} %collective-permute-done.6.refs_6_), channel_id=1, source_target_pairs={{0,32},{8,232},{16,48},{24,248},{32,0},{40,72},{48,16},{56,88},{64... | collective-permute-start | bytes 589832 | tf_op jit(solution)/shard_map/ppermute | solution.py:278
  45.2 2.0 %attend.7 = (f32[1536,128]{1,0:T(8,128)S(1)}, f32[1536,128]{1,0:T(8,128)S(1)}, f32[1536,128]{1,0:T(8,128)S(1)}) custom-call(bf16[768,128]{1,0:T(8,128)(2,1)S(1)} %pad_maximum_fusion.refs_0_.refs_1_, bf16[768,128]{1,0:T(8,128)(2,1)S(1)} %collective-permute-done.1.refs_1_.refs_2_, f32[1536,128]{1,0:T(8,128)S(1)} %get-tuple-element.31.refs_2_, ...), custom_call_target="tpu_custom_call" | custom-call | flops 603979776 | bytes 2359296 | tf_op jit(solution)/shard_map/attend/pallas_call | solution.py:178
  47.2 0.0 collective-permute-done.4.refs_5_
  47.2 3.8 %collective-permute-start.8 = (bf16[2,2,192,128]{3,2,1,0:T(8,128)(2,1)S(1)}, bf16[2,2,192,128]{3,2,1,0:T(8,128)(2,1)S(1)}, u32[]{:S(2)}, u32[]{:S(2)}) collective-permute-start(bf16[2,2,192,128]{3,2,1,0:T(8,128)(2,1)S(1)} %collective-permute-done.4.refs_5_), channel_id=1, source_target_pairs={{0,32},{8,232},{16,48},{24,248},{32,0},{40,72},{48,16},{56,88},{64... | collective-permute-start | bytes 589832 | tf_op jit(solution)/shard_map/ppermute | solution.py:281
  51.1 2.5 %collective-permute-done.7.refs_6_ = bf16[2,2,192,128]{3,2,1,0:T(8,128)(2,1)S(1)} collective-permute-done((bf16[2,2,192,128]{3,2,1,0:T(8,128)(2,1)S(1)}, bf16[2,2,192,128]{3,2,1,0:T(8,128)(2,1)S(1)}, u32[]{:S(2)}, u32[]{:S(2)}) %collective-permute-start.7) | collective-permute-done | bytes 196640 | tf_op jit(solution)/shard_map/ppermute | solution.py:278
  53.6 2.0 %attend.8 = (f32[1536,128]{1,0:T(8,128)S(1)}, f32[1536,128]{1,0:T(8,128)S(1)}, f32[1536,128]{1,0:T(8,128)S(1)}) custom-call(bf16[768,128]{1,0:T(8,128)(2,1)S(1)} %pad_maximum_fusion.refs_0_.refs_1_, bf16[768,128]{1,0:T(8,128)(2,1)S(1)} %collective-permute-done.1.refs_1_.refs_2_, f32[1536,128]{1,0:T(8,128)S(1)} %get-tuple-element.38.refs_2_, ...), custom_call_target="tpu_custom_call" | custom-call | flops 603979776 | bytes 2359296 | tf_op jit(solution)/shard_map/attend/pallas_call | solution.py:178
  55.5 2.4 %collective-permute-done.8.refs_6_ = bf16[2,2,192,128]{3,2,1,0:T(8,128)(2,1)S(1)} collective-permute-done((bf16[2,2,192,128]{3,2,1,0:T(8,128)(2,1)S(1)}, bf16[2,2,192,128]{3,2,1,0:T(8,128)(2,1)S(1)}, u32[]{:S(2)}, u32[]{:S(2)}) %collective-permute-start.8) | collective-permute-done | bytes 196640 | tf_op jit(solution)/shard_map/ppermute | solution.py:281
  58.0 1.4 %attend.9 = bf16[8,208,128]{2,1,0:T(8,128)(2,1)S(1)} custom-call(s32[1]{0:T(128)} %bitcast.refs_0_, bf16[768,128]{1,0:T(8,128)(2,1)S(1)} %pad_maximum_fusion.refs_0_.refs_1_, bf16[768,128]{1,0:T(8,128)(2,1)S(1)} %collective-permute-done.1.refs_1_.refs_2_, f32[1536,128]{1,0:T(8,128)S(1)} %get-tuple-element.42.refs_3_, ...), custom_call_target="tpu_custom_call" | custom-call | flops 301989888 | bytes 2359296 | tf_op jit(solution)/shard_map/attend/pallas_call | solution.py:178
  59.4 16.5 %all_to_all.10.parts_ref = bf16[8,208,128]{2,1,0:T(8,128)(2,1)S(1)} all-to-all(bf16[8,208,128]{2,1,0:T(8,128)(2,1)S(1)} %attend.9), channel_id=1, replica_groups={{0,16,256,272,8,24,264,280},{32,48,288,304,40,56,296,312},{64,80,320,33..., dimensions={0} | all-to-all | bytes 851968 | tf_op jit(solution)/shard_map/all_to_all | solution.py:284
  75.9 0.0 copy-start.1
  75.9 0.0 copy-start
  75.9 1.4 %merge.1 = bf16[8,192,256]{2,1,0:T(8,128)(2,1)} custom-call(bf16[8,208,128]{2,1,0:T(8,128)(2,1)S(1)} %all_to_all.10.parts_ref), custom_call_target="tpu_custom_call" | custom-call | tf_op jit(solution)/shard_map/merge/pallas_call | solution.py:219
  77.3 6.6 %all-to-all-start.1 = ((bf16[8,192,256]{2,1,0:T(8,128)(2,1)}), bf16[8,192,256]{2,1,0:T(8,128)(2,1)S(1)}, u32[]{:S(2)}, u32[]{:S(2)}) async-start(bf16[8,192,256]{2,1,0:T(8,128)(2,1)} %merge.1), calls=%async_computation.1 | async-start | bytes 1572864 | tf_op jit(solution)/shard_map/all_to_all | solution.py:288
  83.9 0.0 copy-done.1
  83.9 13.5 %all-to-all-done.1.parts_ref = bf16[8,192,256]{2,1,0:T(8,128)(2,1)S(1)} async-done(((bf16[8,192,256]{2,1,0:T(8,128)(2,1)}), bf16[8,192,256]{2,1,0:T(8,128)(2,1)S(1)}, u32[]{:S(2)}, u32[]{:S(2)}) %all-to-all-start.1) | async-done | bytes 786464 | tf_op jit(solution)/shard_map/all_to_all | solution.py:288
  97.4 0.0 copy-done
  97.4 1.2 %project.1 = bf16[192,384]{1,0:T(8,128)(2,1)} custom-call(bf16[8,192,256]{2,1,0:T(8,128)(2,1)S(1)} %all-to-all-done.1.parts_ref, bf16[2048,384]{1,0:T(8,128)(2,1)S(1)} %copy-done, f32[1,384]{1,0:T(1,128)S(1)} %broadcast_in_dim.15.gate_ref), custom_call_target="tpu_custom_call" | custom-call | tf_op jit(solution)/shard_map/project/pallas_call | solution.py:237
  (4 shorter events, 0.1 us)
Async XLA Ops:
  13.3 12.0 %collective-permute-start.2 = (bf16[2,2,192,128]{3,2,1,0:T(8,128)(2,1)S(1)}, bf16[2,2,192,128]{3,2,1,0:T(8,128)(2,1)S(1)}, u32[]{:S(2)}, u32[]{:S(2)}) collective-permute-start(bf16[2,2,192,128]{3,2,1,0:T(8,128)(2,1)S(1)} %get-tuple-element.47.refs_3_), channel_id=1, source_target_pairs={{0,224},{8,40},{16,240},{24,56},{32,64},{40,8},{48,80},{56,24},{64... | collective-permute-start | bytes 589832 | tf_op jit(solution)/shard_map/ppermute | solution.py:267
  15.2 12.1 %collective-permute-start = (bf16[384,128]{1,0:T(8,128)(2,1)S(1)}, bf16[384,128]{1,0:T(8,128)(2,1)S(1)}, u32[]{:S(2)}, u32[]{:S(2)}) collective-permute-start(bf16[384,128]{1,0:T(8,128)(2,1)S(1)} %bitcast.8), channel_id=1, source_target_pairs={{0,16},{8,24},{16,0},{24,8},{32,48},{40,56},{48,32},{56,40},{64,80... | collective-permute-start | bytes 294920 | tf_op jit(solution)/shard_map/ppermute | solution.py:269
  17.1 14.7 %collective-permute-start.5 = (bf16[2,2,192,128]{3,2,1,0:T(8,128)(2,1)S(1)}, bf16[2,2,192,128]{3,2,1,0:T(8,128)(2,1)S(1)}, u32[]{:S(2)}, u32[]{:S(2)}) collective-permute-start(bf16[2,2,192,128]{3,2,1,0:T(8,128)(2,1)S(1)} %get-tuple-element.47.refs_3_), channel_id=1, source_target_pairs={{0,32},{8,232},{16,48},{24,248},{32,0},{40,72},{48,16},{56,88},{64... | collective-permute-start | bytes 589832 | tf_op jit(solution)/shard_map/ppermute | solution.py:268
  25.2 8.9 %collective-permute-start.3 = (bf16[2,2,192,128]{3,2,1,0:T(8,128)(2,1)S(1)}, bf16[2,2,192,128]{3,2,1,0:T(8,128)(2,1)S(1)}, u32[]{:S(2)}, u32[]{:S(2)}) collective-permute-start(bf16[2,2,192,128]{3,2,1,0:T(8,128)(2,1)S(1)} %collective-permute-done.2.refs_5_), channel_id=1, source_target_pairs={{0,32},{8,232},{16,48},{24,248},{32,0},{40,72},{48,16},{56,88},{64... | collective-permute-start | bytes 589832 | tf_op jit(solution)/shard_map/ppermute | solution.py:270
  27.3 10.8 %collective-permute-start.1 = (bf16[768,128]{1,0:T(8,128)(2,1)S(1)}, bf16[768,128]{1,0:T(8,128)(2,1)S(1)}, u32[]{:S(2)}, u32[]{:S(2)}) collective-permute-start(bf16[768,128]{1,0:T(8,128)(2,1)S(1)} %pad_maximum_fusion.refs_0_.refs_1_), channel_id=1, source_target_pairs={{0,256},{8,264},{16,272},{24,280},{32,288},{40,296},{48,304},{56,3... | collective-permute-start | bytes 589832 | tf_op jit(solution)/shard_map/ppermute | solution.py:272
  31.8 9.8 %collective-permute-start.6 = (bf16[2,2,192,128]{3,2,1,0:T(8,128)(2,1)S(1)}, bf16[2,2,192,128]{3,2,1,0:T(8,128)(2,1)S(1)}, u32[]{:S(2)}, u32[]{:S(2)}) collective-permute-start(bf16[2,2,192,128]{3,2,1,0:T(8,128)(2,1)S(1)} %collective-permute-done.5.refs_6_), channel_id=1, source_target_pairs={{0,224},{8,40},{16,240},{24,56},{32,64},{40,8},{48,80},{56,24},{64... | collective-permute-start | bytes 589832 | tf_op jit(solution)/shard_map/ppermute | solution.py:271
  34.1 13.1 %collective-permute-start.4 = (bf16[2,2,192,128]{3,2,1,0:T(8,128)(2,1)S(1)}, bf16[2,2,192,128]{3,2,1,0:T(8,128)(2,1)S(1)}, u32[]{:S(2)}, u32[]{:S(2)}) collective-permute-start(bf16[2,2,192,128]{3,2,1,0:T(8,128)(2,1)S(1)} %collective-permute-done.3.refs_5_), channel_id=1, source_target_pairs={{0,224},{8,40},{16,240},{24,56},{32,64},{40,8},{48,80},{56,24},{64... | collective-permute-start | bytes 589832 | tf_op jit(solution)/shard_map/ppermute | solution.py:273
  41.7 11.9 %collective-permute-start.7 = (bf16[2,2,192,128]{3,2,1,0:T(8,128)(2,1)S(1)}, bf16[2,2,192,128]{3,2,1,0:T(8,128)(2,1)S(1)}, u32[]{:S(2)}, u32[]{:S(2)}) collective-permute-start(bf16[2,2,192,128]{3,2,1,0:T(8,128)(2,1)S(1)} %collective-permute-done.6.refs_6_), channel_id=1, source_target_pairs={{0,32},{8,232},{16,48},{24,248},{32,0},{40,72},{48,16},{56,88},{64... | collective-permute-start | bytes 589832 | tf_op jit(solution)/shard_map/ppermute | solution.py:278
  47.2 10.8 %collective-permute-start.8 = (bf16[2,2,192,128]{3,2,1,0:T(8,128)(2,1)S(1)}, bf16[2,2,192,128]{3,2,1,0:T(8,128)(2,1)S(1)}, u32[]{:S(2)}, u32[]{:S(2)}) collective-permute-start(bf16[2,2,192,128]{3,2,1,0:T(8,128)(2,1)S(1)} %collective-permute-done.4.refs_5_), channel_id=1, source_target_pairs={{0,32},{8,232},{16,48},{24,248},{32,0},{40,72},{48,16},{56,88},{64... | collective-permute-start | bytes 589832 | tf_op jit(solution)/shard_map/ppermute | solution.py:281
  75.9 8.0 %copy-start.1 = (f32[384]{0:T(512)S(1)}, f32[384]{0:T(512)}, u32[]{:S(2)}) copy-start(f32[384]{0:T(512)} %param.16) | copy-start | bytes 4612
  75.9 21.5 %copy-start = (bf16[2048,384]{1,0:T(8,128)(2,1)S(1)}, bf16[2048,384]{1,0:T(8,128)(2,1)}, u32[]{:S(2)}) copy-start(bf16[2048,384]{1,0:T(8,128)(2,1)} %weight_ref.1) | copy-start | bytes 4718596
  77.3 20.1 %all-to-all-start.1 = ((bf16[8,192,256]{2,1,0:T(8,128)(2,1)}), bf16[8,192,256]{2,1,0:T(8,128)(2,1)S(1)}, u32[]{:S(2)}, u32[]{:S(2)}) async-start(bf16[8,192,256]{2,1,0:T(8,128)(2,1)} %merge.1), calls=%async_computation.1 | async-start | bytes 1572864 | tf_op jit(solution)/shard_map/all_to_all | solution.py:288
